TPU v7x, 32 devices: a whole 2x2x4 slice. The times are simulated.
32 devices in a mesh: ment: 8 (over z, x), ent: 4 (over y, core).
Axes of the slice: x: 2, y: 2, z: 4, core: 2. Of those that a mesh axis runs over, the one named last changes fastest.
Arguments:
- hidden_in: bfloat16 [512, 32, 1024], P('ment'), may hold values from -6 to 6
- w_qkv: bfloat16 [1024, 3, 1024], P(None, None, 'ent'), may hold values from -0.1875 to 0.1875
- w_out: bfloat16 [1024, 1024], P('ent'), may hold values from -0.1875 to 0.1875
- ln_gain: float32 [1024], replicated, may hold values from 0.5 to 1.5
- ln_bias: float32 [1024], replicated, may hold values from -3 to 3
- table: bfloat16 [32, 256, 1024], P('ent'), may hold values from -0.5 to 0.5
- key_len: int32 [512], P('ment'), may hold values from 4 to 32
- gold_block: int32 [512], P('ment'), may hold values from 0 to 31
- gold_row: int32 [512], P('ment'), may hold values from 0 to 255
- neg_blocks: int32 [8, 4], P('ment'), may hold values from 0 to 31, as said below
Outputs:
- grad_hidden: bfloat16 [512, 32, 1024], P(('ment', 'ent'))
- grad_qkv: float32 [1024, 3, 1024], P('ment', None, 'ent')
- grad_wo: float32 [1024, 1024], P('ent', 'ment')
- grad_ln: float32 [2, 1024], P(None, 'ment')
- grad_table: float32 [32, 256, 1024], P('ent', 'ment')
Inputs may be any that keep to these rules, and one draw needn't show every extreme that they name: `neg_blocks`: each row lists 4 different blocks.
All inputs are finite; a program needn't handle non-finite values.
Results may differ from a plain program's by a relative error of at most 0.028.
Values may be sent and summed in bfloat16 or wider, within the bound.
No kernel may reach another device: no remote copies, remote signals or barrier semaphores. Data moves between devices by JAX's collectives and lax.ppermute only.
A program may use at most 128 MiB of HBM per device.

v0:
```python
import jax
import jax.numpy as jnp
from jax import lax
from jax.sharding import PartitionSpec as P

HD = 64


ln_eps = 1e-06


def contract(left, right, left_dim, right_dim):
    return lax.dot_general(
        left, right, (((left_dim,), (right_dim,)), ((), ())), preferred_element_type=jnp.float32
    )


def on_device(
    hidden_in, w_qkv, w_out, ln_gain, ln_bias, table, key_len, gold_block, gold_row, neg_blocks
):
    ment_rows, seq_len, width = hidden_in.shape
    local_cols = w_qkv.shape[2]
    local_heads = local_cols // HD
    own_blocks, block_rows = (table.shape[0], table.shape[1])
    score_scale = HD ** (-0.5)
    owner = lax.axis_index("ent")
    first_block = owner * own_blocks
    cls_rows = hidden_in[:, 0, :]
    w_query = w_qkv[:, 0, :]
    w_keyval = w_qkv[:, 1:, :].reshape(width, 2 * local_cols)
    query = jnp.dot(cls_rows, w_query, preferred_element_type=jnp.float32).astype(jnp.bfloat16)
    keyval = jnp.dot(
        hidden_in.reshape(ment_rows * seq_len, width), w_keyval, preferred_element_type=jnp.float32
    )
    keyval = keyval.astype(jnp.bfloat16).reshape(ment_rows, seq_len, 2, local_heads, HD)
    key_heads = keyval[:, :, 0]
    value_heads = keyval[:, :, 1]
    query_heads = query.reshape(ment_rows, local_heads, HD)
    attention_scores = (
        jnp.einsum("ybn,yqbn->ybq", query_heads, key_heads, preferred_element_type=jnp.float32)
        * score_scale
    )
    valid = (jnp.arange(seq_len, dtype=jnp.int32)[None, :] < key_len[:, None]).astype(jnp.float32)
    expo = jnp.exp(attention_scores) * valid[:, None, :]
    probs = expo / jnp.sum(expo, axis=-1, keepdims=True)
    probability_half = probs.astype(jnp.bfloat16)
    context_rows = jnp.einsum(
        "qjp,qpjb->qjb", probability_half, value_heads, preferred_element_type=jnp.float32
    )
    context_rows = context_rows.reshape(ment_rows, local_cols).astype(jnp.bfloat16)
    attn_part = jnp.dot(context_rows, w_out, preferred_element_type=jnp.float32)
    local_block = gold_block - first_block
    owned = (local_block >= 0) & (local_block < own_blocks)
    safe_block = jnp.clip(local_block, 0, own_blocks - 1)
    flat_table = table.reshape(own_blocks * block_rows, width)
    picked = flat_table[safe_block * block_rows + gold_row]
    picked = jnp.where(owned[:, None], picked.astype(jnp.float32), 0.0)
    attn_out, gold_sum = (
        lax.psum(attn_part.astype(jnp.bfloat16), "ent").astype(jnp.float32),
        lax.psum(picked.astype(jnp.bfloat16), "ent").astype(jnp.float32),
    )
    golds = gold_sum.astype(jnp.bfloat16)
    resid = cls_rows.astype(jnp.float32) + attn_out
    centre = resid - jnp.mean(resid, axis=-1, keepdims=True)
    rstd = lax.rsqrt(jnp.mean(centre * centre, axis=-1, keepdims=True) + ln_eps)
    normed = centre * rstd
    embed = (normed * ln_gain + ln_bias).astype(jnp.bfloat16)
    inbatch = contract(embed, golds, 1, 1)
    negscore = contract(embed, flat_table, 1, 1)
    block_ids = first_block + jnp.arange(own_blocks, dtype=jnp.int32)
    listed = jnp.any(neg_blocks[0][:, None] == block_ids[None, :], axis=0).astype(jnp.float32)
    row_mask = jnp.repeat(listed, block_rows)
    neg_part = jnp.sum(jnp.exp(negscore) * row_mask[None, :], axis=1)
    neg_total = lax.psum(neg_part, "ent")
    lse = jnp.log(jnp.sum(jnp.exp(inbatch), axis=1) + neg_total)
    eye = jnp.eye(ment_rows, dtype=jnp.float32)
    w_inb = (jnp.exp(inbatch - lse[:, None]) - eye).astype(jnp.bfloat16)
    w_neg = (jnp.exp(negscore - lse[:, None]) * row_mask[None, :]).astype(jnp.bfloat16)
    embed_part = jnp.dot(w_neg, flat_table, preferred_element_type=jnp.float32)
    d_embed = jnp.dot(w_inb, golds, preferred_element_type=jnp.float32) + lax.psum(
        embed_part.astype(jnp.bfloat16), "ent"
    ).astype(jnp.float32)
    ln_terms = jnp.stack([jnp.sum(d_embed * normed, axis=0), jnp.sum(d_embed, axis=0)])
    upper = d_embed * ln_gain
    d_resid = rstd * (
        upper
        - jnp.mean(upper, axis=-1, keepdims=True)
        - normed * jnp.mean(upper * normed, axis=-1, keepdims=True)
    )
    d_resid_bf = d_resid.astype(jnp.bfloat16)
    wo_term = contract(context_rows, d_resid_bf, 0, 0)
    grad_wo, grad_ln = (
        lax.psum_scatter(wo_term, "ment", scatter_dimension=1, tiled=True),
        lax.psum_scatter(ln_terms, "ment", scatter_dimension=1, tiled=True),
    )
    d_context = contract(d_resid_bf, w_out, 1, 1).astype(jnp.bfloat16)
    context_head_gradient = d_context.reshape(ment_rows, local_heads, HD)
    probability_gradient = jnp.einsum(
        "ybn,yqbn->ybq", context_head_gradient, value_heads, preferred_element_type=jnp.float32
    )
    score_gradient = probs * (
        probability_gradient - jnp.sum(probs * probability_gradient, axis=-1, keepdims=True)
    )
    query_gradient = (
        jnp.einsum("qjp,qpjb->qjb", score_gradient, key_heads, preferred_element_type=jnp.float32)
        * score_scale
    )
    query_gradient = query_gradient.reshape(ment_rows, local_cols).astype(jnp.bfloat16)
    key_gradient = (
        jnp.einsum("ryk,ryo->rkyo", score_gradient, query_heads, preferred_element_type=jnp.float32)
        * score_scale
    )
    value_gradient = jnp.einsum(
        "ryk,ryo->rkyo", probability_half, context_head_gradient, preferred_element_type=jnp.float32
    )
    d_keyval = (
        jnp.stack([key_gradient, value_gradient], axis=2)
        .reshape(ment_rows, seq_len, 2 * local_cols)
        .astype(jnp.bfloat16)
    )
    flat_grad = d_keyval.reshape(ment_rows * seq_len, 2 * local_cols)
    count = lax.axis_size("ment") * (width // lax.axis_size("ment"))
    kv_term = contract(hidden_in.reshape(ment_rows * seq_len, count), flat_grad, 0, 0)
    query_term = contract(hidden_in[:, 0, :], query_gradient, 0, 0)
    grad_qkv = lax.psum_scatter(
        jnp.concatenate([query_term[:, None, :], kv_term.reshape(count, 2, local_cols)], axis=1),
        "ment",
        scatter_dimension=0,
        tiled=True,
    )
    share = ment_rows // lax.axis_size("ent")
    grad_part = d_keyval.reshape(share * lax.axis_size("ent") * seq_len, 2 * local_cols)
    token_term = contract(grad_part, w_keyval, 1, 1).reshape(
        share * lax.axis_size("ent"), seq_len, width
    )
    summed = lax.psum_scatter(
        token_term.at[:, 0, :].add(contract(query_gradient, w_query, 1, 1)).astype(jnp.bfloat16),
        "ent",
        scatter_dimension=0,
        tiled=True,
    ).astype(jnp.float32)
    resid_mine = lax.dynamic_slice_in_dim(d_resid, owner * share, share, 0)
    grad_hidden = summed.at[:, 0, :].add(resid_mine).astype(jnp.bfloat16)
    gold_terms = contract(w_inb, embed, 0, 0)
    weight_blocks = w_neg.reshape(ment_rows, own_blocks, block_rows)
    count = lax.axis_size("ment") * (block_rows // lax.axis_size("ment"))
    neg_term = jnp.einsum("mbr,md->rbd", weight_blocks, embed, preferred_element_type=jnp.float32)
    inside = owned & (gold_row >= 0) & (gold_row < count)
    row_slot = jnp.where(inside, gold_row, count)
    reduced = lax.psum_scatter(
        neg_term.at[row_slot, safe_block].add(gold_terms, mode="drop"),
        "ment",
        scatter_dimension=0,
        tiled=True,
    )
    grad_table = jnp.transpose(reduced, (1, 0, 2))
    return (grad_hidden, grad_qkv, grad_wo, grad_ln, grad_table)


def solution(mesh):
    placed = (
        P("ment", None, None),
        P(None, None, "ent"),
        P("ent", None),
        P(),
        P(),
        P("ent", None, None),
        P("ment"),
        P("ment"),
        P("ment"),
        P("ment", None),
    )
    return jax.shard_map(
        on_device,
        mesh=mesh,
        in_specs=placed,
        out_specs=(
            P(("ment", "ent"), None, None),
            P("ment", None, "ent"),
            P("ent", "ment"),
            P(None, "ment"),
            P("ent", "ment", None),
        ),
        check_vma=False,
    )
```

profile of v0, /device:TPU:0, one launch (start us, length us, event | category | flops | bytes accessed | tf_op | source)
XLA Modules:
  0.0 549.4 jit_solution(3051830851212606151)
XLA Ops:
  14.6 4.5 convolution_convert_fusion
  19.1 3.7 reshape.170
  22.8 4.8 slice_bitcast_fusion
  30.6 6.0 %fusion.13 = f32[64,4,32]{1,2,0:T(8,128)S(1)} fusion(f32[64,4,1,32]{1,3,0,2:T(8,128)S(1)} %copy.42, f32[64,32]{1,0:T(8,128)S(1)} %fusion.34), kind=kOutput, calls=%fused_computation.32 | output fusion | flops 41247 | bytes 73728 | tf_op jit(solution)/shard_map/div | solution.py:45
  41.1 3.5 gather_fusion
  46.5 34.7 %all-reduce.6.cloned.1.call-done = (bf16[64,1024]{1,0:T(8,128)(2,1)}, bf16[64,1024]{1,0:T(8,128)(2,1)}) async-done(((bf16[64,1024]{1,0:T(8,128)(2,1)}, bf16[64,1024]{1,0:T(8,128)(2,1)}), (bf16[64,1024]{1,0:T(8,128)(2,1)}, bf16[64,1024]{1,0:T(8,128)(2,1)})) %all-reduce.6.cloned.1.call-update) | async-done | bytes 262160 | tf_op jit(solution)/shard_map/psum | solution.py:60
  85.5 3.7 multiply_reduce_fusion
  89.3 5.8 %psum.30 = f32[64]{0:T(128)S(1)} all-reduce(f32[64]{0:T(128)S(1)} %get-tuple-element.58), channel_id=1, replica_groups=mesh['ment'=8,'ent'=4] {'ent'}, use_global_device_ids=true, to_apply=%region_8.9 | all-reduce | flops 64 | bytes 512 | tf_op jit(solution)/shard_map/psum | solution.py:74
  95.2 3.7 convolution_convert_fusion.1
  99.3 3.3 copy.34
  102.6 2.5 reshape.198
  105.2 25.5 %all-reduce.4.cloned.1.call-done = bf16[64,1024]{1,0:T(8,128)(2,1)} async-done(((bf16[64,1024]{1,0:T(8,128)(2,1)}), bf16[64,1024]{1,0:T(8,128)(2,1)}) %all-reduce.4.cloned.1.call-update) | async-done | bytes 131088 | tf_op jit(solution)/shard_map/psum | solution.py:80
  132.7 2.8 fusion
  138.1 2.6 fusion.9
  145.2 2.5 multiply_bitcast_fusion.1
  147.7 2.5 multiply_bitcast_fusion
  150.2 5.4 maximum_convert_fusion
  155.6 6.6 %convert_element_type.118 = bf16[64,32,512]{2,1,0:T(8,128)(2,1)S(1)} reshape(bf16[64,32,2,4,64]{4,3,2,1,0:T(4,128)(2,1)} %maximum_convert_fusion) | data formatting | bytes 4194304 | tf_op jit(solution)/shard_map/convert_element_type | solution.py:119
  162.3 4.5 fusion.61
  166.8 3.2 copy-done.2
  170.3 6.1 %scatter-add.14 = f32[64,32,1024]{2,1,0:T(8,128)} dynamic-update-slice(f32[64,32,1024]{2,1,0:T(8,128)} %copy-done.2, f32[64,1,1024]{2,1,0:T(1,128)S(1)} %slice_add_fusion, s32[]{:T(128)} %constant.76.clone.1, s32[]{:T(128)} %constant.76.clone.1, s32[]{:T(128)} %constant.76.clone.1) | dynamic-update-slice | bytes 524292 | tf_op jit(solution)/shard_map/scatter-add | solution.py:137
  176.4 6.0 %convert_element_type.121 = bf16[64,32,1024]{2,1,0:T(8,128)(2,1)} convert(f32[64,32,1024]{2,1,0:T(8,128)} %scatter-add.14) | non-fusion elementwise | flops 2097152 | bytes 12582912 | tf_op jit(solution)/shard_map/convert_element_type | solution.py:137
  183.1 4.5 convolution_bitcast_fusion
  187.6 9.0 %copy.38 = f32[256,8,1024]{2,1,0:T(8,128)} copy(f32[256,8,1024]{0,2,1:T(8,128)} %convolution_bitcast_fusion) | data formatting | bytes 16777216 | tf_op jit(solution)/shard_map/mbr,md->rbd/transpose | solution.py:147
  196.8 10.5 %scatter_fusion = f32[256,8,1024]{2,1,0:T(8,128)} fusion(f32[256,8,1024]{2,1,0:T(8,128)} %copy.38, s32[64]{0:T(128)S(1)} %fusion.38, f32[64,1024]{1,0:T(8,128)S(1)} %fusion.39), kind=kCustom, calls=%fused_computation.1 | custom fusion | flops 65536 | bytes 786944 | tf_op jit(solution)/shard_map/scatter-add | solution.py:151
  211.2 6.6 %fusion.62 = f32[512,1024,1]{1,0,2:T(8,128)} fusion(bf16[64,32,512]{2,1,0:T(8,128)(2,1)} %copy-done.4, bf16[64,32,1024]{2,1,0:T(8,128)(2,1)} %param.14), kind=kOutput, calls=%fused_computation.109 | convolution fusion | flops 2147483648 | bytes 8388608 | tf_op jit(solution)/shard_map/dot_general | solution.py:13
  220.2 3.2 pad_maximum_fusion
  225.0 19.8 %reduce-scatter.8.cloned.1.call-done = bf16[16,32,1024]{2,1,0:T(8,128)(2,1)} async-done(((bf16[64,32,1024]{2,1,0:T(8,128)(2,1)}), bf16[16,32,1024]{2,1,0:T(8,128)(2,1)}) %reduce-scatter.8.cloned.1.call-update) | async-done | bytes 1048592 | tf_op jit(solution)/shard_map/reduce_scatter | solution.py:136
  247.9 149.4 %reduce-scatter.14.cloned.1.call-done = f32[32,8,1024]{2,1,0:T(8,128)} async-done(((f32[256,8,1024]{2,1,0:T(8,128)}), f32[32,8,1024]{2,1,0:T(8,128)}) %reduce-scatter.14.cloned.1.call-update) | async-done | bytes 1048592 | tf_op jit(solution)/shard_map/reduce_scatter | solution.py:150
  397.3 2.8 copy.39
  400.1 64.3 %reduce-scatter.12.cloned.1.call-done = f32[256,128]{1,0:T(8,128)} async-done(((f32[256,1024]{1,0:T(8,128)}), f32[256,128]{1,0:T(8,128)}) %reduce-scatter.12.cloned.1.call-update) | async-done | bytes 131088 | tf_op jit(solution)/shard_map/reduce_scatter | solution.py:93
  464.4 78.2 %reduce-scatter.10.cloned.1.call-done = f32[128,3,256]{2,0,1:T(8,128)} async-done(((f32[1024,3,256]{2,0,1:T(8,128)}), f32[128,3,256]{2,0,1:T(8,128)}) %reduce-scatter.10.cloned.1.call-update) | async-done | bytes 393232 | tf_op jit(solution)/shard_map/reduce_scatter | solution.py:125
  (114 shorter events, 42.5 us)
Async XLA Ops:
  7.2 38.2 %copy-start = (bf16[256,1024]{1,0:T(8,128)(2,1)S(1)}, bf16[256,1024]{1,0:T(8,128)(2,1)}, u32[]{:S(2)}) copy-start(bf16[256,1024]{1,0:T(8,128)(2,1)} %param.16) | copy-start | bytes 1572868
  7.2 74.0 %all-reduce.6.cloned.1.call-start = ((), (), s32[]{:S(2)}) async-start(), calls=%async_computation.11 | async-start | bytes 524288 | tf_op jit(solution)/shard_map/psum | solution.py:60
  27.6 1.4 copy-start.6
  36.6 1.0 copy-start.3
  38.6 7.7 %copy-start.18 = (s32[1,4]{1,0:T(1,128)S(1)}, s32[1,4]{1,0:T(1,128)}, u32[]{:S(2)}) copy-start(s32[1,4]{1,0:T(1,128)} %param.23) | copy-start | bytes 52
  40.9 42.5 %copy-start.14 = (f32[1024]{0:T(1024)S(1)}, f32[1024]{0:T(1024)}, u32[]{:S(2)}) copy-start(f32[1024]{0:T(1024)} %param.17) | copy-start | bytes 12292
  40.9 42.5 %copy-start.15 = (f32[1024]{0:T(1024)S(1)}, f32[1024]{0:T(1024)}, u32[]{:S(2)}) copy-start(f32[1024]{0:T(1024)} %param.18) | copy-start | bytes 12292
  41.1 48.2 %copy-start.9 = (bf16[64,256]{1,0:T(8,128)(2,1)}, bf16[64,256]{1,0:T(8,128)(2,1)S(1)}, u32[]{:S(2)}) copy-start(bf16[64,256]{1,0:T(8,128)(2,1)S(1)} %convert_element_type.103) | copy-start | bytes 98308
  46.2 84.5 %all-reduce.4.cloned.1.call-start = ((), (), s32[]{:S(2)}) async-start(), calls=%async_computation.5 | async-start | bytes 262144 | tf_op jit(solution)/shard_map/psum | solution.py:80
  85.5 45.2 %copy-start.12 = (f32[64,64]{0,1:T(8,128)}, f32[64,64]{0,1:T(8,128)S(1)}, u32[]{:S(2)}) copy-start(f32[64,64]{0,1:T(8,128)S(1)} %get-tuple-element.57) | copy-start | bytes 49156
  98.9 124.6 %reduce-scatter.16.cloned.1.call-start = ((), (), s32[]{:S(2)}) async-start(), calls=%async_computation.10 | async-start | bytes 589824
  99.3 31.4 %copy-start.5 = (bf16[64,1024]{1,0:T(8,128)(2,1)S(1)}, bf16[64,1024]{1,0:T(8,128)(2,1)}, u32[]{:S(2)}) copy-start(bf16[64,1024]{1,0:T(8,128)(2,1)} %get-tuple-element.49) | copy-start | bytes 393220
  99.3 31.4 %copy-start.11 = (bf16[64,1024]{1,0:T(8,128)(2,1)S(1)}, bf16[64,1024]{1,0:T(8,128)(2,1)}, u32[]{:S(2)}) copy-start(bf16[64,1024]{1,0:T(8,128)(2,1)} %get-tuple-element.48) | copy-start | bytes 393220
  136.6 108.1 %reduce-scatter.8.cloned.1.call-start = ((), (), s32[]{:S(2)}) async-start(), calls=%async_computation.6 | async-start | bytes 5242880 | tf_op jit(solution)/shard_map/reduce_scatter | solution.py:136
  143.9 6.3 %copy-start.7 = (bf16[64,256]{1,0:T(8,128)(2,1)}, bf16[64,256]{1,0:T(8,128)(2,1)S(1)}, u32[]{:S(2)}) copy-start(bf16[64,256]{1,0:T(8,128)(2,1)S(1)} %convert_element_type.120) | copy-start | bytes 98308
  162.2 4.5 copy-start.4
  166.7 3.2 copy-start.2
  182.4 0.7 copy-start.16
  182.4 0.7 copy-start.17
  182.5 214.8 %reduce-scatter.14.cloned.1.call-start = ((), (), s32[]{:S(2)}) async-start(), calls=%async_computation.9 | async-start | bytes 9437184 | tf_op jit(solution)/shard_map/reduce_scatter | solution.py:150
  187.6 9.0 %copy-start.13 = (f32[64,64]{0,1:T(8,128)S(1)}, f32[64,64]{0,1:T(8,128)}, u32[]{:S(2)}) copy-start(f32[64,64]{0,1:T(8,128)} %copy-done.12) | copy-start | bytes 49156
  207.3 0.8 copy-start.10
  207.3 2.2 copy-start.8
  207.3 257.1 %reduce-scatter.12.cloned.1.call-start = ((), (), s32[]{:S(2)}) async-start(), calls=%async_computation.8 | async-start | bytes 1179648 | tf_op jit(solution)/shard_map/reduce_scatter | solution.py:93
  209.5 333.1 %reduce-scatter.10.cloned.1.call-start = ((), (), s32[]{:S(2)}) async-start(), calls=%async_computation.7 | async-start | bytes 3538944 | tf_op jit(solution)/shard_map/reduce_scatter | solution.py:125
  246.3 296.3 %copy-start.1 = (bf16[256,1024]{1,0:T(8,128)(2,1)S(1)}, bf16[256,1024]{1,0:T(8,128)(2,1)}, u32[]{:S(2)}) copy-start(bf16[256,1024]{1,0:T(8,128)(2,1)} %param.16) | copy-start | bytes 1572868
Sparse Core Ops, SparseCore 0:
  46.4 34.7 all-reduce.5
  99.0 31.6 all-reduce.3
  136.7 61.8 reduce-scatter.15
  201.2 43.5 reduce-scatter.7
  248.2 149.0 reduce-scatter.13
  401.5 62.8 reduce-scatter.11
  468.6 73.9 reduce-scatter.9
where the time goes:
time: 551 us; the launch traced here: 549 us
  waiting for transfers between devices  372 us (68%)
  local copies, waits for them, and re-layouts  63.8 us (12%)
  other arithmetic  48.6 us (9%)
  matrix products  44 us (8%)
  between operations  14.6 us (3%)
  blocking collectives  5.76 us (1%)
    reduce_scatter x1, waiting for transfers between devices, on_device(): lax.psum_scatter(neg_term.at[row_slot, safe_block].add(gold_terms, mode='...  149 us
    reduce_scatter x1, waiting for transfers between devices, on_device(): lax.psum_scatter(jnp.concatenate([query_term[:, None, :], kv_term.reshape...  78.2 us
    reduce_scatter x1, waiting for transfers between devices, on_device(): lax.psum_scatter(wo_term, 'ment', scatter_dimension=1, tiled=True)  64.3 us
    psum x1, waiting for transfers between devices, on_device(): lax.psum(picked.astype(jnp.bfloat16), 'ent').astype(jnp.float32)  34.7 us
    psum x1, waiting for transfers between devices, on_device(): lax.psum(embed_part.astype(jnp.bfloat16), 'ent').astype(jnp.float32)  25.5 us
    reduce_scatter x1, waiting for transfers between devices, on_device(): lax.psum_scatter(token_term.at[:, 0, :].add(contract(query_gradient, w_qu...  19.8 us
    dot_general x9, matrix products, contract(): lax.dot_general(left, right, (((left_dim,), (right_dim,)), ((), ())), pre...  19.3 us
    unnamed x44, local copies, waits for them, and re-layouts  12.1 us
  transfers between devices with their start and end apart: 7, of which 6 were waited for; matrix products, arithmetic and copies ran while one was open for 17% of the time, Pallas kernels for 0%

commit v1 on v0

v1 whole, which is shorter than its diff:
```python
import functools

import jax
import jax.numpy as jnp
from jax import lax
from jax.experimental import pallas as pl
from jax.experimental.pallas import tpu as pltpu
from jax.sharding import PartitionSpec as P

HD = 64
EPS = 1e-06
GROUP = 8
LOW = -1e30
BF = jnp.bfloat16
F32 = jnp.float32
VMEM = pl.BlockSpec(memory_space=pltpu.VMEM)
SMEM = pl.BlockSpec(memory_space=pltpu.SMEM)


def mm(a, b):
    return jnp.dot(a, b, preferred_element_type=F32)


def mm_nt(a, b):
    return lax.dot_general(a, b, (((1,), (1,)), ((), ())), preferred_element_type=F32)


def mm_tn(a, b):
    return lax.dot_general(a, b, (((0,), (0,)), ((), ())), preferred_element_type=F32)


def sds(shape, dtype):
    return jax.ShapeDtypeStruct(shape, dtype)


def call(body, outs, ins, scratch=(), flops=0, moved=0, limit=40):
    smem = sum(1 for x in ins if x.ndim == 1 and x.dtype == jnp.int32)
    return pl.pallas_call(
        body,
        out_shape=outs,
        in_specs=[SMEM] * smem + [VMEM] * (len(ins) - smem),
        out_specs=[VMEM] * len(outs),
        scratch_shapes=list(scratch),
        compiler_params=pltpu.CompilerParams(vmem_limit_bytes=limit * 2**20),
        cost_estimate=pl.CostEstimate(flops=flops, bytes_accessed=moved, transcendentals=0),
    )(*ins)


def head_mask(heads, cols):
    head = lax.broadcasted_iota(jnp.int32, (1, heads, 1, cols), 1)
    col = lax.broadcasted_iota(jnp.int32, (1, heads, 1, cols), 3)
    return (col // HD == head).astype(F32)


def spread_heads(rows, heads):
    count, cols = rows.shape
    split = rows.reshape(count // GROUP, 1, GROUP, cols)
    return (split * head_mask(heads, cols)).reshape(heads * count, cols).astype(BF)


def pick_heads(rows, heads):
    count, cols = rows.shape
    split = rows.reshape(count // (heads * GROUP), heads, GROUP, cols)
    return jnp.sum(split * head_mask(heads, cols), axis=1).reshape(count // heads, cols)


def forward_body(
    ids, key_len, hid, w_ref, wo_ref, attn, cls_out, ctx_out, probs_out, mix_out, qx_out, *rest
):
    pays, buf = rest[:4], rest[4]
    tokens, width = hid.shape
    cols = w_ref.shape[2]
    heads = cols // HD
    count = key_len.shape[0]
    seq = tokens // count
    span = GROUP * seq
    rows = GROUP * heads
    groups = count // GROUP
    pick = lax.broadcasted_iota(jnp.int32, (GROUP, span), 1) == seq * lax.broadcasted_iota(
        jnp.int32, (GROUP, span), 0
    )
    pick = pick.astype(F32).astype(BF)
    cls = jnp.concatenate([mm(pick, hid[g * span : (g + 1) * span, :]) for g in range(groups)], axis=0)
    cls = cls.astype(BF)
    cls_out[...] = cls
    query = mm(cls, w_ref[0]).astype(BF).astype(F32)
    qx = spread_heads(query, heads)
    qx_out[...] = qx
    buf[:, 0:width] = mm_nt(qx, w_ref[1]).astype(BF)
    col = lax.broadcasted_iota(jnp.int32, (1, span), 1)
    row_ment = lax.broadcasted_iota(jnp.int32, (rows, span), 0) % GROUP
    diag = row_ment == lax.broadcasted_iota(jnp.int32, (rows, span), 1) // seq
    for g in range(groups):
        x = hid[g * span : (g + 1) * span, :]
        here = slice(g * rows, (g + 1) * rows)
        limit = jnp.zeros((1, span), jnp.int32)
        for m in range(GROUP):
            limit = jnp.where(col // seq == m, key_len[g * GROUP + m], limit)
        live = jnp.logical_and(diag, col % seq < limit)
        score = jnp.where(live, mm_nt(buf[here, 0:width], x) * HD ** (-0.5), LOW)
        expo = jnp.exp(score - jnp.max(score, axis=1, keepdims=True))
        expo = jnp.where(live, expo, 0.0)
        probs = expo / jnp.sum(expo, axis=1, keepdims=True)
        probs_out[here, :] = probs
        half = probs.astype(BF)
        buf[here, width : width + span] = half
        mix_out[here, :] = mm(half, x).astype(BF)
    ctx = pick_heads(mm(mix_out[...], w_ref[2]), heads).astype(BF)
    ctx_out[...] = ctx
    attn[...] = mm(ctx, wo_ref[...]).astype(BF)
    share = buf.shape[0] // 4
    for k in range(4):
        pays[k][...] = buf[pl.ds(pl.multiple_of((ids[1] ^ k) * share, share), share), :]


def as_column(row):
    n = row.shape[1]
    eye = lax.broadcasted_iota(jnp.int32, (n, n), 0) == lax.broadcasted_iota(jnp.int32, (n, n), 1)
    return jnp.sum(jnp.where(eye, row.astype(F32), 0.0), axis=1, keepdims=True)


def gold_place(gold_block, gold_row, first_block, block_rows):
    return as_column((gold_block[...] - first_block) * block_rows + gold_row[...]).astype(jnp.int32)


def gold_body(ids, gold_block, gold_row, table, _, gold_out):
    blocks, block_rows, width = table.shape
    place = gold_place(gold_block, gold_row, ids[1] * blocks, block_rows)
    total = jnp.zeros(gold_out.shape, F32)
    for b in range(blocks):
        at = lax.broadcasted_iota(jnp.int32, (gold_out.shape[0], block_rows), 1) + b * block_rows
        total += mm((at == place).astype(F32).astype(BF), table[b])
    gold_out[...] = total.astype(BF)


def candidates(ids, negs, place, tile_rows, blocks, block_rows, part):
    count = place.shape[0]
    col = lax.broadcasted_iota(jnp.int32, (1, blocks * tile_rows), 1)
    block = col // tile_rows
    at = block * block_rows + part * tile_rows + col % tile_rows
    hot = (at == place).astype(F32)
    named = block + ids[1] * blocks
    listed = named == negs[0]
    for k in range(1, negs.shape[0]):
        listed = jnp.logical_or(listed, named == negs[k])
    times = listed.astype(F32) + jnp.sum(hot, axis=0, keepdims=True)
    return hot, jnp.broadcast_to(times, (count, blocks * tile_rows))


def score_body(
    ids, negs, a0, a1, a2, a3, cls, gain, bias, gold_block, gold_row, table,
    embed_out, normed_out, rstd_out, score_out, pay,
):
    blocks, block_rows, width = table.shape
    parts = score_out.shape[0]
    tile_rows = block_rows // parts
    attn = (a0[...].astype(F32) + a1[...].astype(F32)) + (a2[...].astype(F32) + a3[...].astype(F32))
    resid = cls[...].astype(F32) + attn
    centre = resid - jnp.mean(resid, axis=1, keepdims=True)
    rstd = lax.rsqrt(jnp.mean(centre * centre, axis=1, keepdims=True) + EPS)
    normed = centre * rstd
    normed_out[...] = normed
    rstd_out[...] = jnp.broadcast_to(rstd, rstd_out.shape)
    embed = (normed * gain[...] + bias[...]).astype(BF)
    embed_out[...] = embed
    place = gold_place(gold_block, gold_row, ids[1] * blocks, block_rows)
    top = jnp.full((embed.shape[0], 1), LOW, F32)
    counts = []

    def tile(d):
        start = pl.multiple_of((ids[0] ^ d) * tile_rows, tile_rows)
        return table[:, pl.ds(start, tile_rows), :].reshape(blocks * tile_rows, width)

    for d in range(parts):
        score = mm_nt(embed, tile(d))
        score_out[d] = score
        _, times = candidates(ids, negs, place, tile_rows, blocks, block_rows, ids[0] ^ d)
        top = jnp.maximum(top, jnp.max(jnp.where(times > 0, score, LOW), axis=1, keepdims=True))
        counts.append(times)
    total = jnp.zeros((embed.shape[0], 1), F32)
    mean = jnp.zeros((embed.shape[0], width), F32)
    for d in range(parts):
        times = counts[d]
        expo = jnp.where(times > 0, times * jnp.exp(jnp.minimum(score_out[d] - top, 0.0)), 0.0)
        total += jnp.sum(expo, axis=1, keepdims=True)
        mean += mm(expo.astype(BF), tile(d))
    some = total > 0
    safe = jnp.where(some, total, 1.0)
    logsum = jnp.where(some, top + jnp.log(safe), LOW)
    pay[:, 0:width] = (mean / safe).astype(BF)
    high = logsum.astype(BF).astype(F32)
    mid = (logsum - high).astype(BF).astype(F32)
    low = logsum - high - mid
    lane = lax.broadcasted_iota(jnp.int32, (embed.shape[0], 128), 1)
    stats = jnp.where(lane == 0, high, jnp.where(lane == 1, mid, jnp.where(lane == 2, low, 0.0)))
    pay[:, width : width + 128] = stats.astype(BF)


def loss_body(
    ids, negs, p0, p1, p2, p3, g0, g1, g2, g3, normed_ref, rstd_ref, gain, score, gold_block, gold_row,
    w_ref, wo_ref, mix, dv_out, own_resid, vsend, vkeep, *rest,
):
    outs, (resid_buf, wide, grad_buf) = rest[:8], rest[8:]
    width = normed_ref.shape[1]
    parts, count, tile_cols = score.shape
    blocks = 8
    tile_rows = tile_cols // blocks
    heads = w_ref.shape[2] // HD
    pays = [p0, p1, p2, p3]
    logs = [jnp.sum(p[:, width : width + 128].astype(F32), axis=1, keepdims=True) for p in pays]
    top = jnp.maximum(jnp.maximum(logs[0], logs[1]), jnp.maximum(logs[2], logs[3]))
    lse = top + jnp.log(sum(jnp.exp(v - top) for v in logs))
    golds = (g0[...].astype(F32) + g1[...].astype(F32)) + (g2[...].astype(F32) + g3[...].astype(F32))
    d_embed = sum(jnp.exp(v - lse) * p[:, 0:width].astype(F32) for v, p in zip(logs, pays)) - golds
    normed = normed_ref[...]
    first = jnp.sum(d_embed * normed, axis=0, keepdims=True)
    second = jnp.sum(d_embed, axis=0, keepdims=True)
    first_high = first.astype(BF).astype(F32)
    second_high = second.astype(BF).astype(F32)
    line = lax.broadcasted_iota(jnp.int32, (16, width), 0)
    lines = jnp.where(line == 0, first_high, 0.0)
    lines = jnp.where(line == 1, second_high, lines)
    lines = jnp.where(line == 2, first - first_high, lines)
    lines = jnp.where(line == 3, second - second_high, lines)
    upper = d_embed * gain[...]
    d_resid = rstd_ref[:, 0:1] * (
        upper
        - jnp.mean(upper, axis=1, keepdims=True)
        - normed * jnp.mean(upper * normed, axis=1, keepdims=True)
    )
    resid_buf[...] = d_resid
    share = own_resid.shape[0]
    own_resid[...] = resid_buf[pl.ds(pl.multiple_of(ids[1] * share, share), share), :]
    half = d_resid.astype(BF)
    wide[0:count, :] = half
    wide[count : count + 16, :] = lines.astype(BF)
    d_ctx = mm_nt(half, wo_ref[...]).astype(BF).astype(F32)
    dx = spread_heads(d_ctx, heads)
    dv_out[...] = mm_nt(dx, w_ref[2]).astype(BF)
    grad_buf[...] = mm_tn(mix[...], dx)
    store_parts(ids, grad_buf, vsend, vkeep, 0)
    place = gold_place(gold_block, gold_row, ids[1] * blocks, parts * tile_rows)
    step = width // parts
    for d in range(parts):
        part = ids[0] ^ d
        hot, times = candidates(ids, negs, place, tile_rows, blocks, parts * tile_rows, part)
        expo = jnp.where(times > 0, times * jnp.exp(score[d] - lse), 0.0)
        outs[d][0:count, 0:tile_cols] = (expo - hot).astype(BF)
        outs[d][count : count + 16, 0:tile_cols] = jnp.zeros((16, tile_cols), BF)
        outs[d][:, tile_cols : tile_cols + step] = wide[:, pl.ds(pl.multiple_of(part * step, step), step)]


def store_parts(ids, grad_buf, send, keep, at):
    parts = 2 * send.shape[0]
    step = grad_buf.shape[0] // parts
    cols = grad_buf.shape[1]
    for d in range(parts):
        part = grad_buf[pl.ds(pl.multiple_of((ids[0] ^ d) * step, step), step), :]
        if d % 2:
            send[d // 2, :, at : at + cols] = part.astype(BF)
        else:
            keep[d // 2, :, at : at + cols] = part


def backward_body(
    ids, hid, w_ref, probs_ref, dv, qx, cls, send, keep, *rest
):
    pays, (tbuf, buf, grad_buf, zbuf) = rest[:4], rest[4:]
    tokens, width = hid.shape
    heads = w_ref.shape[2] // HD
    count = cls.shape[0]
    seq = tokens // count
    span = GROUP * seq
    rows = GROUP * heads
    for g in range(count // GROUP):
        x = hid[g * span : (g + 1) * span, :]
        here = slice(g * rows, (g + 1) * rows)
        probs = probs_ref[here, :]
        d_probs = mm_nt(dv[here, :], x)
        d_scores = probs * (d_probs - jnp.sum(probs * d_probs, axis=1, keepdims=True))
        half = (d_scores * HD ** (-0.5)).astype(BF)
        buf[here, :] = half
        tbuf[here, :] = mm(half, x).astype(BF)
    grad_buf[...] = mm_tn(tbuf[...], qx[...])
    store_parts(ids, grad_buf, send, keep, 0)
    d_query = pick_heads(mm(tbuf[...], w_ref[1]), heads).astype(BF)
    grad_buf[...] = mm_tn(cls[...], d_query)
    store_parts(ids, grad_buf, send, keep, grad_buf.shape[1])
    zbuf[...] = mm_nt(d_query, w_ref[0]).astype(BF)
    share = buf.shape[0] // 4
    few = count // 4
    for k in range(4):
        peer = ids[1] ^ k
        mine = pl.ds(pl.multiple_of(peer * share, share), share)
        pays[k][0:share, 0:width] = dv[mine, :]
        pays[k][0:share, width : width + span] = buf[mine, :]
        pays[k][share : share + few, 0:width] = zbuf[pl.ds(pl.multiple_of(peer * few, few), few), :]
        pays[k][share : share + few, width : width + span] = jnp.zeros((few, span), BF)


def pair_body(keep, got, own, s1, s2, s3):
    own[...] = keep[0] + got[0].astype(F32)
    for k, out in ((1, s1), (2, s2), (3, s3)):
        out[...] = (keep[k] + got[k].astype(F32)).astype(BF)


def hidden_body(e0, e1, e2, e3, l0, l1, l2, l3, own_resid, out):
    early, late = (e0, e1, e2, e3), (l0, l1, l2, l3)
    mentions, seq, width = out.shape
    share = early[0].shape[0]
    groups = mentions // GROUP
    rows = share // groups
    span = GROUP * seq
    first = own_resid[...]
    for part in late:
        first = first + part[share : share + mentions, 0:width].astype(F32)
    token = lax.broadcasted_iota(jnp.int32, (GROUP, seq, width), 1)
    for g in range(groups):
        here = slice(g * rows, (g + 1) * rows)
        left = [e[here, width : width + span] for e in early] + [v[here, width : width + span] for v in late]
        right = [v[here, 0:width] for v in late] + [e[here, 0:width] for e in early]
        grad = mm_tn(jnp.concatenate(left, axis=0), jnp.concatenate(right, axis=0))
        add = first[g * GROUP : (g + 1) * GROUP, :].reshape(GROUP, 1, width)
        grad = grad.reshape(GROUP, seq, width) + jnp.where(token == 0, add, 0.0)
        out[g * GROUP : (g + 1) * GROUP] = grad.astype(BF)


def table_body(*refs):
    ids = refs[0]
    w = refs[1:9]
    mine, theirs, out = refs[9:17], refs[17], refs[18]
    blocks, tile_rows, width = out.shape
    half = width // 2
    count = mine[0].shape[0]
    left = jnp.concatenate([r[0:count, 0 : blocks * tile_rows] for r in w], axis=0)
    right = jnp.concatenate([r[:, 0:half] for r in mine], axis=0)
    side = ids[1] & 1
    grad = mm_tn(left, right).reshape(blocks, tile_rows, half)
    out[:, :, pl.ds(pl.multiple_of(side * half, half), half)] = grad
    other = mm_tn(left, theirs[...]).reshape(blocks, tile_rows, half)
    out[:, :, pl.ds(pl.multiple_of((1 - side) * half, half), half)] = other


def small_body(*refs):
    w, got, wo_out, ln_out = refs[0:8], refs[8:16], refs[16], refs[17]
    cols = wo_out.shape[0]
    step = wo_out.shape[1]
    count = got[0].shape[0]
    at = w[0].shape[1] - step
    left = jnp.concatenate([r[:, r.shape[1] - cols : r.shape[1]] for r in got], axis=0)
    right = jnp.concatenate([r[0:count, at : at + step] for r in w], axis=0)
    wo_out[...] = mm_tn(left, right)
    lines = sum(r[count : count + 16, at : at + step].astype(F32) for r in w)
    ln_out[...] = lines[0:2, :] + lines[2:4, :]


def sum_body(v0, v1, v2, v3, b0, b1, b2, b3, out):
    cols = v0.shape[1]
    out[2] = (v0[...] + v1[...].astype(F32)) + (v2[...].astype(F32) + v3[...].astype(F32))
    both = (b0[...] + b1[...].astype(F32)) + (b2[...].astype(F32) + b3[...].astype(F32))
    out[1] = both[:, 0:cols]
    out[0] = both[:, cols : 2 * cols]


def swap(x, axis, size, k):
    return lax.ppermute(x, axis, [(i, i ^ k) for i in range(size)])


def after(x, *others):
    return lax.optimization_barrier((x, *others))[0]


def on_device(
    hidden_in, w_qkv, w_out, ln_gain, ln_bias, table, key_len, gold_block, gold_row, neg_blocks
):
    count, seq, width = hidden_in.shape
    cols = w_qkv.shape[2]
    heads = cols // HD
    blocks, block_rows = table.shape[0], table.shape[1]
    ments, ents = lax.axis_size("ment"), lax.axis_size("ent")
    parts = 8
    direct = ments == parts
    mine = lax.axis_index("ment") if direct else 0
    ids = jnp.stack([jnp.int32(mine), lax.axis_index("ent").astype(jnp.int32)])
    hid = hidden_in.reshape(count * seq, width)
    w = jnp.transpose(w_qkv, (1, 0, 2))
    gain, bias = ln_gain.reshape(1, width), ln_bias.reshape(1, width)
    g_block, g_row = gold_block.reshape(1, count), gold_row.reshape(1, count)
    negs = neg_blocks.reshape(neg_blocks.shape[1])
    span = GROUP * seq
    hrows = heads * count
    share = hrows // ents

    def ent(x, k):
        return swap(x, "ent", ents, k)

    def ment(x, k):
        return swap(x, "ment", ments, k)

    attn, cls, ctx, probs, mix, qx, *early = call(
        forward_body,
        [
            sds((count, width), BF),
            sds((count, width), BF),
            sds((count, cols), BF),
            sds((hrows, span), F32),
            sds((hrows, width), BF),
            sds((hrows, cols), BF),
        ]
        + [sds((share, width + span), BF)] * 4,
        [ids, key_len, hid, w, w_out],
        [pltpu.VMEM((hrows, width + span), BF)],
        flops=10**9,
        moved=8 * 2**20,
    )
    attns = [attn] + [ent(attn, k) for k in range(1, ents)]
    gold = call(
        gold_body,
        [sds((count, width), BF)],
        [ids, g_block, g_row, table, ctx],
        flops=3 * 10**8,
        moved=4 * 2**20,
    )[0]
    embed, normed, rstd, score, pay = call(
        score_body,
        [
            sds((count, width), BF),
            sds((count, width), F32),
            sds((count, 128), F32),
            sds((parts, count, blocks * block_rows // parts), F32),
            sds((count, width + 128), BF),
        ],
        [ids, negs, *attns, cls, gain, bias, g_block, g_row, table],
        flops=6 * 10**8,
        moved=6 * 2**20,
    )
    early_got = [early[0]] + [ent(after(e, attns[2]), k) for k, e in enumerate(early) if k]
    golds = [gold] + [ent(gold, k) for k in range(1, ents)]
    pays = [pay] + [ent(pay, k) for k in range(1, ents)]
    step = width // parts
    dv, own_resid, vsend, vkeep, *tiles = call(
        loss_body,
        [
            sds((hrows, width), BF),
            sds((count // ents, width), F32),
            sds((parts // 2, step, cols), BF),
            sds((parts // 2, step, cols), F32),
        ]
        + [sds((count + 16, blocks * block_rows // parts + step), BF)] * parts,
        [ids, negs, *pays, *golds, normed, rstd, gain, score, g_block, g_row, w, w_out, mix],
        [
            pltpu.VMEM((count, width), F32),
            pltpu.VMEM((count + 16, width), BF),
            pltpu.VMEM((width, cols), F32),
        ],
        flops=3 * 10**8,
        moved=6 * 2**20,
    )
    send, keep, *late = call(
        backward_body,
        [sds((parts // 2, step, 2 * cols), BF), sds((parts // 2, step, 2 * cols), F32)]
        + [sds((share + count // ents, width + span), BF)] * 4,
        [ids, hid, w, probs, dv, qx, cls],
        [
            pltpu.VMEM((hrows, width), BF),
            pltpu.VMEM((hrows, span), BF),
            pltpu.VMEM((width, cols), F32),
            pltpu.VMEM((count, width), BF),
        ],
        flops=10**9,
        moved=8 * 2**20,
    )
    late_got = [late[0]] + [ent(v, k) for k, v in enumerate(late) if k]
    grad_hidden = call(
        hidden_body,
        [sds((count // ents, seq, width), BF)],
        [*early_got, *late_got, own_resid],
        flops=3 * 10**8,
        moved=4 * 2**20,
    )[0]
    if not direct:
        return (grad_hidden, *any_size(embed, ctx, tiles, vsend, vkeep, send, keep, blocks, block_rows))

    def scatter(sent, kept):
        got = ment(sent, 1)
        own, *sums = call(
            pair_body,
            [sds(kept.shape[1:], F32)] + [sds(kept.shape[1:], BF)] * 3,
            [kept, got],
            moved=2 * 2**20,
        )
        return [own] + [ment(s, 2 * (k + 1)) for k, s in enumerate(sums)]

    side = lax.axis_index("ent") & 1
    half = width // 2
    packed = jnp.concatenate([lax.dynamic_slice_in_dim(embed, side * half, half, 1), ctx], axis=1)
    gathered = [packed] + [ment(packed, k) for k in range(1, parts)]
    theirs = ent(jnp.concatenate([g[:, :half] for g in gathered], axis=0), 1)
    w_got = [tiles[0]] + [ment(t, k) for k, t in enumerate(tiles) if k]
    vsum = scatter(vsend, vkeep)
    bsum = scatter(send, keep)
    grad_table = call(
        table_body,
        [sds((blocks, block_rows // parts, width), F32)],
        [ids, *w_got, *gathered, theirs],
        flops=3 * 10**8,
        moved=4 * 2**20,
    )[0]
    grad_wo, grad_ln = call(
        small_body,
        [sds((cols, step), F32), sds((2, step), F32)],
        [*w_got, *gathered],
        flops=10**8,
        moved=2**20,
    )
    grad_qkv = call(sum_body, [sds((3, step, cols), F32)], [*vsum, *bsum], moved=2**20)[0]
    return (grad_hidden, jnp.transpose(grad_qkv, (1, 0, 2)), grad_wo, grad_ln, grad_table)


def any_size(embed, ctx, tiles, vsend, vkeep, send, keep, blocks, block_rows):
    ments = lax.axis_size("ment")
    count, width = embed.shape
    parts = len(tiles)
    tile_rows = block_rows // parts
    step = width // parts
    stacked = jnp.stack(tiles)
    weights = stacked[:, :count, : blocks * tile_rows].reshape(parts, count, blocks, tile_rows)
    weights = jnp.transpose(weights, (1, 2, 0, 3)).reshape(count, blocks, ments, block_rows // ments)
    weights = lax.all_to_all(jnp.transpose(weights, (2, 0, 1, 3)), "ment", 0, 0)
    embeds = lax.all_gather(embed, "ment")
    grad_table = jnp.einsum("smbr,smd->brd", weights, embeds, preferred_element_type=F32)
    resid = jnp.transpose(stacked[:, :count, blocks * tile_rows :], (1, 0, 2)).reshape(count, ments, -1)
    resid = lax.all_to_all(jnp.transpose(resid, (1, 0, 2)), "ment", 0, 0)
    ctxs = lax.all_gather(ctx, "ment")
    grad_wo = jnp.einsum("smc,smd->cd", ctxs, resid, preferred_element_type=F32)
    lines = jnp.transpose(stacked[:, count:, blocks * tile_rows :], (1, 0, 2)).reshape(16, width).astype(F32)
    grad_ln = lax.psum_scatter(lines[0:2] + lines[2:4], "ment", scatter_dimension=1, tiled=True)

    def whole(sent, kept):
        both = jnp.stack([kept, sent.astype(F32)], axis=1)
        return both.reshape(width, kept.shape[2])

    value, both = whole(vsend, vkeep), whole(send, keep)
    cols = value.shape[1]
    stack = jnp.stack([both[:, cols:], both[:, :cols], value], axis=1)
    grad_qkv = lax.psum_scatter(stack, "ment", scatter_dimension=0, tiled=True)
    return grad_qkv, grad_wo, grad_ln, grad_table


def solution(mesh):
    placed = (
        P("ment", None, None),
        P(None, None, "ent"),
        P("ent", None),
        P(),
        P(),
        P("ent", None, None),
        P("ment"),
        P("ment"),
        P("ment"),
        P("ment", None),
    )
    return jax.shard_map(
        on_device,
        mesh=mesh,
        in_specs=placed,
        out_specs=(
            P(("ment", "ent"), None, None),
            P("ment", None, "ent"),
            P("ent", "ment"),
            P(None, "ment"),
            P("ent", "ment", None),
        ),
        check_vma=False,
    )
```

time: 551 us -> 130 us (0.24)
  waiting for transfers between devices: 372 us -> 49.6 us
  local copies, waits for them, and re-layouts: 63.8 us -> 7.57 us
  other arithmetic: 48.6 us -> 0.09 us
  starting transfers between devices: 0.69 us -> 46.4 us
  matrix products: 44 us -> 0 us
  Pallas kernels: 0 us -> 25.3 us
  between operations: 14.6 us -> 0.93 us
  blocking collectives: 5.76 us -> 0 us
    reduce_scatter x4 -> x0, waiting for transfers between devices: 312 us -> none  [the longest x1 149 us: on_device(): lax.psum_scatter(neg_term.at[row_slot, safe_block].add(gold_terms, mode='...]
    psum x2 -> x0, waiting for transfers between devices: 60.3 us -> none  [the longest x1 34.7 us: on_device(): lax.psum(picked.astype(jnp.bfloat16), 'ent').astype(jnp.float32)]
    ppermute x0 -> x38, waiting for transfers between devices: none -> 49.6 us  [swap(): return lax.ppermute(x, axis, [(i, i ^ k) for i in range(size)])]
    ppermute x0 -> x38, starting transfers between devices: none -> 46.4 us  [swap(): return lax.ppermute(x, axis, [(i, i ^ k) for i in range(size)])]
    dot_general x19 -> x0, matrix products: 44 us -> none  [the longest x9 19.3 us: contract(): lax.dot_general(left, right, (((left_dim,), (right_dim,)), ((), ())), pre...]
    pallas_call x0 -> x11, Pallas kernels: none -> 25.3 us  [call(): pl.pallas_call(body, out_shape=outs, in_specs=[SMEM] * smem + [VMEM] * (l...]
    convert_element_type x12 -> x0, other arithmetic: 17 us -> none  [the longest x1 6.01 us: on_device(): token_term.at[:, 0, :].add(contract(query_gradient, w_query, 1, 1))]
    scatter-add x1 -> x0, other arithmetic: 10.5 us -> none  [on_device(): neg_term.at[row_slot, safe_block].add(gold_terms, mode='drop')]
  transfers between devices with their start and end apart: 7 -> 38, of which waited for: 6 -> 13; matrix products, arithmetic and copies ran while one was open for 17% -> 0% of each run, Pallas kernels for 0% -> 11%
where the time goes in v1:
time: 130 us
  waiting for transfers between devices  49.6 us (38%)
  starting transfers between devices  46.4 us (36%)
  Pallas kernels  25.3 us (19%)
  local copies, waits for them, and re-layouts  7.57 us (6%)
    ppermute x38, waiting for transfers between devices, swap(): return lax.ppermute(x, axis, [(i, i ^ k) for i in range(size)])  49.6 us
    ppermute x38, starting transfers between devices, swap(): return lax.ppermute(x, axis, [(i, i ^ k) for i in range(size)])  46.4 us
    pallas_call x11, Pallas kernels, call(): pl.pallas_call(body, out_shape=outs, in_specs=[SMEM] * smem + [VMEM] * (l...  25.3 us
    unnamed x35, local copies, waits for them, and re-layouts  7.56 us
  transfers between devices with their start and end apart: 38, of which 13 were waited for; matrix products, arithmetic and copies ran while one was open for 0% of the time, Pallas kernels for 11%

profile of v1, /device:TPU:0, one launch (start us, length us, event | category | flops | bytes accessed | tf_op | source)
XLA Modules:
  0.0 129.8 jit_solution(6965918772187113103)
XLA Ops:
  0.8 2.2 %copy-done.2 = bf16[64,32,1024]{2,1,0:T(8,128)(2,1)S(1)} copy-done((bf16[64,32,1024]{2,1,0:T(8,128)(2,1)S(1)}, bf16[64,32,1024]{2,1,0:T(8,128)(2,1)}, u32[]{:S(2)}) %copy-start.2) | copy-done | bytes 4194328
  6.1 7.4 %shard_map.137 = (bf16[64,1024]{1,0:T(8,128)(2,1)S(1)}, bf16[64,1024]{1,0:T(8,128)(2,1)S(1)}, bf16[64,256]{1,0:T(8,128)(2,1)S(1)}, f32[256,256]{1,0:T(8,128)S(1)...) custom-call(s32[2]{0:T(128)S(1)} %pad_add_fusion.ids.refs_0_, ...), custom_call_target="tpu_custom_call" | custom-call | flops 1000000000 | bytes 8388608 | tf_op jit(solution)/shard_map/pallas_call | solution.py:38
  13.4 3.0 %collective-permute-start = (bf16[64,1024]{1,0:T(8,128)(2,1)S(1)}, bf16[64,1024]{1,0:T(8,128)(2,1)S(1)}, u32[]{:S(2)}, u32[]{:S(2)}) collective-permute-start(bf16[64,1024]{1,0:T(8,128)(2,1)S(1)} %get-tuple-element.53.a0), channel_id=1, source_target_pairs={{0,2},{1,3},{2,0},{3,1},{4,6},{5,7},{6,4},{7,5},{8,10},{9,11},{10,... | collective-permute-start | bytes 393224 | tf_op jit(solution)/shard_map/ppermute | solution.py:366
  16.7 3.7 %collective-permute-done.a2 = bf16[64,1024]{1,0:T(8,128)(2,1)S(1)} collective-permute-done((bf16[64,1024]{1,0:T(8,128)(2,1)S(1)}, bf16[64,1024]{1,0:T(8,128)(2,1)S(1)}, u32[]{:S(2)}, u32[]{:S(2)}) %collective-permute-start) | collective-permute-done | bytes 131104 | tf_op jit(solution)/shard_map/ppermute | solution.py:366
  20.4 1.9 %collective-permute-done.5.a3 = bf16[64,1024]{1,0:T(8,128)(2,1)S(1)} collective-permute-done((bf16[64,1024]{1,0:T(8,128)(2,1)S(1)}, bf16[64,1024]{1,0:T(8,128)(2,1)S(1)}, u32[]{:S(2)}, u32[]{:S(2)}) %collective-permute-start.5) | collective-permute-done | bytes 131104 | tf_op jit(solution)/shard_map/ppermute | solution.py:366
  22.4 2.2 %copy-done = bf16[8,256,1024]{2,1,0:T(8,128)(2,1)S(1)} copy-done((bf16[8,256,1024]{2,1,0:T(8,128)(2,1)S(1)}, bf16[8,256,1024]{2,1,0:T(8,128)(2,1)}, u32[]{:S(2)}) %copy-start) | copy-done | bytes 4194328
  24.6 3.0 %shard_map.138 = (bf16[64,1024]{1,0:T(8,128)(2,1)S(1)}, f32[64,1024]{1,0:T(8,128)S(1)}, f32[64,128]{1,0:T(8,128)S(1)}, f32[8,64,256]{2,1,0:T(8,128)S(1)}, bf16[64,1152]{1,0:T(8,128)(2,1)S(1)}) custom-call(s32[2]{0:T(128)S(1)} %pad_add_fusion.ids.refs_0_, s32[4]{0:T(128)S(1)} %bitcast.24, bf16[64,1024]{1,0:T(8,128)(2,1)S(1)} %get-tuple-element.53.a0, ...), custom_call_target="tpu_custom_call" | custom-call | flops 600000000 | bytes 6291456 | tf_op jit(solution)/shard_map/pallas_call | solution.py:38
  27.7 1.5 %collective-permute-start.30 = (bf16[64,768]{1,0:T(8,128)(2,1)S(1)}, bf16[64,768]{1,0:T(8,128)(2,1)S(1)}, u32[]{:S(2)}, u32[]{:S(2)}) collective-permute-start(bf16[64,768]{1,0:T(8,128)(2,1)S(1)} %pad_maximum_fusion.refs_8_.refs_9_), channel_id=1, source_target_pairs={{0,4},{4,0},{8,12},{12,8},{16,20},{20,16},{24,28},{28,24},{1,5},{5... | collective-permute-start | bytes 294920 | tf_op jit(solution)/shard_map/ppermute | solution.py:366
  30.9 1.5 %collective-permute-start.10 = (bf16[64,1024]{1,0:T(8,128)(2,1)S(1)}, bf16[64,1024]{1,0:T(8,128)(2,1)S(1)}, u32[]{:S(2)}, u32[]{:S(2)}) collective-permute-start(bf16[64,1024]{1,0:T(8,128)(2,1)S(1)} %shard_map.139.g0), channel_id=1, source_target_pairs={{0,2},{1,3},{2,0},{3,1},{4,6},{5,7},{6,4},{7,5},{8,10},{9,11},{10,... | collective-permute-start | bytes 393224 | tf_op jit(solution)/shard_map/ppermute | solution.py:366
  32.5 1.6 %collective-permute-start.31 = (bf16[64,768]{1,0:T(8,128)(2,1)S(1)}, bf16[64,768]{1,0:T(8,128)(2,1)S(1)}, u32[]{:S(2)}, u32[]{:S(2)}) collective-permute-start(bf16[64,768]{1,0:T(8,128)(2,1)S(1)} %pad_maximum_fusion.refs_8_.refs_9_), channel_id=1, source_target_pairs={{0,8},{4,12},{8,0},{12,4},{16,24},{20,28},{24,16},{28,20},{1,9},{5... | collective-permute-start | bytes 294920 | tf_op jit(solution)/shard_map/ppermute | solution.py:366
  35.4 2.7 %collective-permute-done.31.refs_10_.refs_11_ = bf16[64,768]{1,0:T(8,128)(2,1)S(1)} collective-permute-done((bf16[64,768]{1,0:T(8,128)(2,1)S(1)}, bf16[64,768]{1,0:T(8,128)(2,1)S(1)}, u32[]{:S(2)}, u32[]{:S(2)}) %collective-permute-start.31) | collective-permute-done | bytes 98336 | tf_op jit(solution)/shard_map/ppermute | solution.py:366
  38.1 2.6 %collective-permute-start.33 = (bf16[64,768]{1,0:T(8,128)(2,1)S(1)}, bf16[64,768]{1,0:T(8,128)(2,1)S(1)}, u32[]{:S(2)}, u32[]{:S(2)}) collective-permute-start(bf16[64,768]{1,0:T(8,128)(2,1)S(1)} %pad_maximum_fusion.refs_8_.refs_9_), channel_id=1, source_target_pairs={{0,16},{4,20},{8,24},{12,28},{16,0},{20,4},{24,8},{28,12},{1,17},{... | collective-permute-start | bytes 294920 | tf_op jit(solution)/shard_map/ppermute | solution.py:366
  40.7 2.7 %collective-permute-start.34 = (bf16[64,768]{1,0:T(8,128)(2,1)S(1)}, bf16[64,768]{1,0:T(8,128)(2,1)S(1)}, u32[]{:S(2)}, u32[]{:S(2)}) collective-permute-start(bf16[64,768]{1,0:T(8,128)(2,1)S(1)} %pad_maximum_fusion.refs_8_.refs_9_), channel_id=1, source_target_pairs={{0,20},{4,16},{8,28},{12,24},{16,4},{20,0},{24,12},{28,8},{1,21},{... | collective-permute-start | bytes 294920 | tf_op jit(solution)/shard_map/ppermute | solution.py:366
  43.4 4.6 %collective-permute-done.33.refs_12_.refs_13_ = bf16[64,768]{1,0:T(8,128)(2,1)S(1)} collective-permute-done((bf16[64,768]{1,0:T(8,128)(2,1)S(1)}, bf16[64,768]{1,0:T(8,128)(2,1)S(1)}, u32[]{:S(2)}, u32[]{:S(2)}) %collective-permute-start.33) | collective-permute-done | bytes 98336 | tf_op jit(solution)/shard_map/ppermute | solution.py:366
  48.0 3.4 %collective-permute-start.35 = (bf16[64,768]{1,0:T(8,128)(2,1)S(1)}, bf16[64,768]{1,0:T(8,128)(2,1)S(1)}, u32[]{:S(2)}, u32[]{:S(2)}) collective-permute-start(bf16[64,768]{1,0:T(8,128)(2,1)S(1)} %pad_maximum_fusion.refs_8_.refs_9_), channel_id=1, source_target_pairs={{0,24},{4,28},{8,16},{12,20},{16,8},{20,12},{24,0},{28,4},{1,25},{... | collective-permute-start | bytes 294920 | tf_op jit(solution)/shard_map/ppermute | solution.py:366
  51.5 1.5 %collective-permute-start.7 = (bf16[64,1152]{1,0:T(8,128)(2,1)S(1)}, bf16[64,1152]{1,0:T(8,128)(2,1)S(1)}, u32[]{:S(2)}, u32[]{:S(2)}) collective-permute-start(bf16[64,1152]{1,0:T(8,128)(2,1)S(1)} %get-tuple-element.61.p0), channel_id=1, source_target_pairs={{0,2},{1,3},{2,0},{3,1},{4,6},{5,7},{6,4},{7,5},{8,10},{9,11},{10,... | collective-permute-start | bytes 442376 | tf_op jit(solution)/shard_map/ppermute | solution.py:366
  53.0 1.5 %collective-permute-done.35.refs_14_.refs_15_ = bf16[64,768]{1,0:T(8,128)(2,1)S(1)} collective-permute-done((bf16[64,768]{1,0:T(8,128)(2,1)S(1)}, bf16[64,768]{1,0:T(8,128)(2,1)S(1)}, u32[]{:S(2)}, u32[]{:S(2)}) %collective-permute-start.35) | collective-permute-done | bytes 98336 | tf_op jit(solution)/shard_map/ppermute | solution.py:366
  54.5 3.0 %collective-permute-start.36 = (bf16[64,768]{1,0:T(8,128)(2,1)S(1)}, bf16[64,768]{1,0:T(8,128)(2,1)S(1)}, u32[]{:S(2)}, u32[]{:S(2)}) collective-permute-start(bf16[64,768]{1,0:T(8,128)(2,1)S(1)} %pad_maximum_fusion.refs_8_.refs_9_), channel_id=1, source_target_pairs={{0,28},{4,24},{8,20},{12,16},{16,12},{20,8},{24,4},{28,0},{1,29},{... | collective-permute-start | bytes 294920 | tf_op jit(solution)/shard_map/ppermute | solution.py:366
  60.7 2.0 %shard_map.140 = (bf16[256,1024]{1,0:T(8,128)(2,1)S(1)}, f32[16,1024]{1,0:T(8,128)S(1)}, bf16[4,128,256]{2,1,0:T(8,128)(2,1)S(1)}, f32[4,128,256]{2,1,0:T(8,128)...) custom-call(s32[2]{0:T(128)S(1)} %pad_add_fusion.ids.refs_0_, ...), custom_call_target="tpu_custom_call" | custom-call | flops 300000000 | bytes 6291456 | tf_op jit(solution)/shard_map/pallas_call | solution.py:38
  64.1 6.1 %shard_map.141 = (bf16[4,128,512]{2,1,0:T(8,128)(2,1)S(1)}, f32[4,128,512]{2,1,0:T(8,128)S(1)}, bf16[80,1280]{1,0:T(8,128)(2,1)S(1)}, bf16[80,1280]{1,0:T(8,128)...) custom-call(s32[2]{0:T(128)S(1)} %pad_add_fusion.ids.refs_0_, bf16[2048,1024]{1,0:T(8,128)(2,1)S(1)} %bitcast.11, ...), custom_call_target="tpu_custom_call" | custom-call | flops 1000000000 | bytes 8388608 | tf_op jit(solution)/shard_map/pallas_call | solution.py:38
  71.1 1.5 %collective-permute-start.23 = (bf16[80,384]{1,0:T(8,128)(2,1)S(1)}, bf16[80,384]{1,0:T(8,128)(2,1)S(1)}, u32[]{:S(2)}, u32[]{:S(2)}) collective-permute-start(bf16[80,384]{1,0:T(8,128)(2,1)S(1)} %get-tuple-element.87), channel_id=1, source_target_pairs={{0,4},{4,0},{8,12},{12,8},{16,20},{20,16},{24,28},{28,24},{1,5},{5... | collective-permute-start | bytes 184328 | tf_op jit(solution)/shard_map/ppermute | solution.py:366
  72.6 13.3 %collective-permute-done.23.refs_1_.refs_2_ = bf16[80,384]{1,0:T(8,128)(2,1)S(1)} collective-permute-done((bf16[80,384]{1,0:T(8,128)(2,1)S(1)}, bf16[80,384]{1,0:T(8,128)(2,1)S(1)}, u32[]{:S(2)}, u32[]{:S(2)}) %collective-permute-start.23) | collective-permute-done | bytes 61472 | tf_op jit(solution)/shard_map/ppermute | solution.py:366
  85.9 3.2 %collective-permute-start.26 = (bf16[80,384]{1,0:T(8,128)(2,1)S(1)}, bf16[80,384]{1,0:T(8,128)(2,1)S(1)}, u32[]{:S(2)}, u32[]{:S(2)}) collective-permute-start(bf16[80,384]{1,0:T(8,128)(2,1)S(1)} %get-tuple-element.90), channel_id=1, source_target_pairs={{0,16},{4,20},{8,24},{12,28},{16,0},{20,4},{24,8},{28,12},{1,17},{... | collective-permute-start | bytes 184328 | tf_op jit(solution)/shard_map/ppermute | solution.py:366
  89.1 1.9 %collective-permute-done.25.refs_3_.refs_4_ = bf16[80,384]{1,0:T(8,128)(2,1)S(1)} collective-permute-done((bf16[80,384]{1,0:T(8,128)(2,1)S(1)}, bf16[80,384]{1,0:T(8,128)(2,1)S(1)}, u32[]{:S(2)}, u32[]{:S(2)}) %collective-permute-start.25) | collective-permute-done | bytes 61472 | tf_op jit(solution)/shard_map/ppermute | solution.py:366
  93.4 4.2 %collective-permute-done.27.refs_5_.refs_6_ = bf16[80,384]{1,0:T(8,128)(2,1)S(1)} collective-permute-done((bf16[80,384]{1,0:T(8,128)(2,1)S(1)}, bf16[80,384]{1,0:T(8,128)(2,1)S(1)}, u32[]{:S(2)}, u32[]{:S(2)}) %collective-permute-start.27) | collective-permute-done | bytes 61472 | tf_op jit(solution)/shard_map/ppermute | solution.py:366
  97.7 3.1 %collective-permute-start.29 = (bf16[80,384]{1,0:T(8,128)(2,1)S(1)}, bf16[80,384]{1,0:T(8,128)(2,1)S(1)}, u32[]{:S(2)}, u32[]{:S(2)}) collective-permute-start(bf16[80,384]{1,0:T(8,128)(2,1)S(1)} %get-tuple-element.93), channel_id=1, source_target_pairs={{0,28},{4,24},{8,20},{12,16},{16,12},{20,8},{24,4},{28,0},{1,29},{... | collective-permute-start | bytes 184328 | tf_op jit(solution)/shard_map/ppermute | solution.py:366
  100.8 3.8 %collective-permute-done.29.refs_7_.refs_8_ = bf16[80,384]{1,0:T(8,128)(2,1)S(1)} collective-permute-done((bf16[80,384]{1,0:T(8,128)(2,1)S(1)}, bf16[80,384]{1,0:T(8,128)(2,1)S(1)}, u32[]{:S(2)}, u32[]{:S(2)}) %collective-permute-start.29) | collective-permute-done | bytes 61472 | tf_op jit(solution)/shard_map/ppermute | solution.py:366
  105.6 2.1 %collective-permute-start.20 = (bf16[128,512]{1,0:T(8,128)(2,1)S(1)}, bf16[128,512]{1,0:T(8,128)(2,1)S(1)}, u32[]{:S(2)}, u32[]{:S(2)}) collective-permute-start(bf16[128,512]{1,0:T(8,128)(2,1)S(1)} %get-tuple-element.83), channel_id=1, source_target_pairs={{0,8},{4,12},{8,0},{12,4},{16,24},{20,28},{24,16},{28,20},{1,9},{5... | collective-permute-start | bytes 393224 | tf_op jit(solution)/shard_map/ppermute | solution.py:366
  107.7 4.6 %collective-permute-done.13.l2 = bf16[80,1280]{1,0:T(8,128)(2,1)S(1)} collective-permute-done((bf16[80,1280]{1,0:T(8,128)(2,1)S(1)}, bf16[80,1280]{1,0:T(8,128)(2,1)S(1)}, u32[]{:S(2)}, u32[]{:S(2)}) %collective-permute-start.13) | collective-permute-done | bytes 204832 | tf_op jit(solution)/shard_map/ppermute | solution.py:366
  113.0 3.1 %collective-permute-start.22 = (bf16[128,512]{1,0:T(8,128)(2,1)S(1)}, bf16[128,512]{1,0:T(8,128)(2,1)S(1)}, u32[]{:S(2)}, u32[]{:S(2)}) collective-permute-start(bf16[128,512]{1,0:T(8,128)(2,1)S(1)} %get-tuple-element.85), channel_id=1, source_target_pairs={{0,24},{4,28},{8,16},{12,20},{16,8},{20,12},{24,0},{28,4},{1,25},{... | collective-permute-start | bytes 393224 | tf_op jit(solution)/shard_map/ppermute | solution.py:366
  120.9 2.0 %shard_map.147 = f32[8,32,1024]{2,1,0:T(8,128)} custom-call(s32[2]{0:T(128)S(1)} %pad_add_fusion.ids.refs_0_, bf16[80,384]{1,0:T(8,128)(2,1)S(1)} %get-tuple-element.86.refs_0_.refs_1_, bf16[80,384]{1,0:T(8,128)(2,1)S(1)} %collective-permute-done.23.refs_1_.refs_2_, bf16[80,384]{1,0:T(8,128)(2,1)S(1)} %collective-permute-done.24.refs_2_.refs_3_, ...), custom_call_target="tpu_custom_call" | custom-call | flops 300000000 | bytes 4194304 | tf_op jit(solution)/shard_map/pallas_call | solution.py:38
  122.9 6.1 %collective-permute-done.17.v2 = bf16[128,256]{1,0:T(8,128)(2,1)S(1)} collective-permute-done((bf16[128,256]{1,0:T(8,128)(2,1)S(1)}, bf16[128,256]{1,0:T(8,128)(2,1)S(1)}, u32[]{:S(2)}, u32[]{:S(2)}) %collective-permute-start.17) | collective-permute-done | bytes 65568 | tf_op jit(solution)/shard_map/ppermute | solution.py:366
  (93 shorter events, 22.0 us)
Async XLA Ops:
  13.4 7.0 %collective-permute-start = (bf16[64,1024]{1,0:T(8,128)(2,1)S(1)}, bf16[64,1024]{1,0:T(8,128)(2,1)S(1)}, u32[]{:S(2)}, u32[]{:S(2)}) collective-permute-start(bf16[64,1024]{1,0:T(8,128)(2,1)S(1)} %get-tuple-element.53.a0), channel_id=1, source_target_pairs={{0,2},{1,3},{2,0},{3,1},{4,6},{5,7},{6,4},{7,5},{8,10},{9,11},{10,... | collective-permute-start | bytes 393224 | tf_op jit(solution)/shard_map/ppermute | solution.py:366
  27.7 6.5 %collective-permute-start.30 = (bf16[64,768]{1,0:T(8,128)(2,1)S(1)}, bf16[64,768]{1,0:T(8,128)(2,1)S(1)}, u32[]{:S(2)}, u32[]{:S(2)}) collective-permute-start(bf16[64,768]{1,0:T(8,128)(2,1)S(1)} %pad_maximum_fusion.refs_8_.refs_9_), channel_id=1, source_target_pairs={{0,4},{4,0},{8,12},{12,8},{16,20},{20,16},{24,28},{28,24},{1,5},{5... | collective-permute-start | bytes 294920 | tf_op jit(solution)/shard_map/ppermute | solution.py:366
  30.6 20.9 %collective-permute-start.9 = (bf16[64,1024]{1,0:T(8,128)(2,1)S(1)}, bf16[64,1024]{1,0:T(8,128)(2,1)S(1)}, u32[]{:S(2)}, u32[]{:S(2)}) collective-permute-start(bf16[64,1024]{1,0:T(8,128)(2,1)S(1)} %shard_map.139.g0), channel_id=1, source_target_pairs={{0,1},{1,0},{2,3},{3,2},{4,5},{5,4},{6,7},{7,6},{8,9},{9,8},{10,11... | collective-permute-start | bytes 393224 | tf_op jit(solution)/shard_map/ppermute | solution.py:366
  30.9 23.6 %collective-permute-start.10 = (bf16[64,1024]{1,0:T(8,128)(2,1)S(1)}, bf16[64,1024]{1,0:T(8,128)(2,1)S(1)}, u32[]{:S(2)}, u32[]{:S(2)}) collective-permute-start(bf16[64,1024]{1,0:T(8,128)(2,1)S(1)} %shard_map.139.g0), channel_id=1, source_target_pairs={{0,2},{1,3},{2,0},{3,1},{4,6},{5,7},{6,4},{7,5},{8,10},{9,11},{10,... | collective-permute-start | bytes 393224 | tf_op jit(solution)/shard_map/ppermute | solution.py:366
  32.5 25.0 %collective-permute-start.11 = (bf16[64,1024]{1,0:T(8,128)(2,1)S(1)}, bf16[64,1024]{1,0:T(8,128)(2,1)S(1)}, u32[]{:S(2)}, u32[]{:S(2)}) collective-permute-start(bf16[64,1024]{1,0:T(8,128)(2,1)S(1)} %shard_map.139.g0), channel_id=1, source_target_pairs={{0,3},{1,2},{2,1},{3,0},{4,7},{5,6},{6,5},{7,4},{8,11},{9,10},{10,... | collective-permute-start | bytes 393224 | tf_op jit(solution)/shard_map/ppermute | solution.py:366
  34.1 6.6 %collective-permute-start.32 = (bf16[64,768]{1,0:T(8,128)(2,1)S(1)}, bf16[64,768]{1,0:T(8,128)(2,1)S(1)}, u32[]{:S(2)}, u32[]{:S(2)}) collective-permute-start(bf16[64,768]{1,0:T(8,128)(2,1)S(1)} %pad_maximum_fusion.refs_8_.refs_9_), channel_id=1, source_target_pairs={{0,12},{4,8},{8,4},{12,0},{16,28},{20,24},{24,20},{28,16},{1,13},{... | collective-permute-start | bytes 294920 | tf_op jit(solution)/shard_map/ppermute | solution.py:366
  38.1 9.9 %collective-permute-start.33 = (bf16[64,768]{1,0:T(8,128)(2,1)S(1)}, bf16[64,768]{1,0:T(8,128)(2,1)S(1)}, u32[]{:S(2)}, u32[]{:S(2)}) collective-permute-start(bf16[64,768]{1,0:T(8,128)(2,1)S(1)} %pad_maximum_fusion.refs_8_.refs_9_), channel_id=1, source_target_pairs={{0,16},{4,20},{8,24},{12,28},{16,0},{20,4},{24,8},{28,12},{1,17},{... | collective-permute-start | bytes 294920 | tf_op jit(solution)/shard_map/ppermute | solution.py:366
  40.7 10.7 %collective-permute-start.34 = (bf16[64,768]{1,0:T(8,128)(2,1)S(1)}, bf16[64,768]{1,0:T(8,128)(2,1)S(1)}, u32[]{:S(2)}, u32[]{:S(2)}) collective-permute-start(bf16[64,768]{1,0:T(8,128)(2,1)S(1)} %pad_maximum_fusion.refs_8_.refs_9_), channel_id=1, source_target_pairs={{0,20},{4,16},{8,28},{12,24},{16,4},{20,0},{24,12},{28,8},{1,21},{... | collective-permute-start | bytes 294920 | tf_op jit(solution)/shard_map/ppermute | solution.py:366
  48.0 6.5 %collective-permute-start.35 = (bf16[64,768]{1,0:T(8,128)(2,1)S(1)}, bf16[64,768]{1,0:T(8,128)(2,1)S(1)}, u32[]{:S(2)}, u32[]{:S(2)}) collective-permute-start(bf16[64,768]{1,0:T(8,128)(2,1)S(1)} %pad_maximum_fusion.refs_8_.refs_9_), channel_id=1, source_target_pairs={{0,24},{4,28},{8,16},{12,20},{16,8},{20,12},{24,0},{28,4},{1,25},{... | collective-permute-start | bytes 294920 | tf_op jit(solution)/shard_map/ppermute | solution.py:366
  51.4 7.5 %collective-permute-start.6 = (bf16[64,1152]{1,0:T(8,128)(2,1)S(1)}, bf16[64,1152]{1,0:T(8,128)(2,1)S(1)}, u32[]{:S(2)}, u32[]{:S(2)}) collective-permute-start(bf16[64,1152]{1,0:T(8,128)(2,1)S(1)} %get-tuple-element.61.p0), channel_id=1, source_target_pairs={{0,1},{1,0},{2,3},{3,2},{4,5},{5,4},{6,7},{7,6},{8,9},{9,8},{10,11... | collective-permute-start | bytes 442376 | tf_op jit(solution)/shard_map/ppermute | solution.py:366
  51.5 7.8 %collective-permute-start.7 = (bf16[64,1152]{1,0:T(8,128)(2,1)S(1)}, bf16[64,1152]{1,0:T(8,128)(2,1)S(1)}, u32[]{:S(2)}, u32[]{:S(2)}) collective-permute-start(bf16[64,1152]{1,0:T(8,128)(2,1)S(1)} %get-tuple-element.61.p0), channel_id=1, source_target_pairs={{0,2},{1,3},{2,0},{3,1},{4,6},{5,7},{6,4},{7,5},{8,10},{9,11},{10,... | collective-permute-start | bytes 442376 | tf_op jit(solution)/shard_map/ppermute | solution.py:366
  54.5 15.7 %collective-permute-start.36 = (bf16[64,768]{1,0:T(8,128)(2,1)S(1)}, bf16[64,768]{1,0:T(8,128)(2,1)S(1)}, u32[]{:S(2)}, u32[]{:S(2)}) collective-permute-start(bf16[64,768]{1,0:T(8,128)(2,1)S(1)} %pad_maximum_fusion.refs_8_.refs_9_), channel_id=1, source_target_pairs={{0,28},{4,24},{8,20},{12,16},{16,12},{20,8},{24,4},{28,0},{1,29},{... | collective-permute-start | bytes 294920 | tf_op jit(solution)/shard_map/ppermute | solution.py:366
  57.5 13.5 %collective-permute-start.1 = (bf16[64,1280]{1,0:T(8,128)(2,1)S(1)}, bf16[64,1280]{1,0:T(8,128)(2,1)S(1)}, u32[]{:S(2)}, u32[]{:S(2)}) collective-permute-start(bf16[64,1280]{1,0:T(8,128)(2,1)S(1)} %get-tuple-element.54), channel_id=1, source_target_pairs={{0,1},{1,0},{2,3},{3,2},{4,5},{5,4},{6,7},{7,6},{8,9},{9,8},{10,11... | collective-permute-start | bytes 491528 | tf_op jit(solution)/shard_map/ppermute | solution.py:366
  58.9 12.2 %collective-permute-start.2 = (bf16[64,1280]{1,0:T(8,128)(2,1)S(1)}, bf16[64,1280]{1,0:T(8,128)(2,1)S(1)}, u32[]{:S(2)}, u32[]{:S(2)}) collective-permute-start(bf16[64,1280]{1,0:T(8,128)(2,1)S(1)} %get-tuple-element.56), channel_id=1, source_target_pairs={{0,2},{1,3},{2,0},{3,1},{4,6},{5,7},{6,4},{7,5},{8,10},{9,11},{10,... | collective-permute-start | bytes 491528 | tf_op jit(solution)/shard_map/ppermute | solution.py:366
  59.3 13.2 %collective-permute-start.3 = (bf16[64,1280]{1,0:T(8,128)(2,1)S(1)}, bf16[64,1280]{1,0:T(8,128)(2,1)S(1)}, u32[]{:S(2)}, u32[]{:S(2)}) collective-permute-start(bf16[64,1280]{1,0:T(8,128)(2,1)S(1)} %get-tuple-element.58), channel_id=1, source_target_pairs={{0,3},{1,2},{2,1},{3,0},{4,7},{5,6},{6,5},{7,4},{8,11},{9,10},{10,... | collective-permute-start | bytes 491528 | tf_op jit(solution)/shard_map/ppermute | solution.py:366
  62.7 42.7 %collective-permute-start.15 = (bf16[4,128,256]{2,1,0:T(8,128)(2,1)S(1)}, bf16[4,128,256]{2,1,0:T(8,128)(2,1)S(1)}, u32[]{:S(2)}, u32[]{:S(2)}) collective-permute-start(bf16[4,128,256]{2,1,0:T(8,128)(2,1)S(1)} %get-tuple-element.75), channel_id=1, source_target_pairs={{0,4},{4,0},{8,12},{12,8},{16,20},{20,16},{24,28},{28,24},{1,5},{5... | collective-permute-start | bytes 786440 | tf_op jit(solution)/shard_map/ppermute | solution.py:366
  70.2 35.2 %collective-permute-start.19 = (bf16[4,128,512]{2,1,0:T(8,128)(2,1)S(1)}, bf16[4,128,512]{2,1,0:T(8,128)(2,1)S(1)}, u32[]{:S(2)}, u32[]{:S(2)}) collective-permute-start(bf16[4,128,512]{2,1,0:T(8,128)(2,1)S(1)} %get-tuple-element.81), channel_id=1, source_target_pairs={{0,4},{4,0},{8,12},{12,8},{16,20},{20,16},{24,28},{28,24},{1,5},{5... | collective-permute-start | bytes 1572872 | tf_op jit(solution)/shard_map/ppermute | solution.py:366
  71.0 46.5 %collective-permute-start.37 = (bf16[512,512]{1,0:T(8,128)(2,1)S(1)}, bf16[512,512]{1,0:T(8,128)(2,1)S(1)}, u32[]{:S(2)}, u32[]{:S(2)}) collective-permute-start(bf16[512,512]{1,0:T(8,128)(2,1)S(1)} %slice_dynamic-update-slice_fusion), channel_id=1, source_target_pairs={{0,1},{1,0},{2,3},{3,2},{4,5},{5,4},{6,7},{7,6},{8,9},{9,8},{10,11... | collective-permute-start | bytes 1572872 | tf_op jit(solution)/shard_map/ppermute | solution.py:366
  71.1 14.8 %collective-permute-start.23 = (bf16[80,384]{1,0:T(8,128)(2,1)S(1)}, bf16[80,384]{1,0:T(8,128)(2,1)S(1)}, u32[]{:S(2)}, u32[]{:S(2)}) collective-permute-start(bf16[80,384]{1,0:T(8,128)(2,1)S(1)} %get-tuple-element.87), channel_id=1, source_target_pairs={{0,4},{4,0},{8,12},{12,8},{16,20},{20,16},{24,28},{28,24},{1,5},{5... | collective-permute-start | bytes 184328 | tf_op jit(solution)/shard_map/ppermute | solution.py:366
  72.6 13.3 %collective-permute-start.24 = (bf16[80,384]{1,0:T(8,128)(2,1)S(1)}, bf16[80,384]{1,0:T(8,128)(2,1)S(1)}, u32[]{:S(2)}, u32[]{:S(2)}) collective-permute-start(bf16[80,384]{1,0:T(8,128)(2,1)S(1)} %get-tuple-element.88), channel_id=1, source_target_pairs={{0,8},{4,12},{8,0},{12,4},{16,24},{20,28},{24,16},{28,20},{1,9},{5... | collective-permute-start | bytes 184328 | tf_op jit(solution)/shard_map/ppermute | solution.py:366
  85.9 6.4 %collective-permute-start.26 = (bf16[80,384]{1,0:T(8,128)(2,1)S(1)}, bf16[80,384]{1,0:T(8,128)(2,1)S(1)}, u32[]{:S(2)}, u32[]{:S(2)}) collective-permute-start(bf16[80,384]{1,0:T(8,128)(2,1)S(1)} %get-tuple-element.90), channel_id=1, source_target_pairs={{0,16},{4,20},{8,24},{12,28},{16,0},{20,4},{24,8},{28,12},{1,17},{... | collective-permute-start | bytes 184328 | tf_op jit(solution)/shard_map/ppermute | solution.py:366
  91.0 6.7 %collective-permute-start.27 = (bf16[80,384]{1,0:T(8,128)(2,1)S(1)}, bf16[80,384]{1,0:T(8,128)(2,1)S(1)}, u32[]{:S(2)}, u32[]{:S(2)}) collective-permute-start(bf16[80,384]{1,0:T(8,128)(2,1)S(1)} %get-tuple-element.91), channel_id=1, source_target_pairs={{0,20},{4,16},{8,28},{12,24},{16,4},{20,0},{24,12},{28,8},{1,21},{... | collective-permute-start | bytes 184328 | tf_op jit(solution)/shard_map/ppermute | solution.py:366
  92.3 8.5 %collective-permute-start.28 = (bf16[80,384]{1,0:T(8,128)(2,1)S(1)}, bf16[80,384]{1,0:T(8,128)(2,1)S(1)}, u32[]{:S(2)}, u32[]{:S(2)}) collective-permute-start(bf16[80,384]{1,0:T(8,128)(2,1)S(1)} %get-tuple-element.92), channel_id=1, source_target_pairs={{0,24},{4,28},{8,16},{12,20},{16,8},{20,12},{24,0},{28,4},{1,25},{... | collective-permute-start | bytes 184328 | tf_op jit(solution)/shard_map/ppermute | solution.py:366
  97.7 6.9 %collective-permute-start.29 = (bf16[80,384]{1,0:T(8,128)(2,1)S(1)}, bf16[80,384]{1,0:T(8,128)(2,1)S(1)}, u32[]{:S(2)}, u32[]{:S(2)}) collective-permute-start(bf16[80,384]{1,0:T(8,128)(2,1)S(1)} %get-tuple-element.93), channel_id=1, source_target_pairs={{0,28},{4,24},{8,20},{12,16},{16,12},{20,8},{24,4},{28,0},{1,29},{... | collective-permute-start | bytes 184328 | tf_op jit(solution)/shard_map/ppermute | solution.py:366
  104.6 7.7 %collective-permute-start.13 = (bf16[80,1280]{1,0:T(8,128)(2,1)S(1)}, bf16[80,1280]{1,0:T(8,128)(2,1)S(1)}, u32[]{:S(2)}, u32[]{:S(2)}) collective-permute-start(bf16[80,1280]{1,0:T(8,128)(2,1)S(1)} %get-tuple-element.71), channel_id=1, source_target_pairs={{0,2},{1,3},{2,0},{3,1},{4,6},{5,7},{6,4},{7,5},{8,10},{9,11},{10,... | collective-permute-start | bytes 614408 | tf_op jit(solution)/shard_map/ppermute | solution.py:366
  105.4 7.7 %collective-permute-start.14 = (bf16[80,1280]{1,0:T(8,128)(2,1)S(1)}, bf16[80,1280]{1,0:T(8,128)(2,1)S(1)}, u32[]{:S(2)}, u32[]{:S(2)}) collective-permute-start(bf16[80,1280]{1,0:T(8,128)(2,1)S(1)} %get-tuple-element.72), channel_id=1, source_target_pairs={{0,3},{1,2},{2,1},{3,0},{4,7},{5,6},{6,5},{7,4},{8,11},{9,10},{10,... | collective-permute-start | bytes 614408 | tf_op jit(solution)/shard_map/ppermute | solution.py:366
  105.5 10.7 %collective-permute-start.16 = (bf16[128,256]{1,0:T(8,128)(2,1)S(1)}, bf16[128,256]{1,0:T(8,128)(2,1)S(1)}, u32[]{:S(2)}, u32[]{:S(2)}) collective-permute-start(bf16[128,256]{1,0:T(8,128)(2,1)S(1)} %get-tuple-element.77), channel_id=1, source_target_pairs={{0,8},{4,12},{8,0},{12,4},{16,24},{20,28},{24,16},{28,20},{1,9},{5... | collective-permute-start | bytes 196616 | tf_op jit(solution)/shard_map/ppermute | solution.py:366
  105.6 23.3 %collective-permute-start.20 = (bf16[128,512]{1,0:T(8,128)(2,1)S(1)}, bf16[128,512]{1,0:T(8,128)(2,1)S(1)}, u32[]{:S(2)}, u32[]{:S(2)}) collective-permute-start(bf16[128,512]{1,0:T(8,128)(2,1)S(1)} %get-tuple-element.83), channel_id=1, source_target_pairs={{0,8},{4,12},{8,0},{12,4},{16,24},{20,28},{24,16},{28,20},{1,9},{5... | collective-permute-start | bytes 393224 | tf_op jit(solution)/shard_map/ppermute | solution.py:366
  112.3 16.7 %collective-permute-start.21 = (bf16[128,512]{1,0:T(8,128)(2,1)S(1)}, bf16[128,512]{1,0:T(8,128)(2,1)S(1)}, u32[]{:S(2)}, u32[]{:S(2)}) collective-permute-start(bf16[128,512]{1,0:T(8,128)(2,1)S(1)} %get-tuple-element.84), channel_id=1, source_target_pairs={{0,16},{4,20},{8,24},{12,28},{16,0},{20,4},{24,8},{28,12},{1,17},{... | collective-permute-start | bytes 393224 | tf_op jit(solution)/shard_map/ppermute | solution.py:366
  113.0 15.9 %collective-permute-start.22 = (bf16[128,512]{1,0:T(8,128)(2,1)S(1)}, bf16[128,512]{1,0:T(8,128)(2,1)S(1)}, u32[]{:S(2)}, u32[]{:S(2)}) collective-permute-start(bf16[128,512]{1,0:T(8,128)(2,1)S(1)} %get-tuple-element.85), channel_id=1, source_target_pairs={{0,24},{4,28},{8,16},{12,20},{16,8},{20,12},{24,0},{28,4},{1,25},{... | collective-permute-start | bytes 393224 | tf_op jit(solution)/shard_map/ppermute | solution.py:366
  116.2 12.8 %collective-permute-start.17 = (bf16[128,256]{1,0:T(8,128)(2,1)S(1)}, bf16[128,256]{1,0:T(8,128)(2,1)S(1)}, u32[]{:S(2)}, u32[]{:S(2)}) collective-permute-start(bf16[128,256]{1,0:T(8,128)(2,1)S(1)} %get-tuple-element.78), channel_id=1, source_target_pairs={{0,16},{4,20},{8,24},{12,28},{16,0},{20,4},{24,8},{28,12},{1,17},{... | collective-permute-start | bytes 196616 | tf_op jit(solution)/shard_map/ppermute | solution.py:366
  117.5 11.4 %collective-permute-start.18 = (bf16[128,256]{1,0:T(8,128)(2,1)S(1)}, bf16[128,256]{1,0:T(8,128)(2,1)S(1)}, u32[]{:S(2)}, u32[]{:S(2)}) collective-permute-start(bf16[128,256]{1,0:T(8,128)(2,1)S(1)} %get-tuple-element.79), channel_id=1, source_target_pairs={{0,24},{4,28},{8,16},{12,20},{16,8},{20,12},{24,0},{28,4},{1,25},{... | collective-permute-start | bytes 196616 | tf_op jit(solution)/shard_map/ppermute | solution.py:366
  (20 other events, 260.9 us)

commit v2 on v1

v2 whole, which is shorter than its diff:
```python
import functools

import jax
import jax.numpy as jnp
from jax import lax
from jax.experimental import pallas as pl
from jax.experimental.pallas import tpu as pltpu
from jax.sharding import PartitionSpec as P

HD = 64
EPS = 1e-06
GROUP = 8
LOW = -1e30
BF = jnp.bfloat16
F32 = jnp.float32
VMEM = pl.BlockSpec(memory_space=pltpu.VMEM)
SMEM = pl.BlockSpec(memory_space=pltpu.SMEM)
HBM = pl.BlockSpec(memory_space=pltpu.HBM)


def mm(a, b):
    return jnp.dot(a, b, preferred_element_type=F32)


def mm_nt(a, b):
    return lax.dot_general(a, b, (((1,), (1,)), ((), ())), preferred_element_type=F32)


def mm_tn(a, b):
    return lax.dot_general(a, b, (((0,), (0,)), ((), ())), preferred_element_type=F32)


def sds(shape, dtype):
    return jax.ShapeDtypeStruct(shape, dtype)


def call(body, outs, ins, scratch=(), flops=0, moved=0, limit=20, outside=0):
    smem = sum(1 for x in ins if x.ndim == 1 and x.dtype == jnp.int32)
    inside = len(ins) - smem - outside
    return pl.pallas_call(
        body,
        out_shape=outs,
        in_specs=[SMEM] * smem + [VMEM] * inside + [HBM] * outside,
        out_specs=[VMEM] * len(outs),
        scratch_shapes=list(scratch),
        compiler_params=pltpu.CompilerParams(vmem_limit_bytes=limit * 2**20),
        cost_estimate=pl.CostEstimate(flops=flops, bytes_accessed=moved, transcendentals=0),
    )(*ins)


def head_mask(heads, cols):
    head = lax.broadcasted_iota(jnp.int32, (1, heads, 1, cols), 1)
    col = lax.broadcasted_iota(jnp.int32, (1, heads, 1, cols), 3)
    return (col // HD == head).astype(F32)


def spread_heads(rows, heads):
    count, cols = rows.shape
    split = rows.reshape(count // GROUP, 1, GROUP, cols)
    return (split * head_mask(heads, cols)).reshape(heads * count, cols).astype(BF)


def pick_heads(rows, heads):
    count, cols = rows.shape
    split = rows.reshape(count // (heads * GROUP), heads, GROUP, cols)
    return jnp.sum(split * head_mask(heads, cols), axis=1).reshape(count // heads, cols)


def forward_body(
    key_len, hid_in, w_in, wo_in, attn, cls_out, ctx_out, probs_out, mix_out, qx_out, qk_out, fold_out,
    hid, w_ref, wo_ref, sems,
):
    tokens, width = hid.shape
    cols = w_ref.shape[2]
    heads = cols // HD
    count = key_len.shape[0]
    seq = tokens // count
    span = GROUP * seq
    rows = GROUP * heads
    groups = count // GROUP
    part = [pltpu.make_async_copy(w_in.at[0], w_ref.at[0], sems.at[groups])]
    part += [
        pltpu.make_async_copy(
            hid_in.at[pl.ds(g * span, span), :], hid.at[pl.ds(g * span, span), :], sems.at[g]
        )
        for g in range(groups)
    ]
    part += [pltpu.make_async_copy(w_in.at[k], w_ref.at[k], sems.at[groups + k]) for k in (1, 2)]
    part += [pltpu.make_async_copy(wo_in, wo_ref, sems.at[groups + 3])]
    for copy in part:
        copy.start()
    pick = lax.broadcasted_iota(jnp.int32, (GROUP, span), 1) == seq * lax.broadcasted_iota(
        jnp.int32, (GROUP, span), 0
    )
    pick = pick.astype(F32).astype(BF)
    firsts = []
    for g in range(groups):
        part[1 + g].wait()
        firsts.append(mm(pick, hid[g * span : (g + 1) * span, :]))
    cls = jnp.concatenate(firsts, axis=0).astype(BF)
    cls_out[...] = cls
    part[0].wait()
    query = mm(cls, w_ref[0]).astype(BF).astype(F32)
    qx = spread_heads(query, heads)
    qx_out[...] = qx
    part[groups + 1].wait()
    qk_out[...] = mm_nt(qx, w_ref[1]).astype(BF)
    fold = fold_matrix(span, seq, 0)
    col = lax.broadcasted_iota(jnp.int32, (1, span), 1)
    diag = diagonal(rows, span, seq)
    for g in range(groups):
        x = hid[g * span : (g + 1) * span, :]
        here = slice(g * rows, (g + 1) * rows)
        limit = jnp.zeros((1, span), jnp.int32)
        for m in range(GROUP):
            limit = jnp.where(col // seq == m, key_len[g * GROUP + m], limit)
        live = jnp.logical_and(diag, col % seq < limit)
        score = jnp.where(live, mm_nt(qk_out[here, :], x) * HD ** (-0.5), LOW)
        expo = jnp.exp(score - jnp.max(score, axis=1, keepdims=True))
        expo = jnp.where(live, expo, 0.0)
        probs = expo / jnp.sum(expo, axis=1, keepdims=True)
        probs_out[here, :] = probs
        half = probs.astype(BF)
        fold_out[here, :] = mm(half, fold).astype(BF)
        mix_out[here, :] = mm(half, x).astype(BF)
    part[groups + 2].wait()
    ctx = pick_heads(mm(mix_out[...], w_ref[2]), heads).astype(BF)
    ctx_out[...] = ctx
    part[groups + 3].wait()
    attn[...] = mm(ctx, wo_ref[...]).astype(BF)


def diagonal(rows, span, seq):
    row = lax.broadcasted_iota(jnp.int32, (rows, span), 0) % GROUP
    return row == lax.broadcasted_iota(jnp.int32, (rows, span), 1) // seq


def fold_matrix(span, seq, at):
    token = lax.broadcasted_iota(jnp.int32, (span, 128), 0) % seq
    lane = lax.broadcasted_iota(jnp.int32, (span, 128), 1)
    return (token + at == lane).astype(F32).astype(BF)


def unfold(lines, rows, span, seq, at):
    token = lax.broadcasted_iota(jnp.int32, (128, span), 1) % seq
    lane = lax.broadcasted_iota(jnp.int32, (128, span), 0)
    wide = mm(lines, (token + at == lane).astype(F32).astype(BF))
    return jnp.where(diagonal(rows, span, seq), wide, 0.0).astype(BF)


def as_column(row):
    n = row.shape[1]
    eye = lax.broadcasted_iota(jnp.int32, (n, n), 0) == lax.broadcasted_iota(jnp.int32, (n, n), 1)
    return jnp.sum(jnp.where(eye, row.astype(F32), 0.0), axis=1, keepdims=True)


def as_row(column):
    n = column.shape[0]
    eye = lax.broadcasted_iota(jnp.int32, (n, n), 0) == lax.broadcasted_iota(jnp.int32, (n, n), 1)
    return jnp.sum(jnp.where(eye, column, 0.0), axis=0, keepdims=True)


def three(x):
    high = x.astype(BF).astype(F32)
    mid = (x - high).astype(BF).astype(F32)
    return high, mid, x - high - mid


def score_body(
    ids, negs, parts, cls, gain, bias, gold_block, gold_row, table, ctx,
    embed_out, normed_out, rstd_out, pay, packed, rows_out, score_buf,
):
    blocks, block_rows, width = table.shape
    count = cls.shape[0]
    half = width // 2
    cols = ctx.shape[1]
    attn = sum(parts[k].astype(F32) for k in range(parts.shape[0]))
    resid = cls[...].astype(F32) + attn
    centre = resid - jnp.mean(resid, axis=1, keepdims=True)
    rstd = lax.rsqrt(jnp.mean(centre * centre, axis=1, keepdims=True) + EPS)
    normed = centre * rstd
    normed_out[...] = normed
    rstd_out[...] = jnp.broadcast_to(rstd, rstd_out.shape)
    embed = (normed * gain[...] + bias[...]).astype(BF)
    embed_out[...] = embed
    first = ids[1] * blocks
    g_block, g_row = as_column(gold_block[...]), as_column(gold_row[...])
    side = ids[1] & 1
    packed[:, 0:half] = embed_out[:, pl.ds(pl.multiple_of(side * half, half), half)]
    packed[:, half : half + cols] = ctx[...]
    tile_rows = rows_out.shape[1]
    rows_out[...] = table[:, pl.ds(pl.multiple_of(ids[0] * tile_rows, tile_rows), tile_rows), :]
    place = (g_block - first.astype(F32)) * block_rows + g_row
    top = jnp.full((count, 1), LOW, F32)
    counts = []
    for b in range(blocks):
        score = mm_nt(embed, table[b])
        score_buf[b] = score
        at = lax.broadcasted_iota(jnp.int32, (count, block_rows), 1) + b * block_rows
        hot = (at.astype(F32) == place).astype(F32)
        times = jnp.sum(hot, axis=0, keepdims=True)
        listed = jnp.int32(0)
        for k in range(negs.shape[0]):
            listed = jnp.where(negs[k] == first + b, 1, listed)
        times = jnp.broadcast_to(times + listed.astype(F32), (count, block_rows))
        top = jnp.maximum(top, jnp.max(jnp.where(times > 0, score, LOW), axis=1, keepdims=True))
        counts.append((times, hot))
    total = jnp.zeros((count, 1), F32)
    mean = jnp.zeros((2 * count, width), F32)
    for b in range(blocks):
        times, hot = counts[b]
        expo = jnp.where(times > 0, times * jnp.exp(jnp.minimum(score_buf[b] - top, 0.0)), 0.0)
        total += jnp.sum(expo, axis=1, keepdims=True)
        mean += mm(jnp.concatenate([expo, hot], axis=0).astype(BF), table[b])
    some = total > 0
    safe = jnp.where(some, total, 1.0)
    store_mean(pay, mean[0:count] / safe, jnp.where(some, top + jnp.log(safe), LOW))
    pay[:, width + 128 :] = mean[count:].astype(BF)


def store_mean(pay, mean, logsum):
    count, width = mean.shape
    pay[:, 0:width] = mean.astype(BF)
    high, mid, low = three(logsum)
    lane = lax.broadcasted_iota(jnp.int32, (count, 128), 1)
    stats = jnp.where(lane == 0, high, jnp.where(lane == 1, mid, jnp.where(lane == 2, low, 0.0)))
    pay[:, width : width + 128] = stats.astype(BF)


def merge_means(p, q, width):
    one, two = [jnp.sum(v[:, width : width + 128].astype(F32), axis=1, keepdims=True) for v in (p, q)]
    top = jnp.maximum(one, two)
    logsum = top + jnp.log(jnp.exp(one - top) + jnp.exp(two - top))
    mean = jnp.exp(one - logsum) * p[:, 0:width].astype(F32)
    golds = p[:, width + 128 :].astype(F32) + q[:, width + 128 :].astype(F32)
    return mean + jnp.exp(two - logsum) * q[:, 0:width].astype(F32), logsum, golds


def merge_body(p, q, out):
    width = (out.shape[1] - 128) // 2
    mean, logsum, golds = merge_means(p[...], q[...], width)
    store_mean(out, mean, logsum)
    out[:, width + 128 :] = golds.astype(BF)


def loss_body(
    ids, negs, p0, p1, normed_ref, rstd_ref, gain, w_ref, wo_ref, mix, gold_block, gold_row,
    dv_out, own_resid, vsend, vkeep, wide, resid_buf, grad_buf,
):
    count, width = normed_ref.shape
    heads = w_ref.shape[2] // HD
    mean, lse, golds = merge_means(p0[...], p1[...], width)
    d_embed = mean - golds
    normed = normed_ref[...]
    upper = d_embed * gain[...]
    d_resid = rstd_ref[:, 0:1] * (
        upper
        - jnp.mean(upper, axis=1, keepdims=True)
        - normed * jnp.mean(upper * normed, axis=1, keepdims=True)
    )
    half = d_resid.astype(BF)
    d_ctx = mm_nt(half, wo_ref[...]).astype(BF).astype(F32)
    dx = spread_heads(d_ctx, heads)
    dv_out[...] = mm_nt(dx, w_ref[2]).astype(BF)
    grad_buf[...] = mm_tn(mix[...], dx)
    store_parts(ids, grad_buf, vsend, vkeep)
    resid_buf[...] = d_resid
    share = own_resid.shape[0]
    own_resid[...] = resid_buf[pl.ds(pl.multiple_of(ids[1] * share, share), share), :]
    first = jnp.sum(d_embed * normed, axis=0, keepdims=True)
    second = jnp.sum(d_embed, axis=0, keepdims=True)
    first_high = first.astype(BF).astype(F32)
    second_high = second.astype(BF).astype(F32)
    lane = lax.broadcasted_iota(jnp.int32, (1, count), 1)
    lists = jnp.zeros((1, count), F32)
    for k in range(negs.shape[0]):
        lists = jnp.where(lane == k, negs[k].astype(F32), lists)
    logs = [*three(as_row(lse)), gold_block[...].astype(F32), gold_row[...].astype(F32), lists]
    logs = [jnp.concatenate([v] * (width // count), axis=1) for v in logs]
    line = lax.broadcasted_iota(jnp.int32, (16, width), 0)
    lines = jnp.zeros((16, width), F32)
    for k, v in enumerate(
        [first_high, second_high, first - first_high, second - second_high] + logs
    ):
        lines = jnp.where(line == k, v, lines)
    wide[0:count, :] = half
    wide[count : count + 16, :] = lines.astype(BF)


def store_parts(ids, grad_buf, send, keep):
    parts = 2 * send.shape[0]
    step = grad_buf.shape[0] // parts
    for d in range(parts):
        part = grad_buf[pl.ds(pl.multiple_of((ids[0] ^ d) * step, step), step), :]
        if d % 2:
            send[d // 2] = part.astype(BF)
        else:
            keep[d // 2] = part


def backward_body(
    ids, hid, w_ref, probs_ref, dv, qk, folded, far, near, own, tbuf, d_query_out, buf, zbuf
):
    tokens, width = hid.shape
    heads = w_ref.shape[2] // HD
    count = d_query_out.shape[0]
    seq = tokens // count
    span = GROUP * seq
    rows = GROUP * heads
    fold = fold_matrix(span, seq, seq)
    for g in range(count // GROUP):
        x = hid[g * span : (g + 1) * span, :]
        here = slice(g * rows, (g + 1) * rows)
        probs = probs_ref[here, :]
        d_probs = mm_nt(dv[here, :], x)
        d_scores = probs * (d_probs - jnp.sum(probs * d_probs, axis=1, keepdims=True))
        half = (d_scores * HD ** (-0.5)).astype(BF)
        buf[here, :] = (folded[here, :].astype(F32) + mm(half, fold)).astype(BF)
        tbuf[here, :] = mm(half, x).astype(BF)
    d_query = pick_heads(mm(tbuf[...], w_ref[1]), heads).astype(BF)
    d_query_out[...] = d_query
    zbuf[...] = mm_nt(d_query, w_ref[0]).astype(BF)
    share = dv.shape[0] // 4
    few = count // 4
    for k, out in ((0, own), (1, near), (2, far.at[0]), (3, far.at[1])):
        peer = ids[1] ^ k
        mine = pl.ds(pl.multiple_of(peer * share, share), share)
        out[0:share, 0:width] = dv[mine, :]
        out[0:share, width : 2 * width] = qk[mine, :]
        out[0:share, 2 * width :] = buf[mine, :]
        out[share : share + few, 0:width] = zbuf[pl.ds(pl.multiple_of(peer * few, few), few), :]
        out[share : share + few, width:] = jnp.zeros((few, width + 128), BF)


def spread_body(tbuf, qx, d_query, cls, wide, spread, grad_buf):
    count, width = cls.shape
    cols = qx.shape[1]
    grad_buf[...] = mm_tn(tbuf[...], qx[...])
    step = width // spread.shape[0]
    at = (step, step + count, step + 2 * count)
    for r in range(spread.shape[0]):
        here = slice(r * step, (r + 1) * step)
        spread[r, 0:step, :] = grad_buf[here, :].astype(BF)
        spread[r, at[0] : at[1], :] = d_query[...]
        spread[r, at[1] : at[2], 0:step] = cls[:, here]
        spread[r, at[1] : at[2], step : 2 * step] = wide[0:count, here]
        spread[r, at[2] :, 0:step] = wide[count:, here]
        spread[r, at[2] :, step:] = jnp.zeros((16, spread.shape[2] - step), BF)


def fold_x_body(keep, got, kept, sent):
    for k in range(2):
        kept[k] = keep[2 * k] + got[2 * k].astype(F32)
        sent[k] = (keep[2 * k + 1] + got[2 * k + 1].astype(F32)).astype(BF)


def fold_z_body(keep, got, kept, sent):
    kept[...] = keep[0] + got[0].astype(F32)
    sent[...] = (keep[1] + got[1].astype(F32)).astype(BF)


def hidden_body(p0, p1, p2, p3, own_resid, out):
    pays = (p0, p1, p2, p3)
    mentions, seq, width = out.shape
    share = p0.shape[0] - mentions
    groups = mentions // GROUP
    rows = share // groups
    span = GROUP * seq
    first = own_resid[...]
    for p in pays:
        first = first + p[share : share + mentions, 0:width].astype(F32)
    token = lax.broadcasted_iota(jnp.int32, (GROUP, seq, width), 1)
    for g in range(groups):
        here = slice(g * rows, (g + 1) * rows)
        left = [unfold(p[here, 2 * width :], rows, span, seq, 0) for p in pays]
        left += [unfold(p[here, 2 * width :], rows, span, seq, seq) for p in pays]
        right = [p[here, 0:width] for p in pays] + [p[here, width : 2 * width] for p in pays]
        grad = mm_tn(jnp.concatenate(left, axis=0), jnp.concatenate(right, axis=0))
        add = first[g * GROUP : (g + 1) * GROUP, :].reshape(GROUP, 1, width)
        grad = grad.reshape(GROUP, seq, width) + jnp.where(token == 0, add, 0.0)
        out[g * GROUP : (g + 1) * GROUP] = grad.astype(BF)


ORDER = (0, 4, 2, 6, 1, 5, 3, 7)


def table_body(listings, ids, mine_all, other_all, spread, rows_ref, out, weights):
    blocks, tile_rows, width = out.shape
    half = width // 2
    count = mine_all.shape[1]
    at = spread.shape[1] - 16
    step = width // spread.shape[0]
    tile = blocks * tile_rows
    side = ids[1] & 1
    mine = pl.ds(pl.multiple_of(side * half, half), half)
    theirs = pl.ds(pl.multiple_of((1 - side) * half, half), half)
    rows_mine = rows_ref[:, :, mine].reshape(tile, half)
    rows_theirs = rows_ref[:, :, theirs].reshape(tile, half)
    sources = [mine_all[k] for k in range(mine_all.shape[0])]
    others = [other_all[k] for k in range(mine_all.shape[0])]
    left = jnp.concatenate([s[:, 0:half] for s in sources], axis=0)
    right = jnp.concatenate([s[:, 0:half] for s in others], axis=0)
    score = mm_nt(left, rows_mine) + mm_nt(right, rows_theirs)
    col = lax.broadcasted_iota(jnp.int32, (1, tile), 1)
    block = (col // tile_rows + ids[1] * blocks).astype(F32)
    row = (col % tile_rows + ids[0] * tile_rows).astype(F32)
    for d, source in enumerate(sources):
        lines = spread[ids[0] ^ ORDER[d], at:, 0:count].astype(F32)
        lse = as_column(lines[4:5] + lines[5:6] + lines[6:7])
        hot = jnp.logical_and(as_column(lines[7:8]) == block, as_column(lines[8:9]) == row).astype(F32)
        times = jnp.sum(hot, axis=0, keepdims=True)
        listed = jnp.zeros((1, tile), F32)
        for k in range(listings):
            listed = jnp.where(lines[9:10, k : k + 1] == block, 1.0, listed)
        times = jnp.broadcast_to(times + listed, (count, tile))
        expo = jnp.exp(score[d * count : (d + 1) * count, :] - lse)
        expo = jnp.where(times > 0, times * expo, 0.0)
        weights[d * count : (d + 1) * count, :] = (expo - hot).astype(BF)
    out[:, :, mine] = mm_tn(weights[...], left).reshape(blocks, tile_rows, half)
    out[:, :, theirs] = mm_tn(weights[...], right).reshape(blocks, tile_rows, half)


def small_body(ids, gathered, spread, v0, v1, qkv_out, wo_out, ln_out):
    cols, step = wo_out.shape
    count = gathered.shape[1]
    at = gathered.shape[2] - cols
    parts = spread.shape[0]
    rows = (step, step + count, step + 2 * count)
    left = [gathered[d, :, at : at + cols] for d in range(parts)]
    right = [spread[ids[0] ^ d, rows[1] : rows[2], step : 2 * step] for d in ORDER]
    wo_out[...] = mm_tn(jnp.concatenate(left, axis=0), jnp.concatenate(right, axis=0))
    total = sum(spread[r, rows[2] :, 0:step].astype(F32) for r in range(parts))
    ln_out[...] = total[0:2, :] + total[2:4, :]
    left = [spread[r, rows[1] : rows[2], 0:step] for r in range(parts)]
    right = [spread[r, rows[0] : rows[1], :] for r in range(parts)]
    qkv_out[0] = mm_tn(jnp.concatenate(left, axis=0), jnp.concatenate(right, axis=0))
    qkv_out[1] = sum(spread[r, 0:step, :].astype(F32) for r in range(parts))
    qkv_out[2] = v0[...] + v1[...].astype(F32)


def swap(x, axis, size, k):
    return lax.ppermute(x, axis, [(i, i ^ k) for i in range(size)])


def after(x, *others):
    return lax.optimization_barrier((x, *others))[0]


def on_device(
    hidden_in, w_qkv, w_out, ln_gain, ln_bias, table, key_len, gold_block, gold_row, neg_blocks
):
    count, seq, width = hidden_in.shape
    cols = w_qkv.shape[2]
    heads = cols // HD
    blocks, block_rows = table.shape[0], table.shape[1]
    ments, ents = lax.axis_size("ment"), lax.axis_size("ent")
    parts = 8
    direct = ments == parts
    mine = lax.axis_index("ment") if direct else 0
    ids = jnp.stack([jnp.int32(mine), lax.axis_index("ent").astype(jnp.int32)])
    hid = hidden_in.reshape(count * seq, width)
    w = jnp.transpose(w_qkv, (1, 0, 2))
    gain, bias = ln_gain.reshape(1, width), ln_bias.reshape(1, width)
    g_block, g_row = gold_block.reshape(1, count), gold_row.reshape(1, count)
    negs = neg_blocks.reshape(neg_blocks.shape[1])
    span = GROUP * seq
    hrows = heads * count
    share = hrows // ents
    few = count // ents
    step = width // parts
    pairs = parts // 2

    def ent(x, k):
        return swap(x, "ent", ents, k)

    def ment(x, k):
        return swap(x, "ment", ments, k)

    attn, cls, ctx, probs, mix, qx, qk, folded = call(
        forward_body,
        [
            sds((count, width), BF),
            sds((count, width), BF),
            sds((count, cols), BF),
            sds((hrows, span), F32),
            sds((hrows, width), BF),
            sds((hrows, cols), BF),
            sds((hrows, width), BF),
            sds((hrows, 128), BF),
        ],
        [key_len, hid, w, w_out],
        [
            pltpu.VMEM(hid.shape, BF),
            pltpu.VMEM(w.shape, BF),
            pltpu.VMEM(w_out.shape, BF),
            pltpu.SemaphoreType.DMA((count // GROUP + 4,)),
        ],
        flops=10**9,
        moved=8 * 2**20,
        limit=60,
        outside=3,
    )
    attns = lax.all_gather(attn, "ent")
    embed, normed, rstd, pay, packed, table_rows = call(
        score_body,
        [
            sds((count, width), BF),
            sds((count, width), F32),
            sds((count, 128), F32),
            sds((count, 2 * width + 128), BF),
            sds((count, width // 2 + cols), BF),
            sds((blocks, block_rows // parts, width), BF),
        ],
        [ids, negs, attns, cls, gain, bias, g_block, g_row, table, ctx],
        [pltpu.VMEM((blocks, count, block_rows), F32)],
        flops=6 * 10**8,
        moved=6 * 2**20,
    )
    pay_pair = call(merge_body, [sds(pay.shape, BF)], [pay, ent(pay, 1)], moved=2**19)[0]
    pay_other = ent(pay_pair, 2)
    dv, own_resid, vsend, vkeep, wide = call(
        loss_body,
        [
            sds((hrows, width), BF),
            sds((few, width), F32),
            sds((pairs, step, cols), BF),
            sds((pairs, step, cols), F32),
            sds((count + 16, width), BF),
        ],
        [ids, negs, pay_pair, pay_other, normed, rstd, gain, w, w_out, mix, g_block, g_row],
        [pltpu.VMEM((count, width), F32), pltpu.VMEM((width, cols), F32)],
        flops=3 * 10**8,
        moved=6 * 2**20,
    )
    far, near, own, mixed, d_query = call(
        backward_body,
        [
            sds((2, share + few, 2 * width + 128), BF),
            sds((share + few, 2 * width + 128), BF),
            sds((share + few, 2 * width + 128), BF),
            sds((hrows, width), BF),
            sds((count, cols), BF),
        ],
        [ids, hid, w, probs, dv, qk, folded],
        [pltpu.VMEM((hrows, 128), BF), pltpu.VMEM((count, width), BF)],
        flops=10**9,
        moved=8 * 2**20,
    )
    spread = call(
        spread_body,
        [sds((parts, step + 2 * count + 16, cols), BF)],
        [mixed, qx, d_query, cls, wide],
        [pltpu.VMEM((width, cols), F32)],
        flops=10**8,
        moved=3 * 2**20,
    )[0]
    far_got = ent(far, 2)
    pays = [own, ent(near, 1), far_got[0], ent(far_got[1], 1)]
    grad_hidden = call(
        hidden_body,
        [sds((few, seq, width), BF)],
        [*pays, own_resid],
        flops=3 * 10**8,
        moved=4 * 2**20,
    )[0]
    if not direct:
        others = any_size(embed, ctx, spread, vsend, vkeep, wide, table, g_block, g_row, negs)
        return (grad_hidden, *others)

    packed = after(packed, pay_pair)
    zs = jnp.stack([packed, ment(packed, 4)])
    zs = jnp.concatenate([zs, ment(zs, 2)], axis=0)
    tile = (step, cols)
    v_keep, v_sent = call(
        fold_x_body, [sds((2, *tile), F32), sds((2, *tile), BF)], [vkeep, ment(vsend, 1)], moved=2**20
    )
    v_keep, v_send = call(
        fold_z_body, [sds(tile, F32), sds(tile, BF)], [v_keep, ment(v_sent, 2)], moved=2**19
    )
    v_got = ment(v_send, 4)
    gathered = jnp.concatenate([after(zs, v_keep), ment(zs, 1)], axis=0)
    gathered_other = ent(gathered, 1)
    spread = lax.all_to_all(after(spread, v_sent, zs), "ment", 0, 0)
    grad_table = call(
        functools.partial(table_body, negs.shape[0]),
        [sds((blocks, block_rows // parts, width), F32)],
        [ids, gathered, gathered_other, spread, table_rows],
        [pltpu.VMEM((parts * count, blocks * block_rows // parts), BF)],
        flops=5 * 10**8,
        moved=4 * 2**20,
    )[0]
    grad_qkv, grad_wo, grad_ln = call(
        small_body,
        [sds((3, *tile), F32), sds((cols, step), F32), sds((2, step), F32)],
        [ids, gathered, spread, v_keep, v_got],
        flops=10**8,
        moved=2**20,
    )
    return (grad_hidden, jnp.transpose(grad_qkv, (1, 0, 2)), grad_wo, grad_ln, grad_table)


def any_size(embed, ctx, spread, vsend, vkeep, wide, table, g_block, g_row, negs):
    ments = lax.axis_size("ment")
    count, width = embed.shape
    blocks, block_rows = table.shape[0], table.shape[1]
    few_rows = block_rows // ments
    step = width // spread.shape[0]
    sums = wide[count:].astype(F32)
    lse = lax.all_gather(sums[4, :count] + sums[5, :count] + sums[6, :count], "ment")
    blocks_of = lax.all_gather(g_block[0], "ment")
    rows_of = lax.all_gather(g_row[0], "ment")
    lists = lax.all_gather(negs, "ment")
    embeds = lax.all_gather(embed, "ment")
    at = lax.axis_index("ment") * few_rows
    rows = lax.dynamic_slice_in_dim(table, at, few_rows, 1)
    score = jnp.einsum("smd,brd->smbr", embeds, rows, preferred_element_type=F32)
    block = lax.axis_index("ent") * blocks + jnp.arange(blocks, dtype=jnp.int32)
    row = at + jnp.arange(few_rows, dtype=jnp.int32)
    hot = (blocks_of[:, :, None, None] == block[:, None]) & (rows_of[:, :, None, None] == row)
    hot = hot.astype(F32)
    listed = jnp.any(lists[:, :, None] == block, axis=1).astype(F32)
    times = (jnp.sum(hot, axis=1) + listed[:, :, None])[:, None]
    expo = jnp.where(times > 0, times * jnp.exp(score - lse[:, :, None, None]), 0.0)
    grad_table = jnp.einsum("smbr,smd->brd", (expo - hot).astype(BF), embeds, preferred_element_type=F32)
    resid = wide[:count].reshape(count, ments, -1)
    resid = lax.all_to_all(jnp.transpose(resid, (1, 0, 2)), "ment", 0, 0)
    ctxs = lax.all_gather(ctx, "ment")
    grad_wo = jnp.einsum("smc,smd->cd", ctxs, resid, preferred_element_type=F32)
    grad_ln = lax.psum_scatter(sums[0:2] + sums[2:4], "ment", scatter_dimension=1, tiled=True)
    keys = spread[:, :step].astype(F32).reshape(width, -1)
    d_query = spread[0, step : step + count]
    cls = jnp.transpose(spread[:, step + count : step + 2 * count, :step], (1, 0, 2)).reshape(count, width)
    values = jnp.stack([vkeep, vsend.astype(F32)], axis=1).reshape(width, -1)
    whole = jnp.stack([mm_tn(cls, d_query), keys, values], axis=1)
    grad_qkv = lax.psum_scatter(whole, "ment", scatter_dimension=0, tiled=True)
    return grad_qkv, grad_wo, grad_ln, grad_table


def solution(mesh):
    placed = (
        P("ment", None, None),
        P(None, None, "ent"),
        P("ent", None),
        P(),
        P(),
        P("ent", None, None),
        P("ment"),
        P("ment"),
        P("ment"),
        P("ment", None),
    )
    return jax.shard_map(
        on_device,
        mesh=mesh,
        in_specs=placed,
        out_specs=(
            P(("ment", "ent"), None, None),
            P("ment", None, "ent"),
            P("ent", "ment"),
            P(None, "ment"),
            P("ent", "ment", None),
        ),
        check_vma=False,
    )
```

time: 130 us -> 91.2 us (0.70)
  starting transfers between devices: 46.4 us -> 19 us
  waiting for transfers between devices: 49.6 us -> 26.2 us
  blocking collectives: 0 us -> 8.86 us
  Pallas kernels: 25.3 us -> 31.7 us
  local copies, waits for them, and re-layouts: 7.57 us -> 4.02 us
    ppermute x38 -> x12, starting transfers between devices: 46.4 us -> 14.4 us  [swap(): return lax.ppermute(x, axis, [(i, i ^ k) for i in range(size)])]
    ppermute x38 -> x12, waiting for transfers between devices: 49.6 us -> 26.2 us  [swap(): return lax.ppermute(x, axis, [(i, i ^ k) for i in range(size)])]
    all_gather x0 -> x1, blocking collectives: none -> 8.86 us  [on_device(): attns = lax.all_gather(attn, 'ent')]
    pallas_call x11, Pallas kernels: 25.3 us -> 31.7 us  [call(): pl.pallas_call(body, out_shape=outs, in_specs=[SMEM] * smem + [VMEM] * in...]
    all_to_all x0 -> x1, starting transfers between devices: none -> 4.67 us  [on_device(): spread = lax.all_to_all(after(spread, v_sent, zs), 'ment', 0, 0)]
    unnamed x35 -> x39, local copies, waits for them, and re-layouts: 7.56 us -> 3.94 us
  transfers between devices with their start and end apart: 38 -> 13, of which waited for: 13 -> 5; matrix products, arithmetic and copies ran while one was open for 0% -> 0% of each run, Pallas kernels for 11% -> 15%
where the time goes in v2:
time: 91.2 us; the launch traced here: 90.8 us
  Pallas kernels  31.7 us (35%)
  waiting for transfers between devices  26.2 us (29%)
  starting transfers between devices  19 us (21%)
  blocking collectives  8.86 us (10%)
  local copies, waits for them, and re-layouts  4.02 us (4%)
    pallas_call x11, Pallas kernels, call(): pl.pallas_call(body, out_shape=outs, in_specs=[SMEM] * smem + [VMEM] * in...  31.7 us
    ppermute x12, waiting for transfers between devices, swap(): return lax.ppermute(x, axis, [(i, i ^ k) for i in range(size)])  26.2 us
    ppermute x12, starting transfers between devices, swap(): return lax.ppermute(x, axis, [(i, i ^ k) for i in range(size)])  14.4 us
    all_gather x1, blocking collectives, on_device(): attns = lax.all_gather(attn, 'ent')  8.86 us
    all_to_all x1, starting transfers between devices, on_device(): spread = lax.all_to_all(after(spread, v_sent, zs), 'ment', 0, 0)  4.67 us
    unnamed x39, local copies, waits for them, and re-layouts  3.94 us
  transfers between devices with their start and end apart: 13, of which 5 were waited for; matrix products, arithmetic and copies ran while one was open for 0% of the time, Pallas kernels for 15%

profile of v2, /device:TPU:0, one launch (start us, length us, event | category | flops | bytes accessed | tf_op | source)
XLA Modules:
  0.0 90.8 jit_solution(14741133334611824187)
XLA Ops:
  0.7 11.3 %shard_map.137 = (bf16[64,1024]{1,0:T(8,128)(2,1)}, bf16[64,1024]{1,0:T(8,128)(2,1)}, bf16[64,256]{1,0:T(8,128)(2,1)}, f32[256,256]{1,0:T(8,128)}, bf16[256,1024...) custom-call(s32[64]{0:T(128)} %key_len.1, ...), custom_call_target="tpu_custom_call" | custom-call | flops 1000000000 | bytes 8388608 | tf_op jit(solution)/shard_map/pallas_call | solution.py:40
  12.0 8.9 %all-gather = bf16[256,1024]{1,0:T(8,128)(2,1)S(1)} all-gather(bf16[64,1024]{1,0:T(8,128)(2,1)} %get-tuple-element.39), channel_id=2, replica_groups=mesh['ment'=8,'ent'=4] {'ent'}, dimensions={0}, use_global_device_ids=true | all-gather | bytes 655360 | tf_op jit(solution)/shard_map/all_gather | solution.py:503
  20.9 0.1 pad_add_fusion.ids
  21.0 2.2 %copy-done.2 = bf16[8,256,1024]{2,1,0:T(8,128)(2,1)S(1)} copy-done((bf16[8,256,1024]{2,1,0:T(8,128)(2,1)S(1)}, bf16[8,256,1024]{2,1,0:T(8,128)(2,1)}, u32[]{:S(2)}) %copy-start.2) | copy-done | bytes 4194328
  23.2 0.9 copy-done.5
  24.1 0.8 copy-done.13
  24.9 3.5 %shard_map.138 = (bf16[64,1024]{1,0:T(8,128)(2,1)}, f32[64,1024]{1,0:T(8,128)S(1)}, f32[64,128]{1,0:T(8,128)S(1)}, bf16[64,2176]{1,0:T(8,128)(2,1)S(1)}, bf16[64...) custom-call(s32[2]{0:T(128)S(1)} %pad_add_fusion.ids, s32[4]{0:T(128)S(1)} %bitcast.28, ...), custom_call_target="tpu_custom_call" | custom-call | flops 600000000 | bytes 6291456 | tf_op jit(solution)/shard_map/pallas_call | solution.py:40
  28.3 0.3 collective-permute-start
  28.7 1.2 %collective-permute-done.q = bf16[64,2176]{1,0:T(8,128)(2,1)S(1)} collective-permute-done((bf16[64,2176]{1,0:T(8,128)(2,1)S(1)}, bf16[64,2176]{1,0:T(8,128)(2,1)S(1)}, u32[]{:S(2)}, u32[]{:S(2)}) %collective-permute-start) | collective-permute-done | bytes 278560 | tf_op jit(solution)/shard_map/ppermute | solution.py:442
  29.9 0.2 shard_map.139.p0
  30.1 1.2 %collective-permute-start.1 = (bf16[64,2176]{1,0:T(8,128)(2,1)S(1)}, bf16[64,2176]{1,0:T(8,128)(2,1)S(1)}, u32[]{:S(2)}, u32[]{:S(2)}) collective-permute-start(bf16[64,2176]{1,0:T(8,128)(2,1)S(1)} %shard_map.139.p0), channel_id=1, source_target_pairs={{0,2},{1,3},{2,0},{3,1},{4,6},{5,7},{6,4},{7,5},{8,10},{9,11},{10,... | collective-permute-start | bytes 835592 | tf_op jit(solution)/shard_map/ppermute | solution.py:442
  31.3 2.6 %collective-permute-start.5 = (bf16[64,768]{1,0:T(8,128)(2,1)S(1)}, bf16[64,768]{1,0:T(8,128)(2,1)S(1)}, u32[]{:S(2)}, u32[]{:S(2)}) collective-permute-start(bf16[64,768]{1,0:T(8,128)(2,1)S(1)} %get-tuple-element.54), channel_id=1, source_target_pairs={{0,16},{4,20},{8,24},{12,28},{16,0},{20,4},{24,8},{28,12},{1,17},{... | collective-permute-start | bytes 294920 | tf_op jit(solution)/shard_map/ppermute | solution.py:442
  33.9 5.2 %collective-permute-done.5 = bf16[64,768]{1,0:T(8,128)(2,1)S(1)} collective-permute-done((bf16[64,768]{1,0:T(8,128)(2,1)S(1)}, bf16[64,768]{1,0:T(8,128)(2,1)S(1)}, u32[]{:S(2)}, u32[]{:S(2)}) %collective-permute-start.5) | collective-permute-done | bytes 98336 | tf_op jit(solution)/shard_map/ppermute | solution.py:442
  39.1 0.7 collective-permute-start.6
  39.8 1.8 %shard_map.140 = (bf16[256,1024]{1,0:T(8,128)(2,1)S(1)}, f32[16,1024]{1,0:T(8,128)S(1)}, bf16[4,128,256]{2,1,0:T(8,128)(2,1)S(1)}, f32[4,128,256]{2,1,0:T(8,128)S(1)}, bf16[80,1024]{1,0:T(8,128)(2,1)S(1)}) custom-call(s32[2]{0:T(128)S(1)} %pad_add_fusion.ids, s32[4]{0:T(128)S(1)} %bitcast.29, bf16[64,2176]{1,0:T(8,128)(2,1)S(1)} %shard_map.139.p0, ...), custom_call_target="tpu_custom_call" | custom-call | flops 300000000 | bytes 6291456 | tf_op jit(solution)/shard_map/pallas_call | solution.py:40
  41.6 1.6 %collective-permute-start.7 = (bf16[4,128,256]{2,1,0:T(8,128)(2,1)S(1)}, bf16[4,128,256]{2,1,0:T(8,128)(2,1)S(1)}, u32[]{:S(2)}, u32[]{:S(2)}) collective-permute-start(bf16[4,128,256]{2,1,0:T(8,128)(2,1)S(1)} %get-tuple-element.56), channel_id=1, source_target_pairs={{0,4},{4,0},{8,12},{12,8},{16,20},{20,16},{24,28},{28,24},{1,5},{5... | collective-permute-start | bytes 786440 | tf_op jit(solution)/shard_map/ppermute | solution.py:442
  43.2 7.1 %shard_map.141 = (bf16[2,80,2176]{2,1,0:T(8,128)(2,1)}, bf16[80,2176]{1,0:T(8,128)(2,1)}, bf16[80,2176]{1,0:T(8,128)(2,1)S(1)}, bf16[256,1024]{1,0:T(8,128)(2,1)S(1)}, bf16[64,256]{1,0:T(8,128)(2,1)S(1)}) custom-call(s32[2]{0:T(128)S(1)} %pad_add_fusion.ids, bf16[2048,1024]{1,0:T(8,128)(2,1)S(1)} %bitcast.18, bf16[3,1024,256]{2,1,0:T(8,128)(2,1)S(1)} %bitcast.21, ...), custom_call_target="tpu_custom_call" | custom-call | flops 1000000000 | bytes 8388608 | tf_op jit(solution)/shard_map/pallas_call | solution.py:40
  50.3 1.4 %shard_map.145 = bf16[8,272,256]{2,1,0:T(8,128)(2,1)} custom-call(bf16[256,1024]{1,0:T(8,128)(2,1)S(1)} %get-tuple-element.61.tbuf, bf16[256,256]{1,0:T(8,128)(2,1)S(1)} %copy-done.11, bf16[64,256]{1,0:T(8,128)(2,1)S(1)} %get-tuple-element.63.d_query, bf16[64,1024]{1,0:T(8,128)(2,1)S(1)} %copy-done.6, bf16[80,1024]{1,0:T(8,128)(2,1)S(1)} %get-tuple-element.64.wide), custom_call_target="tpu_custom_call" | custom-call | flops 100000000 | bytes 3145728 | tf_op jit(solution)/shard_map/pallas_call | solution.py:40
  51.8 4.7 %all-to-all-start = ((bf16[8,272,256]{2,1,0:T(8,128)(2,1)}), bf16[8,272,256]{2,1,0:T(8,128)(2,1)S(1)}, u32[]{:S(2)}, u32[]{:S(2)}) async-start(bf16[8,272,256]{2,1,0:T(8,128)(2,1)} %shard_map.145), calls=%async_computation | async-start | bytes 2228224 | tf_op jit(solution)/shard_map/all_to_all | solution.py:583
  56.4 0.9 %collective-permute-start.3 = (bf16[2,80,2176]{2,1,0:T(8,128)(2,1)}, bf16[2,80,2176]{2,1,0:T(8,128)(2,1)S(1)}, u32[]{:S(2)}, u32[]{:S(2)}) collective-permute-start(bf16[2,80,2176]{2,1,0:T(8,128)(2,1)} %get-tuple-element.51), channel_id=1, source_target_pairs={{0,2},{1,3},{2,0},{3,1},{4,6},{5,7},{6,4},{7,5},{8,10},{9,11},{10,... | collective-permute-start | bytes 2088968 | tf_op jit(solution)/shard_map/ppermute | solution.py:442
  57.4 2.0 %collective-permute-start.9 = (bf16[4,64,768]{2,1,0:T(8,128)(2,1)S(1)}, bf16[4,64,768]{2,1,0:T(8,128)(2,1)S(1)}, u32[]{:S(2)}, u32[]{:S(2)}) collective-permute-start(bf16[4,64,768]{2,1,0:T(8,128)(2,1)S(1)} %pad_maximum_fusion), channel_id=1, source_target_pairs={{0,4},{4,0},{8,12},{12,8},{16,20},{20,16},{24,28},{28,24},{1,5},{5... | collective-permute-start | bytes 1179656 | tf_op jit(solution)/shard_map/ppermute | solution.py:442
  59.4 1.5 %collective-permute-start.8 = (bf16[2,128,256]{2,1,0:T(8,128)(2,1)S(1)}, bf16[2,128,256]{2,1,0:T(8,128)(2,1)S(1)}, u32[]{:S(2)}, u32[]{:S(2)}) collective-permute-start(bf16[2,128,256]{2,1,0:T(8,128)(2,1)S(1)} %get-tuple-element.58), channel_id=1, source_target_pairs={{0,8},{4,12},{8,0},{12,4},{16,24},{20,28},{24,16},{28,20},{1,9},{5... | collective-permute-start | bytes 393224 | tf_op jit(solution)/shard_map/ppermute | solution.py:442
  60.9 16.1 %collective-permute-done.8.got = bf16[2,128,256]{2,1,0:T(8,128)(2,1)S(1)} collective-permute-done((bf16[2,128,256]{2,1,0:T(8,128)(2,1)S(1)}, bf16[2,128,256]{2,1,0:T(8,128)(2,1)S(1)}, u32[]{:S(2)}, u32[]{:S(2)}) %collective-permute-start.8) | collective-permute-done | bytes 131104 | tf_op jit(solution)/shard_map/ppermute | solution.py:442
  77.0 1.8 %collective-permute-done.9 = bf16[4,64,768]{2,1,0:T(8,128)(2,1)S(1)} collective-permute-done((bf16[4,64,768]{2,1,0:T(8,128)(2,1)S(1)}, bf16[4,64,768]{2,1,0:T(8,128)(2,1)S(1)}, u32[]{:S(2)}, u32[]{:S(2)}) %collective-permute-start.9) | collective-permute-done | bytes 393248 | tf_op jit(solution)/shard_map/ppermute | solution.py:442
  78.8 0.1 collective-permute-start.11
  78.9 0.1 slice_bitcast_fusion
  79.0 0.5 collective-permute-start.4
  79.5 2.9 %collective-permute-start.10 = (bf16[128,256]{1,0:T(8,128)(2,1)S(1)}, bf16[128,256]{1,0:T(8,128)(2,1)S(1)}, u32[]{:S(2)}, u32[]{:S(2)}) collective-permute-start(bf16[128,256]{1,0:T(8,128)(2,1)S(1)} %get-tuple-element.66), channel_id=1, source_target_pairs={{0,16},{4,20},{8,24},{12,28},{16,0},{20,4},{24,8},{28,12},{1,17},{... | collective-permute-start | bytes 196616 | tf_op jit(solution)/shard_map/ppermute | solution.py:442
  82.4 1.8 %shard_map.142 = bf16[16,32,1024]{2,1,0:T(8,128)(2,1)} custom-call(bf16[80,2176]{1,0:T(8,128)(2,1)S(1)} %copy-done.9, bf16[80,2176]{1,0:T(8,128)(2,1)S(1)} %collective-permute-done.2.p1, bf16[80,2176]{1,0:T(8,128)(2,1)S(1)} %get-tuple-element.72.p2, bf16[80,2176]{1,0:T(8,128)(2,1)S(1)} %collective-permute-done.4.p3, f32[16,1024]{1,0:T(8,128)S(1)} %get-tuple-element.52.own_resid), custom_call_target="tpu_custom_call" | custom-call | flops 300000000 | bytes 4194304 | tf_op jit(solution)/shard_map/pallas_call | solution.py:40
  84.3 2.0 %collective-permute-done.10.v1 = bf16[128,256]{1,0:T(8,128)(2,1)S(1)} collective-permute-done((bf16[128,256]{1,0:T(8,128)(2,1)S(1)}, bf16[128,256]{1,0:T(8,128)(2,1)S(1)}, u32[]{:S(2)}, u32[]{:S(2)}) %collective-permute-start.10) | collective-permute-done | bytes 65568 | tf_op jit(solution)/shard_map/ppermute | solution.py:442
  86.2 1.6 %shard_map.146 = (f32[3,128,256]{2,1,0:T(8,128)}, f32[256,128]{1,0:T(8,128)}, f32[2,128]{1,0:T(2,128)}) custom-call(s32[2]{0:T(128)S(1)} %pad_add_fusion.ids, bf16[8,64,768]{2,1,0:T(8,128)(2,1)S(1)} %constant_dynamic-update-slice_fusion.gathered.mine_all, bf16[8,272,256]{2,1,0:T(8,128)(2,1)S(1)} %all-to-all-done.spread, ...), custom_call_target="tpu_custom_call" | custom-call | flops 100000000 | bytes 1048576 | tf_op jit(solution)/shard_map/pallas_call | solution.py:40
  87.8 3.0 %shard_map.147 = f32[8,32,1024]{2,1,0:T(8,128)} custom-call(s32[2]{0:T(128)S(1)} %pad_add_fusion.ids, bf16[8,64,768]{2,1,0:T(8,128)(2,1)S(1)} %constant_dynamic-update-slice_fusion.gathered.mine_all, bf16[8,64,768]{2,1,0:T(8,128)(2,1)S(1)} %collective-permute-done.11.other_all, bf16[8,272,256]{2,1,0:T(8,128)(2,1)S(1)} %all-to-all-done.spread, ...), custom_call_target="tpu_custom_call" | custom-call | flops 500000000 | bytes 4194304 | tf_op jit(solution)/shard_map/pallas_call | solution.py:40
  (50 shorter events, 0.3 us)
Async XLA Ops:
  0.6 20.3 %copy-start.14 = (f32[1024]{0:T(1024)S(1)}, f32[1024]{0:T(1024)}, u32[]{:S(2)}) copy-start(f32[1024]{0:T(1024)} %param.13) | copy-start | bytes 12292
  0.6 20.3 %copy-start.15 = (f32[1024]{0:T(1024)S(1)}, f32[1024]{0:T(1024)}, u32[]{:S(2)}) copy-start(f32[1024]{0:T(1024)} %param.14) | copy-start | bytes 12292
  0.7 20.3 %copy-start.16 = (s32[1,4]{1,0:T(1,128)S(1)}, s32[1,4]{1,0:T(1,128)}, u32[]{:S(2)}) copy-start(s32[1,4]{1,0:T(1,128)} %param.19) | copy-start | bytes 52
  0.7 20.3 %copy-start.17 = (s32[64]{0:T(128)S(1)}, s32[64]{0:T(128)}, u32[]{:S(2)}) copy-start(s32[64]{0:T(128)} %param.17) | copy-start | bytes 772
  0.7 20.3 %copy-start.18 = (s32[64]{0:T(128)S(1)}, s32[64]{0:T(128)}, u32[]{:S(2)}) copy-start(s32[64]{0:T(128)} %param.18) | copy-start | bytes 772
  21.0 2.2 %copy-start.2 = (bf16[8,256,1024]{2,1,0:T(8,128)(2,1)S(1)}, bf16[8,256,1024]{2,1,0:T(8,128)(2,1)}, u32[]{:S(2)}) copy-start(bf16[8,256,1024]{2,1,0:T(8,128)(2,1)} %table.1) | copy-start | bytes 12582916
  23.2 0.9 copy-start.5
  24.1 0.8 copy-start.13
  24.8 15.0 %copy-start.1 = (bf16[1024,3,256]{2,0,1:T(8,128)(2,1)S(1)}, bf16[1024,3,256]{2,0,1:T(8,128)(2,1)}, u32[]{:S(2)}) copy-start(bf16[1024,3,256]{2,0,1:T(8,128)(2,1)} %param.11) | copy-start | bytes 4718596
  24.9 15.0 %copy-start.7 = (bf16[256,1024]{1,0:T(8,128)(2,1)S(1)}, bf16[256,1024]{1,0:T(8,128)(2,1)}, u32[]{:S(2)}) copy-start(bf16[256,1024]{1,0:T(8,128)(2,1)} %get-tuple-element.45.mix) | copy-start | bytes 1572868
  24.9 18.3 %copy-start.4 = (bf16[256,1024]{1,0:T(8,128)(2,1)S(1)}, bf16[256,1024]{1,0:T(8,128)(2,1)}, u32[]{:S(2)}) copy-start(bf16[256,1024]{1,0:T(8,128)(2,1)} %get-tuple-element.47.qk) | copy-start | bytes 1572868
  24.9 18.3 %copy-start.10 = (f32[256,256]{1,0:T(8,128)S(1)}, f32[256,256]{1,0:T(8,128)}, u32[]{:S(2)}) copy-start(f32[256,256]{1,0:T(8,128)} %get-tuple-element.38.probs_ref) | copy-start | bytes 786436
  24.9 18.3 %copy-start.12 = (bf16[256,128]{1,0:T(8,128)(2,1)S(1)}, bf16[256,128]{1,0:T(8,128)(2,1)}, u32[]{:S(2)}) copy-start(bf16[256,128]{1,0:T(8,128)(2,1)} %get-tuple-element.48.folded) | copy-start | bytes 196612
  28.3 11.5 %copy-start.3 = (bf16[256,1024]{1,0:T(8,128)(2,1)S(1)}, bf16[256,1024]{1,0:T(8,128)(2,1)}, u32[]{:S(2)}) copy-start(bf16[256,1024]{1,0:T(8,128)(2,1)} %wo_ref.1) | copy-start | bytes 1572868
  28.3 1.6 %collective-permute-start = (bf16[64,2176]{1,0:T(8,128)(2,1)S(1)}, bf16[64,2176]{1,0:T(8,128)(2,1)S(1)}, u32[]{:S(2)}, u32[]{:S(2)}) collective-permute-start(bf16[64,2176]{1,0:T(8,128)(2,1)S(1)} %get-tuple-element.42.p), channel_id=1, source_target_pairs={{0,1},{1,0},{2,3},{3,2},{4,5},{5,4},{6,7},{7,6},{8,9},{9,8},{10,11... | collective-permute-start | bytes 835592 | tf_op jit(solution)/shard_map/ppermute | solution.py:442
  29.9 13.3 %copy-start = (bf16[64,32,1024]{2,1,0:T(8,128)(2,1)S(1)}, bf16[64,32,1024]{2,1,0:T(8,128)(2,1)}, u32[]{:S(2)}) copy-start(bf16[64,32,1024]{2,1,0:T(8,128)(2,1)} %param.10) | copy-start | bytes 12582916
  30.1 9.7 %collective-permute-start.1 = (bf16[64,2176]{1,0:T(8,128)(2,1)S(1)}, bf16[64,2176]{1,0:T(8,128)(2,1)S(1)}, u32[]{:S(2)}, u32[]{:S(2)}) collective-permute-start(bf16[64,2176]{1,0:T(8,128)(2,1)S(1)} %shard_map.139.p0), channel_id=1, source_target_pairs={{0,2},{1,3},{2,0},{3,1},{4,6},{5,7},{6,4},{7,5},{8,10},{9,11},{10,... | collective-permute-start | bytes 835592 | tf_op jit(solution)/shard_map/ppermute | solution.py:442
  31.3 7.8 %collective-permute-start.5 = (bf16[64,768]{1,0:T(8,128)(2,1)S(1)}, bf16[64,768]{1,0:T(8,128)(2,1)S(1)}, u32[]{:S(2)}, u32[]{:S(2)}) collective-permute-start(bf16[64,768]{1,0:T(8,128)(2,1)S(1)} %get-tuple-element.54), channel_id=1, source_target_pairs={{0,16},{4,20},{8,24},{12,28},{16,0},{20,4},{24,8},{28,12},{1,17},{... | collective-permute-start | bytes 294920 | tf_op jit(solution)/shard_map/ppermute | solution.py:442
  39.1 12.6 %collective-permute-start.6 = (bf16[2,64,768]{2,1,0:T(8,128)(2,1)S(1)}, bf16[2,64,768]{2,1,0:T(8,128)(2,1)S(1)}, u32[]{:S(2)}, u32[]{:S(2)}) collective-permute-start(bf16[2,64,768]{2,1,0:T(8,128)(2,1)S(1)} %pad_maximum_fusion.1), channel_id=1, source_target_pairs={{0,8},{4,12},{8,0},{12,4},{16,24},{20,28},{24,16},{28,20},{1,9},{5... | collective-permute-start | bytes 589832 | tf_op jit(solution)/shard_map/ppermute | solution.py:442
  41.6 10.1 %collective-permute-start.7 = (bf16[4,128,256]{2,1,0:T(8,128)(2,1)S(1)}, bf16[4,128,256]{2,1,0:T(8,128)(2,1)S(1)}, u32[]{:S(2)}, u32[]{:S(2)}) collective-permute-start(bf16[4,128,256]{2,1,0:T(8,128)(2,1)S(1)} %get-tuple-element.56), channel_id=1, source_target_pairs={{0,4},{4,0},{8,12},{12,8},{16,20},{20,16},{24,28},{28,24},{1,5},{5... | collective-permute-start | bytes 786440 | tf_op jit(solution)/shard_map/ppermute | solution.py:442
  43.2 7.1 %copy-start.6 = (bf16[64,1024]{1,0:T(8,128)(2,1)S(1)}, bf16[64,1024]{1,0:T(8,128)(2,1)}, u32[]{:S(2)}) copy-start(bf16[64,1024]{1,0:T(8,128)(2,1)} %get-tuple-element.40.cls) | copy-start | bytes 393220
  43.2 7.1 %copy-start.11 = (bf16[256,256]{1,0:T(8,128)(2,1)S(1)}, bf16[256,256]{1,0:T(8,128)(2,1)}, u32[]{:S(2)}) copy-start(bf16[256,256]{1,0:T(8,128)(2,1)} %get-tuple-element.62.qx) | copy-start | bytes 393220
  50.3 1.5 %copy-start.8 = (bf16[80,2176]{1,0:T(8,128)(2,1)}, bf16[80,2176]{1,0:T(8,128)(2,1)S(1)}, u32[]{:S(2)}) copy-start(bf16[80,2176]{1,0:T(8,128)(2,1)S(1)} %get-tuple-element.49.p0) | copy-start | bytes 1044484
  51.8 34.4 %all-to-all-start = ((bf16[8,272,256]{2,1,0:T(8,128)(2,1)}), bf16[8,272,256]{2,1,0:T(8,128)(2,1)S(1)}, u32[]{:S(2)}, u32[]{:S(2)}) async-start(bf16[8,272,256]{2,1,0:T(8,128)(2,1)} %shard_map.145), calls=%async_computation | async-start | bytes 2228224 | tf_op jit(solution)/shard_map/all_to_all | solution.py:583
  56.4 22.5 %collective-permute-start.3 = (bf16[2,80,2176]{2,1,0:T(8,128)(2,1)}, bf16[2,80,2176]{2,1,0:T(8,128)(2,1)S(1)}, u32[]{:S(2)}, u32[]{:S(2)}) collective-permute-start(bf16[2,80,2176]{2,1,0:T(8,128)(2,1)} %get-tuple-element.51), channel_id=1, source_target_pairs={{0,2},{1,3},{2,0},{3,1},{4,6},{5,7},{6,4},{7,5},{8,10},{9,11},{10,... | collective-permute-start | bytes 2088968 | tf_op jit(solution)/shard_map/ppermute | solution.py:442
  57.4 21.4 %collective-permute-start.9 = (bf16[4,64,768]{2,1,0:T(8,128)(2,1)S(1)}, bf16[4,64,768]{2,1,0:T(8,128)(2,1)S(1)}, u32[]{:S(2)}, u32[]{:S(2)}) collective-permute-start(bf16[4,64,768]{2,1,0:T(8,128)(2,1)S(1)} %pad_maximum_fusion), channel_id=1, source_target_pairs={{0,4},{4,0},{8,12},{12,8},{16,20},{20,16},{24,28},{28,24},{1,5},{5... | collective-permute-start | bytes 1179656 | tf_op jit(solution)/shard_map/ppermute | solution.py:442
  59.4 17.5 %collective-permute-start.8 = (bf16[2,128,256]{2,1,0:T(8,128)(2,1)S(1)}, bf16[2,128,256]{2,1,0:T(8,128)(2,1)S(1)}, u32[]{:S(2)}, u32[]{:S(2)}) collective-permute-start(bf16[2,128,256]{2,1,0:T(8,128)(2,1)S(1)} %get-tuple-element.58), channel_id=1, source_target_pairs={{0,8},{4,12},{8,0},{12,4},{16,24},{20,28},{24,16},{28,20},{1,9},{5... | collective-permute-start | bytes 393224 | tf_op jit(solution)/shard_map/ppermute | solution.py:442
  60.9 21.6 %collective-permute-start.2 = (bf16[80,2176]{1,0:T(8,128)(2,1)}, bf16[80,2176]{1,0:T(8,128)(2,1)S(1)}, u32[]{:S(2)}, u32[]{:S(2)}) collective-permute-start(bf16[80,2176]{1,0:T(8,128)(2,1)} %get-tuple-element.50), channel_id=1, source_target_pairs={{0,1},{1,0},{2,3},{3,2},{4,5},{5,4},{6,7},{7,6},{8,9},{9,8},{10,11... | collective-permute-start | bytes 1044488 | tf_op jit(solution)/shard_map/ppermute | solution.py:442
  77.0 5.5 %copy-start.9 = (bf16[80,2176]{1,0:T(8,128)(2,1)S(1)}, bf16[80,2176]{1,0:T(8,128)(2,1)}, u32[]{:S(2)}) copy-start(bf16[80,2176]{1,0:T(8,128)(2,1)} %copy-done.8) | copy-start | bytes 1044484
  78.8 9.0 %collective-permute-start.11 = (bf16[8,64,768]{2,1,0:T(8,128)(2,1)S(1)}, bf16[8,64,768]{2,1,0:T(8,128)(2,1)S(1)}, u32[]{:S(2)}, u32[]{:S(2)}) collective-permute-start(bf16[8,64,768]{2,1,0:T(8,128)(2,1)S(1)} %constant_dynamic-update-slice_fusion.gathered.mine_all), channel_id=1, source_target_pairs={{0,1},{1,0},{2,3},{3,2},{4,5},{5,4},{6,7},{7,6},{8,9},{9,8},{10,11... | collective-permute-start | bytes 2359304 | tf_op jit(solution)/shard_map/ppermute | solution.py:442
  79.0 3.5 %collective-permute-start.4 = (bf16[80,2176]{1,0:T(8,128)(2,1)S(1)}, bf16[80,2176]{1,0:T(8,128)(2,1)S(1)}, u32[]{:S(2)}, u32[]{:S(2)}) collective-permute-start(bf16[80,2176]{1,0:T(8,128)(2,1)S(1)} %get-tuple-element.71), channel_id=1, source_target_pairs={{0,1},{1,0},{2,3},{3,2},{4,5},{5,4},{6,7},{7,6},{8,9},{9,8},{10,11... | collective-permute-start | bytes 1044488 | tf_op jit(solution)/shard_map/ppermute | solution.py:442
  79.5 6.7 %collective-permute-start.10 = (bf16[128,256]{1,0:T(8,128)(2,1)S(1)}, bf16[128,256]{1,0:T(8,128)(2,1)S(1)}, u32[]{:S(2)}, u32[]{:S(2)}) collective-permute-start(bf16[128,256]{1,0:T(8,128)(2,1)S(1)} %get-tuple-element.66), channel_id=1, source_target_pairs={{0,16},{4,20},{8,24},{12,28},{16,0},{20,4},{24,8},{28,12},{1,17},{... | collective-permute-start | bytes 196616 | tf_op jit(solution)/shard_map/ppermute | solution.py:442

commit v3 on v2

--- a/solution.py
+++ b/solution.py
@@ -105,24 +105,28 @@
     qx_out[...] = qx
     part[groups + 1].wait()
     qk_out[...] = mm_nt(qx, w_ref[1]).astype(BF)
-    fold = fold_matrix(span, seq, 0)
+    score = []
+    live = []
     col = lax.broadcasted_iota(jnp.int32, (1, span), 1)
     diag = diagonal(rows, span, seq)
     for g in range(groups):
-        x = hid[g * span : (g + 1) * span, :]
         here = slice(g * rows, (g + 1) * rows)
+        score.append(mm_nt(qk_out[here, :], hid[g * span : (g + 1) * span, :]))
         limit = jnp.zeros((1, span), jnp.int32)
         for m in range(GROUP):
             limit = jnp.where(col // seq == m, key_len[g * GROUP + m], limit)
-        live = jnp.logical_and(diag, col % seq < limit)
-        score = jnp.where(live, mm_nt(qk_out[here, :], x) * HD ** (-0.5), LOW)
-        expo = jnp.exp(score - jnp.max(score, axis=1, keepdims=True))
-        expo = jnp.where(live, expo, 0.0)
-        probs = expo / jnp.sum(expo, axis=1, keepdims=True)
-        probs_out[here, :] = probs
-        half = probs.astype(BF)
-        fold_out[here, :] = mm(half, fold).astype(BF)
-        mix_out[here, :] = mm(half, x).astype(BF)
+        live.append(jnp.logical_and(diag, col % seq < limit).astype(F32))
+    live = jnp.concatenate(live, axis=0) > 0
+    score = jnp.where(live, jnp.concatenate(score, axis=0) * HD ** (-0.5), LOW)
+    expo = jnp.exp(score - jnp.max(score, axis=1, keepdims=True))
+    expo = jnp.where(live, expo, 0.0)
+    probs = expo / jnp.sum(expo, axis=1, keepdims=True)
+    probs_out[...] = probs
+    half = probs.astype(BF)
+    for g in range(groups):
+        here = slice(g * rows, (g + 1) * rows)
+        mix_out[here, :] = mm(half[here, :], hid[g * span : (g + 1) * span, :]).astype(BF)
+    fold_out[...] = mm(half, fold_matrix(span, seq, 0)).astype(BF)
     part[groups + 2].wait()
     ctx = pick_heads(mm(mix_out[...], w_ref[2]), heads).astype(BF)
     ctx_out[...] = ctx
@@ -307,16 +311,16 @@
     seq = tokens // count
     span = GROUP * seq
     rows = GROUP * heads
-    fold = fold_matrix(span, seq, seq)
-    for g in range(count // GROUP):
-        x = hid[g * span : (g + 1) * span, :]
+    xs = [hid[g * span : (g + 1) * span, :] for g in range(count // GROUP)]
+    d_probs = [mm_nt(dv[g * rows : (g + 1) * rows, :], x) for g, x in enumerate(xs)]
+    d_probs = jnp.concatenate(d_probs, axis=0)
+    probs = probs_ref[...]
+    d_scores = probs * (d_probs - jnp.sum(probs * d_probs, axis=1, keepdims=True))
+    half = (d_scores * HD ** (-0.5)).astype(BF)
+    for g, x in enumerate(xs):
         here = slice(g * rows, (g + 1) * rows)
-        probs = probs_ref[here, :]
-        d_probs = mm_nt(dv[here, :], x)
-        d_scores = probs * (d_probs - jnp.sum(probs * d_probs, axis=1, keepdims=True))
-        half = (d_scores * HD ** (-0.5)).astype(BF)
-        buf[here, :] = (folded[here, :].astype(F32) + mm(half, fold)).astype(BF)
-        tbuf[here, :] = mm(half, x).astype(BF)
+        tbuf[here, :] = mm(half[here, :], x).astype(BF)
+    buf[...] = (folded[...].astype(F32) + mm(half, fold_matrix(span, seq, seq))).astype(BF)
     d_query = pick_heads(mm(tbuf[...], w_ref[1]), heads).astype(BF)
     d_query_out[...] = d_query
     zbuf[...] = mm_nt(d_query, w_ref[0]).astype(BF)
@@ -497,7 +501,7 @@
         ],
         flops=10**9,
         moved=8 * 2**20,
-        limit=60,
+        limit=52,
         outside=3,
     )
     attns = lax.all_gather(attn, "ent")

time: 91.2 us -> 81.2 us (0.89)
  Pallas kernels: 31.7 us -> 24 us
  local copies, waits for them, and re-layouts: 4.02 us -> 1.53 us
  starting transfers between devices: 19 us -> 20.1 us
    pallas_call x11, Pallas kernels: 31.7 us -> 24 us  [call(): pl.pallas_call(body, out_shape=outs, in_specs=[SMEM] * smem + [VMEM] * in...]
    unnamed x39 -> x25, local copies, waits for them, and re-layouts: 3.94 us -> 1.45 us
    all_to_all x1, starting transfers between devices: 4.67 us -> 5.59 us  [on_device(): spread = lax.all_to_all(after(spread, v_sent, zs), 'ment', 0, 0)]
  transfers between devices with their start and end apart: 13 -> 13, of which waited for: 5 -> 6; matrix products, arithmetic and copies ran while one was open for 0% -> 0% of each run, Pallas kernels for 15% -> 13%
where the time goes in v3:
time: 81.2 us; the launch traced here: 81 us
  waiting for transfers between devices  25.8 us (32%)
  Pallas kernels  24 us (30%)
  starting transfers between devices  20.1 us (25%)
  blocking collectives  8.65 us (11%)
  local copies, waits for them, and re-layouts  1.53 us (2%)
    ppermute x12, waiting for transfers between devices, swap(): return lax.ppermute(x, axis, [(i, i ^ k) for i in range(size)])  25.8 us
    pallas_call x11, Pallas kernels, call(): pl.pallas_call(body, out_shape=outs, in_specs=[SMEM] * smem + [VMEM] * in...  24 us
    ppermute x12, starting transfers between devices, swap(): return lax.ppermute(x, axis, [(i, i ^ k) for i in range(size)])  14.5 us
    all_gather x1, blocking collectives, on_device(): attns = lax.all_gather(attn, 'ent')  8.65 us
    all_to_all x1, starting transfers between devices, on_device(): spread = lax.all_to_all(after(spread, v_sent, zs), 'ment', 0, 0)  5.59 us
  transfers between devices with their start and end apart: 13, of which 6 were waited for; matrix products, arithmetic and copies ran while one was open for 0% of the time, Pallas kernels for 13%

profile of v3, /device:TPU:0, one launch (start us, length us, event | category | flops | bytes accessed | tf_op | source)
XLA Modules:
  0.0 81.0 jit_solution(4740029904230032805)
XLA Ops:
  0.6 0.6 copy-done.11
  1.3 6.6 %shard_map.137 = (bf16[64,1024]{1,0:T(8,128)(2,1)S(1)}, bf16[64,1024]{1,0:T(8,128)(2,1)S(1)}, bf16[64,256]{1,0:T(8,128)(2,1)S(1)}, f32[256,256]{1,0:T(8,128)S(1)...) custom-call(s32[64]{0:T(128)S(1)} %copy-done.11, ...), custom_call_target="tpu_custom_call" | custom-call | flops 1000000000 | bytes 8388608 | tf_op jit(solution)/shard_map/pallas_call | solution.py:40
  7.9 8.6 %all-gather = bf16[256,1024]{1,0:T(8,128)(2,1)S(1)} all-gather(bf16[64,1024]{1,0:T(8,128)(2,1)S(1)} %get-tuple-element.39), channel_id=2, replica_groups=mesh['ment'=8,'ent'=4] {'ent'}, dimensions={0}, use_global_device_ids=true | all-gather | bytes 655360 | tf_op jit(solution)/shard_map/all_gather | solution.py:507
  16.5 0.1 pad_add_fusion.ids
  16.7 3.5 %shard_map.138 = (bf16[64,1024]{1,0:T(8,128)(2,1)}, f32[64,1024]{1,0:T(8,128)S(1)}, f32[64,128]{1,0:T(8,128)S(1)}, bf16[64,2176]{1,0:T(8,128)(2,1)S(1)}, bf16[64...) custom-call(s32[2]{0:T(128)S(1)} %pad_add_fusion.ids, s32[4]{0:T(128)S(1)} %bitcast.28, ...), custom_call_target="tpu_custom_call" | custom-call | flops 600000000 | bytes 6291456 | tf_op jit(solution)/shard_map/pallas_call | solution.py:40
  20.1 0.4 collective-permute-start
  20.5 1.2 %collective-permute-done.q = bf16[64,2176]{1,0:T(8,128)(2,1)S(1)} collective-permute-done((bf16[64,2176]{1,0:T(8,128)(2,1)S(1)}, bf16[64,2176]{1,0:T(8,128)(2,1)S(1)}, u32[]{:S(2)}, u32[]{:S(2)}) %collective-permute-start) | collective-permute-done | bytes 278560 | tf_op jit(solution)/shard_map/ppermute | solution.py:446
  21.7 0.2 shard_map.139.p0
  21.9 1.2 %collective-permute-start.1 = (bf16[64,2176]{1,0:T(8,128)(2,1)S(1)}, bf16[64,2176]{1,0:T(8,128)(2,1)S(1)}, u32[]{:S(2)}, u32[]{:S(2)}) collective-permute-start(bf16[64,2176]{1,0:T(8,128)(2,1)S(1)} %shard_map.139.p0), channel_id=1, source_target_pairs={{0,2},{1,3},{2,0},{3,1},{4,6},{5,7},{6,4},{7,5},{8,10},{9,11},{10,... | collective-permute-start | bytes 835592 | tf_op jit(solution)/shard_map/ppermute | solution.py:446
  23.1 2.6 %collective-permute-start.5 = (bf16[64,768]{1,0:T(8,128)(2,1)S(1)}, bf16[64,768]{1,0:T(8,128)(2,1)S(1)}, u32[]{:S(2)}, u32[]{:S(2)}) collective-permute-start(bf16[64,768]{1,0:T(8,128)(2,1)S(1)} %get-tuple-element.54), channel_id=1, source_target_pairs={{0,16},{4,20},{8,24},{12,28},{16,0},{20,4},{24,8},{28,12},{1,17},{... | collective-permute-start | bytes 294920 | tf_op jit(solution)/shard_map/ppermute | solution.py:446
  25.7 5.2 %collective-permute-done.5 = bf16[64,768]{1,0:T(8,128)(2,1)S(1)} collective-permute-done((bf16[64,768]{1,0:T(8,128)(2,1)S(1)}, bf16[64,768]{1,0:T(8,128)(2,1)S(1)}, u32[]{:S(2)}, u32[]{:S(2)}) %collective-permute-start.5) | collective-permute-done | bytes 98336 | tf_op jit(solution)/shard_map/ppermute | solution.py:446
  30.9 0.7 collective-permute-start.6
  31.6 1.8 %shard_map.140 = (bf16[256,1024]{1,0:T(8,128)(2,1)S(1)}, f32[16,1024]{1,0:T(8,128)S(1)}, bf16[4,128,256]{2,1,0:T(8,128)(2,1)S(1)}, f32[4,128,256]{2,1,0:T(8,128)S(1)}, bf16[80,1024]{1,0:T(8,128)(2,1)S(1)}) custom-call(s32[2]{0:T(128)S(1)} %pad_add_fusion.ids, s32[4]{0:T(128)S(1)} %bitcast.29, bf16[64,2176]{1,0:T(8,128)(2,1)S(1)} %shard_map.139.p0, ...), custom_call_target="tpu_custom_call" | custom-call | flops 300000000 | bytes 6291456 | tf_op jit(solution)/shard_map/pallas_call | solution.py:40
  33.4 1.6 %collective-permute-start.7 = (bf16[4,128,256]{2,1,0:T(8,128)(2,1)S(1)}, bf16[4,128,256]{2,1,0:T(8,128)(2,1)S(1)}, u32[]{:S(2)}, u32[]{:S(2)}) collective-permute-start(bf16[4,128,256]{2,1,0:T(8,128)(2,1)S(1)} %get-tuple-element.56), channel_id=1, source_target_pairs={{0,4},{4,0},{8,12},{12,8},{16,20},{20,16},{24,28},{28,24},{1,5},{5... | collective-permute-start | bytes 786440 | tf_op jit(solution)/shard_map/ppermute | solution.py:446
  35.0 4.2 %shard_map.141 = (bf16[2,80,2176]{2,1,0:T(8,128)(2,1)}, bf16[80,2176]{1,0:T(8,128)(2,1)}, bf16[80,2176]{1,0:T(8,128)(2,1)S(1)}, bf16[256,1024]{1,0:T(8,128)(2,1)S(1)}, bf16[64,256]{1,0:T(8,128)(2,1)S(1)}) custom-call(s32[2]{0:T(128)S(1)} %pad_add_fusion.ids, bf16[2048,1024]{1,0:T(8,128)(2,1)S(1)} %bitcast.18, bf16[3,1024,256]{2,1,0:T(8,128)(2,1)S(1)} %bitcast.21, ...), custom_call_target="tpu_custom_call" | custom-call | flops 1000000000 | bytes 8388608 | tf_op jit(solution)/shard_map/pallas_call | solution.py:40
  39.2 0.7 copy-done.4
  39.9 1.4 %shard_map.145 = bf16[8,272,256]{2,1,0:T(8,128)(2,1)} custom-call(bf16[256,1024]{1,0:T(8,128)(2,1)S(1)} %get-tuple-element.61.tbuf, bf16[256,256]{1,0:T(8,128)(2,1)S(1)} %get-tuple-element.62.qx, bf16[64,256]{1,0:T(8,128)(2,1)S(1)} %get-tuple-element.63.d_query, bf16[64,1024]{1,0:T(8,128)(2,1)S(1)} %get-tuple-element.40.cls, ...), custom_call_target="tpu_custom_call" | custom-call | flops 100000000 | bytes 3145728 | tf_op jit(solution)/shard_map/pallas_call | solution.py:40
  41.3 0.1 collective-permute-done.7.got
  41.5 5.6 %all-to-all-start = ((bf16[8,272,256]{2,1,0:T(8,128)(2,1)}), bf16[8,272,256]{2,1,0:T(8,128)(2,1)S(1)}, u32[]{:S(2)}, u32[]{:S(2)}) async-start(bf16[8,272,256]{2,1,0:T(8,128)(2,1)} %shard_map.145), calls=%async_computation | async-start | bytes 2228224 | tf_op jit(solution)/shard_map/all_to_all | solution.py:587
  47.1 0.9 %collective-permute-start.3 = (bf16[2,80,2176]{2,1,0:T(8,128)(2,1)}, bf16[2,80,2176]{2,1,0:T(8,128)(2,1)S(1)}, u32[]{:S(2)}, u32[]{:S(2)}) collective-permute-start(bf16[2,80,2176]{2,1,0:T(8,128)(2,1)} %get-tuple-element.51), channel_id=1, source_target_pairs={{0,2},{1,3},{2,0},{3,1},{4,6},{5,7},{6,4},{7,5},{8,10},{9,11},{10,... | collective-permute-start | bytes 2088968 | tf_op jit(solution)/shard_map/ppermute | solution.py:446
  48.0 2.0 %collective-permute-start.9 = (bf16[4,64,768]{2,1,0:T(8,128)(2,1)S(1)}, bf16[4,64,768]{2,1,0:T(8,128)(2,1)S(1)}, u32[]{:S(2)}, u32[]{:S(2)}) collective-permute-start(bf16[4,64,768]{2,1,0:T(8,128)(2,1)S(1)} %pad_maximum_fusion), channel_id=1, source_target_pairs={{0,4},{4,0},{8,12},{12,8},{16,20},{20,16},{24,28},{28,24},{1,5},{5... | collective-permute-start | bytes 1179656 | tf_op jit(solution)/shard_map/ppermute | solution.py:446
  50.0 1.5 %collective-permute-start.8 = (bf16[2,128,256]{2,1,0:T(8,128)(2,1)S(1)}, bf16[2,128,256]{2,1,0:T(8,128)(2,1)S(1)}, u32[]{:S(2)}, u32[]{:S(2)}) collective-permute-start(bf16[2,128,256]{2,1,0:T(8,128)(2,1)S(1)} %get-tuple-element.58), channel_id=1, source_target_pairs={{0,8},{4,12},{8,0},{12,4},{16,24},{20,28},{24,16},{28,20},{1,9},{5... | collective-permute-start | bytes 393224 | tf_op jit(solution)/shard_map/ppermute | solution.py:446
  51.5 15.6 %collective-permute-done.8.got = bf16[2,128,256]{2,1,0:T(8,128)(2,1)S(1)} collective-permute-done((bf16[2,128,256]{2,1,0:T(8,128)(2,1)S(1)}, bf16[2,128,256]{2,1,0:T(8,128)(2,1)S(1)}, u32[]{:S(2)}, u32[]{:S(2)}) %collective-permute-start.8) | collective-permute-done | bytes 131104 | tf_op jit(solution)/shard_map/ppermute | solution.py:446
  67.2 1.7 %collective-permute-done.9 = bf16[4,64,768]{2,1,0:T(8,128)(2,1)S(1)} collective-permute-done((bf16[4,64,768]{2,1,0:T(8,128)(2,1)S(1)}, bf16[4,64,768]{2,1,0:T(8,128)(2,1)S(1)}, u32[]{:S(2)}, u32[]{:S(2)}) %collective-permute-start.9) | collective-permute-done | bytes 393248 | tf_op jit(solution)/shard_map/ppermute | solution.py:446
  68.9 0.1 collective-permute-start.11
  69.0 0.1 slice_bitcast_fusion
  69.0 0.5 collective-permute-start.4
  69.6 3.0 %collective-permute-start.10 = (bf16[128,256]{1,0:T(8,128)(2,1)S(1)}, bf16[128,256]{1,0:T(8,128)(2,1)S(1)}, u32[]{:S(2)}, u32[]{:S(2)}) collective-permute-start(bf16[128,256]{1,0:T(8,128)(2,1)S(1)} %get-tuple-element.66), channel_id=1, source_target_pairs={{0,16},{4,20},{8,24},{12,28},{16,0},{20,4},{24,8},{28,12},{1,17},{... | collective-permute-start | bytes 196616 | tf_op jit(solution)/shard_map/ppermute | solution.py:446
  72.6 1.8 %shard_map.142 = bf16[16,32,1024]{2,1,0:T(8,128)(2,1)} custom-call(bf16[80,2176]{1,0:T(8,128)(2,1)S(1)} %copy-done.5, bf16[80,2176]{1,0:T(8,128)(2,1)S(1)} %collective-permute-done.2.p1, bf16[80,2176]{1,0:T(8,128)(2,1)S(1)} %get-tuple-element.72.p2, bf16[80,2176]{1,0:T(8,128)(2,1)S(1)} %collective-permute-done.4.p3, f32[16,1024]{1,0:T(8,128)S(1)} %get-tuple-element.52.own_resid), custom_call_target="tpu_custom_call" | custom-call | flops 300000000 | bytes 4194304 | tf_op jit(solution)/shard_map/pallas_call | solution.py:40
  74.4 1.9 %collective-permute-done.10.v1 = bf16[128,256]{1,0:T(8,128)(2,1)S(1)} collective-permute-done((bf16[128,256]{1,0:T(8,128)(2,1)S(1)}, bf16[128,256]{1,0:T(8,128)(2,1)S(1)}, u32[]{:S(2)}, u32[]{:S(2)}) %collective-permute-start.10) | collective-permute-done | bytes 65568 | tf_op jit(solution)/shard_map/ppermute | solution.py:446
  76.4 1.6 %shard_map.146 = (f32[3,128,256]{2,1,0:T(8,128)}, f32[256,128]{1,0:T(8,128)}, f32[2,128]{1,0:T(2,128)}) custom-call(s32[2]{0:T(128)S(1)} %pad_add_fusion.ids, bf16[8,64,768]{2,1,0:T(8,128)(2,1)S(1)} %constant_dynamic-update-slice_fusion.gathered.mine_all, bf16[8,272,256]{2,1,0:T(8,128)(2,1)S(1)} %all-to-all-done.spread, ...), custom_call_target="tpu_custom_call" | custom-call | flops 100000000 | bytes 1048576 | tf_op jit(solution)/shard_map/pallas_call | solution.py:40
  78.0 3.0 %shard_map.147 = f32[8,32,1024]{2,1,0:T(8,128)} custom-call(s32[2]{0:T(128)S(1)} %pad_add_fusion.ids, bf16[8,64,768]{2,1,0:T(8,128)(2,1)S(1)} %constant_dynamic-update-slice_fusion.gathered.mine_all, bf16[8,64,768]{2,1,0:T(8,128)(2,1)S(1)} %collective-permute-done.11.other_all, bf16[8,272,256]{2,1,0:T(8,128)(2,1)S(1)} %all-to-all-done.spread, ...), custom_call_target="tpu_custom_call" | custom-call | flops 500000000 | bytes 4194304 | tf_op jit(solution)/shard_map/pallas_call | solution.py:40
  (36 shorter events, 0.3 us)
Async XLA Ops:
  0.6 0.7 copy-start.11
  1.3 15.3 %copy-start.2 = (bf16[8,256,1024]{2,1,0:T(8,128)(2,1)S(1)}, bf16[8,256,1024]{2,1,0:T(8,128)(2,1)}, u32[]{:S(2)}) copy-start(bf16[8,256,1024]{2,1,0:T(8,128)(2,1)} %table.1) | copy-start | bytes 12582916
  1.3 15.3 %copy-start.6 = (f32[1024]{0:T(1024)S(1)}, f32[1024]{0:T(1024)}, u32[]{:S(2)}) copy-start(f32[1024]{0:T(1024)} %param.13) | copy-start | bytes 12292
  1.3 15.3 %copy-start.7 = (f32[1024]{0:T(1024)S(1)}, f32[1024]{0:T(1024)}, u32[]{:S(2)}) copy-start(f32[1024]{0:T(1024)} %param.14) | copy-start | bytes 12292
  1.3 15.3 %copy-start.8 = (s32[1,4]{1,0:T(1,128)S(1)}, s32[1,4]{1,0:T(1,128)}, u32[]{:S(2)}) copy-start(s32[1,4]{1,0:T(1,128)} %param.19) | copy-start | bytes 52
  1.3 15.3 %copy-start.9 = (s32[64]{0:T(128)S(1)}, s32[64]{0:T(128)}, u32[]{:S(2)}) copy-start(s32[64]{0:T(128)} %param.17) | copy-start | bytes 772
  1.3 15.3 %copy-start.10 = (s32[64]{0:T(128)S(1)}, s32[64]{0:T(128)}, u32[]{:S(2)}) copy-start(s32[64]{0:T(128)} %param.18) | copy-start | bytes 772
  16.7 14.9 %copy-start.1 = (bf16[1024,3,256]{2,0,1:T(8,128)(2,1)S(1)}, bf16[1024,3,256]{2,0,1:T(8,128)(2,1)}, u32[]{:S(2)}) copy-start(bf16[1024,3,256]{2,0,1:T(8,128)(2,1)} %param.11) | copy-start | bytes 4718596
  20.1 11.5 %copy-start.3 = (bf16[256,1024]{1,0:T(8,128)(2,1)S(1)}, bf16[256,1024]{1,0:T(8,128)(2,1)}, u32[]{:S(2)}) copy-start(bf16[256,1024]{1,0:T(8,128)(2,1)} %wo_ref.1) | copy-start | bytes 1572868
  20.1 1.6 %collective-permute-start = (bf16[64,2176]{1,0:T(8,128)(2,1)S(1)}, bf16[64,2176]{1,0:T(8,128)(2,1)S(1)}, u32[]{:S(2)}, u32[]{:S(2)}) collective-permute-start(bf16[64,2176]{1,0:T(8,128)(2,1)S(1)} %get-tuple-element.42.p), channel_id=1, source_target_pairs={{0,1},{1,0},{2,3},{3,2},{4,5},{5,4},{6,7},{7,6},{8,9},{9,8},{10,11... | collective-permute-start | bytes 835592 | tf_op jit(solution)/shard_map/ppermute | solution.py:446
  21.7 13.3 %copy-start = (bf16[64,32,1024]{2,1,0:T(8,128)(2,1)S(1)}, bf16[64,32,1024]{2,1,0:T(8,128)(2,1)}, u32[]{:S(2)}) copy-start(bf16[64,32,1024]{2,1,0:T(8,128)(2,1)} %param.10) | copy-start | bytes 12582916
  21.9 9.7 %collective-permute-start.1 = (bf16[64,2176]{1,0:T(8,128)(2,1)S(1)}, bf16[64,2176]{1,0:T(8,128)(2,1)S(1)}, u32[]{:S(2)}, u32[]{:S(2)}) collective-permute-start(bf16[64,2176]{1,0:T(8,128)(2,1)S(1)} %shard_map.139.p0), channel_id=1, source_target_pairs={{0,2},{1,3},{2,0},{3,1},{4,6},{5,7},{6,4},{7,5},{8,10},{9,11},{10,... | collective-permute-start | bytes 835592 | tf_op jit(solution)/shard_map/ppermute | solution.py:446
  23.1 7.8 %collective-permute-start.5 = (bf16[64,768]{1,0:T(8,128)(2,1)S(1)}, bf16[64,768]{1,0:T(8,128)(2,1)S(1)}, u32[]{:S(2)}, u32[]{:S(2)}) collective-permute-start(bf16[64,768]{1,0:T(8,128)(2,1)S(1)} %get-tuple-element.54), channel_id=1, source_target_pairs={{0,16},{4,20},{8,24},{12,28},{16,0},{20,4},{24,8},{28,12},{1,17},{... | collective-permute-start | bytes 294920 | tf_op jit(solution)/shard_map/ppermute | solution.py:446
  30.9 10.4 %collective-permute-start.6 = (bf16[2,64,768]{2,1,0:T(8,128)(2,1)S(1)}, bf16[2,64,768]{2,1,0:T(8,128)(2,1)S(1)}, u32[]{:S(2)}, u32[]{:S(2)}) collective-permute-start(bf16[2,64,768]{2,1,0:T(8,128)(2,1)S(1)} %pad_maximum_fusion.1), channel_id=1, source_target_pairs={{0,8},{4,12},{8,0},{12,4},{16,24},{20,28},{24,16},{28,20},{1,9},{5... | collective-permute-start | bytes 589832 | tf_op jit(solution)/shard_map/ppermute | solution.py:446
  33.4 8.0 %collective-permute-start.7 = (bf16[4,128,256]{2,1,0:T(8,128)(2,1)S(1)}, bf16[4,128,256]{2,1,0:T(8,128)(2,1)S(1)}, u32[]{:S(2)}, u32[]{:S(2)}) collective-permute-start(bf16[4,128,256]{2,1,0:T(8,128)(2,1)S(1)} %get-tuple-element.56), channel_id=1, source_target_pairs={{0,4},{4,0},{8,12},{12,8},{16,20},{20,16},{24,28},{28,24},{1,5},{5... | collective-permute-start | bytes 786440 | tf_op jit(solution)/shard_map/ppermute | solution.py:446
  39.2 0.7 copy-start.4
  41.5 34.9 %all-to-all-start = ((bf16[8,272,256]{2,1,0:T(8,128)(2,1)}), bf16[8,272,256]{2,1,0:T(8,128)(2,1)S(1)}, u32[]{:S(2)}, u32[]{:S(2)}) async-start(bf16[8,272,256]{2,1,0:T(8,128)(2,1)} %shard_map.145), calls=%async_computation | async-start | bytes 2228224 | tf_op jit(solution)/shard_map/all_to_all | solution.py:587
  47.1 21.9 %collective-permute-start.3 = (bf16[2,80,2176]{2,1,0:T(8,128)(2,1)}, bf16[2,80,2176]{2,1,0:T(8,128)(2,1)S(1)}, u32[]{:S(2)}, u32[]{:S(2)}) collective-permute-start(bf16[2,80,2176]{2,1,0:T(8,128)(2,1)} %get-tuple-element.51), channel_id=1, source_target_pairs={{0,2},{1,3},{2,0},{3,1},{4,6},{5,7},{6,4},{7,5},{8,10},{9,11},{10,... | collective-permute-start | bytes 2088968 | tf_op jit(solution)/shard_map/ppermute | solution.py:446
  48.0 20.9 %collective-permute-start.9 = (bf16[4,64,768]{2,1,0:T(8,128)(2,1)S(1)}, bf16[4,64,768]{2,1,0:T(8,128)(2,1)S(1)}, u32[]{:S(2)}, u32[]{:S(2)}) collective-permute-start(bf16[4,64,768]{2,1,0:T(8,128)(2,1)S(1)} %pad_maximum_fusion), channel_id=1, source_target_pairs={{0,4},{4,0},{8,12},{12,8},{16,20},{20,16},{24,28},{28,24},{1,5},{5... | collective-permute-start | bytes 1179656 | tf_op jit(solution)/shard_map/ppermute | solution.py:446
  50.0 17.1 %collective-permute-start.8 = (bf16[2,128,256]{2,1,0:T(8,128)(2,1)S(1)}, bf16[2,128,256]{2,1,0:T(8,128)(2,1)S(1)}, u32[]{:S(2)}, u32[]{:S(2)}) collective-permute-start(bf16[2,128,256]{2,1,0:T(8,128)(2,1)S(1)} %get-tuple-element.58), channel_id=1, source_target_pairs={{0,8},{4,12},{8,0},{12,4},{16,24},{20,28},{24,16},{28,20},{1,9},{5... | collective-permute-start | bytes 393224 | tf_op jit(solution)/shard_map/ppermute | solution.py:446
  51.5 21.1 %collective-permute-start.2 = (bf16[80,2176]{1,0:T(8,128)(2,1)}, bf16[80,2176]{1,0:T(8,128)(2,1)S(1)}, u32[]{:S(2)}, u32[]{:S(2)}) collective-permute-start(bf16[80,2176]{1,0:T(8,128)(2,1)} %get-tuple-element.50), channel_id=1, source_target_pairs={{0,1},{1,0},{2,3},{3,2},{4,5},{5,4},{6,7},{7,6},{8,9},{9,8},{10,11... | collective-permute-start | bytes 1044488 | tf_op jit(solution)/shard_map/ppermute | solution.py:446
  67.1 5.5 %copy-start.5 = (bf16[80,2176]{1,0:T(8,128)(2,1)S(1)}, bf16[80,2176]{1,0:T(8,128)(2,1)}, u32[]{:S(2)}) copy-start(bf16[80,2176]{1,0:T(8,128)(2,1)} %copy-done.4) | copy-start | bytes 1044484
  68.9 9.1 %collective-permute-start.11 = (bf16[8,64,768]{2,1,0:T(8,128)(2,1)S(1)}, bf16[8,64,768]{2,1,0:T(8,128)(2,1)S(1)}, u32[]{:S(2)}, u32[]{:S(2)}) collective-permute-start(bf16[8,64,768]{2,1,0:T(8,128)(2,1)S(1)} %constant_dynamic-update-slice_fusion.gathered.mine_all), channel_id=1, source_target_pairs={{0,1},{1,0},{2,3},{3,2},{4,5},{5,4},{6,7},{7,6},{8,9},{9,8},{10,11... | collective-permute-start | bytes 2359304 | tf_op jit(solution)/shard_map/ppermute | solution.py:446
  69.0 3.6 %collective-permute-start.4 = (bf16[80,2176]{1,0:T(8,128)(2,1)S(1)}, bf16[80,2176]{1,0:T(8,128)(2,1)S(1)}, u32[]{:S(2)}, u32[]{:S(2)}) collective-permute-start(bf16[80,2176]{1,0:T(8,128)(2,1)S(1)} %get-tuple-element.71), channel_id=1, source_target_pairs={{0,1},{1,0},{2,3},{3,2},{4,5},{5,4},{6,7},{7,6},{8,9},{9,8},{10,11... | collective-permute-start | bytes 1044488 | tf_op jit(solution)/shard_map/ppermute | solution.py:446
  69.6 6.8 %collective-permute-start.10 = (bf16[128,256]{1,0:T(8,128)(2,1)S(1)}, bf16[128,256]{1,0:T(8,128)(2,1)S(1)}, u32[]{:S(2)}, u32[]{:S(2)}) collective-permute-start(bf16[128,256]{1,0:T(8,128)(2,1)S(1)} %get-tuple-element.66), channel_id=1, source_target_pairs={{0,16},{4,20},{8,24},{12,28},{16,0},{20,4},{24,8},{28,12},{1,17},{... | collective-permute-start | bytes 196616 | tf_op jit(solution)/shard_map/ppermute | solution.py:446

commit v4 on v3

--- a/solution.py
+++ b/solution.py
@@ -89,14 +89,16 @@
     part += [pltpu.make_async_copy(wo_in, wo_ref, sems.at[groups + 3])]
     for copy in part:
         copy.start()
-    pick = lax.broadcasted_iota(jnp.int32, (GROUP, span), 1) == seq * lax.broadcasted_iota(
-        jnp.int32, (GROUP, span), 0
-    )
-    pick = pick.astype(F32).astype(BF)
+    line = lax.broadcasted_iota(jnp.int32, (GROUP, width), 0)
     firsts = []
     for g in range(groups):
         part[1 + g].wait()
-        firsts.append(mm(pick, hid[g * span : (g + 1) * span, :]))
+        rows_of = jnp.zeros((GROUP, width), F32)
+        for m in range(GROUP):
+            at = g * span + m * seq
+            row = hid[at : at + 16, :].astype(F32)[0:1, :]
+            rows_of = jnp.where(line == m, row, rows_of)
+        firsts.append(rows_of)
     cls = jnp.concatenate(firsts, axis=0).astype(BF)
     cls_out[...] = cls
     part[0].wait()
@@ -596,7 +598,7 @@
     grad_qkv, grad_wo, grad_ln = call(
         small_body,
         [sds((3, *tile), F32), sds((cols, step), F32), sds((2, step), F32)],
-        [ids, gathered, spread, v_keep, v_got],
+        [ids, gathered, after(spread, grad_table), v_keep, v_got],
         flops=10**8,
         moved=2**20,
     )

time: 81.2 us -> 78.9 us (0.972)
  waiting for transfers between devices: 25.8 us -> 23.8 us
    ppermute x12, waiting for transfers between devices: 25.8 us -> 23.8 us  [swap(): return lax.ppermute(x, axis, [(i, i ^ k) for i in range(size)])]
  transfers between devices with their start and end apart: 13 -> 13, of which waited for: 6 -> 5; matrix products, arithmetic and copies ran while one was open for 0% -> 0% of each run, Pallas kernels for 13% -> 15%
where the time goes in v4:
time: 78.9 us; the launch traced here: 78.7 us
  waiting for transfers between devices  23.8 us (30%)
  Pallas kernels  23.7 us (30%)
  starting transfers between devices  20.1 us (25%)
  blocking collectives  8.65 us (11%)
  local copies, waits for them, and re-layouts  1.53 us (2%)
  between operations  0.8 us (1%)
    ppermute x12, waiting for transfers between devices, swap(): return lax.ppermute(x, axis, [(i, i ^ k) for i in range(size)])  23.8 us
    pallas_call x11, Pallas kernels, call(): pl.pallas_call(body, out_shape=outs, in_specs=[SMEM] * smem + [VMEM] * in...  23.7 us
    ppermute x12, starting transfers between devices, swap(): return lax.ppermute(x, axis, [(i, i ^ k) for i in range(size)])  14.5 us
    all_gather x1, blocking collectives, on_device(): attns = lax.all_gather(attn, 'ent')  8.65 us
    all_to_all x1, starting transfers between devices, on_device(): spread = lax.all_to_all(after(spread, v_sent, zs), 'ment', 0, 0)  5.6 us
  transfers between devices with their start and end apart: 13, of which 5 were waited for; matrix products, arithmetic and copies ran while one was open for 0% of the time, Pallas kernels for 15%

profile of v4, /device:TPU:0, one launch (start us, length us, event | category | flops | bytes accessed | tf_op | source)
XLA Modules:
  0.0 78.7 jit_solution(10832310027381352340)
XLA Ops:
  0.6 0.6 copy-done.11
  1.3 6.2 %shard_map.137 = (bf16[64,1024]{1,0:T(8,128)(2,1)S(1)}, bf16[64,1024]{1,0:T(8,128)(2,1)S(1)}, bf16[64,256]{1,0:T(8,128)(2,1)S(1)}, f32[256,256]{1,0:T(8,128)S(1)...) custom-call(s32[64]{0:T(128)S(1)} %copy-done.11, ...), custom_call_target="tpu_custom_call" | custom-call | flops 1000000000 | bytes 8388608 | tf_op jit(solution)/shard_map/pallas_call | solution.py:40
  7.5 8.6 %all-gather = bf16[256,1024]{1,0:T(8,128)(2,1)S(1)} all-gather(bf16[64,1024]{1,0:T(8,128)(2,1)S(1)} %get-tuple-element.40), channel_id=2, replica_groups=mesh['ment'=8,'ent'=4] {'ent'}, dimensions={0}, use_global_device_ids=true | all-gather | bytes 655360 | tf_op jit(solution)/shard_map/all_gather | solution.py:509
  16.2 0.1 pad_add_fusion.ids
  16.3 0.0 copy-start.1
  16.3 3.5 %shard_map.138 = (bf16[64,1024]{1,0:T(8,128)(2,1)}, f32[64,1024]{1,0:T(8,128)S(1)}, f32[64,128]{1,0:T(8,128)S(1)}, bf16[64,2176]{1,0:T(8,128)(2,1)S(1)}, bf16[64...) custom-call(s32[2]{0:T(128)S(1)} %pad_add_fusion.ids, s32[4]{0:T(128)S(1)} %bitcast.28, ...), custom_call_target="tpu_custom_call" | custom-call | flops 600000000 | bytes 6291456 | tf_op jit(solution)/shard_map/pallas_call | solution.py:40
  19.8 0.4 collective-permute-start
  20.1 1.2 %collective-permute-done.q = bf16[64,2176]{1,0:T(8,128)(2,1)S(1)} collective-permute-done((bf16[64,2176]{1,0:T(8,128)(2,1)S(1)}, bf16[64,2176]{1,0:T(8,128)(2,1)S(1)}, u32[]{:S(2)}, u32[]{:S(2)}) %collective-permute-start) | collective-permute-done | bytes 278560 | tf_op jit(solution)/shard_map/ppermute | solution.py:448
  21.3 0.2 shard_map.139.p0
  21.5 1.2 %collective-permute-start.1 = (bf16[64,2176]{1,0:T(8,128)(2,1)S(1)}, bf16[64,2176]{1,0:T(8,128)(2,1)S(1)}, u32[]{:S(2)}, u32[]{:S(2)}) collective-permute-start(bf16[64,2176]{1,0:T(8,128)(2,1)S(1)} %shard_map.139.p0), channel_id=1, source_target_pairs={{0,2},{1,3},{2,0},{3,1},{4,6},{5,7},{6,4},{7,5},{8,10},{9,11},{10,... | collective-permute-start | bytes 835592 | tf_op jit(solution)/shard_map/ppermute | solution.py:448
  22.7 2.6 %collective-permute-start.5 = (bf16[64,768]{1,0:T(8,128)(2,1)S(1)}, bf16[64,768]{1,0:T(8,128)(2,1)S(1)}, u32[]{:S(2)}, u32[]{:S(2)}) collective-permute-start(bf16[64,768]{1,0:T(8,128)(2,1)S(1)} %get-tuple-element.55), channel_id=1, source_target_pairs={{0,16},{4,20},{8,24},{12,28},{16,0},{20,4},{24,8},{28,12},{1,17},{... | collective-permute-start | bytes 294920 | tf_op jit(solution)/shard_map/ppermute | solution.py:448
  25.3 5.2 %collective-permute-done.5 = bf16[64,768]{1,0:T(8,128)(2,1)S(1)} collective-permute-done((bf16[64,768]{1,0:T(8,128)(2,1)S(1)}, bf16[64,768]{1,0:T(8,128)(2,1)S(1)}, u32[]{:S(2)}, u32[]{:S(2)}) %collective-permute-start.5) | collective-permute-done | bytes 98336 | tf_op jit(solution)/shard_map/ppermute | solution.py:448
  30.5 0.7 collective-permute-start.6
  31.2 1.8 %shard_map.140 = (bf16[256,1024]{1,0:T(8,128)(2,1)S(1)}, f32[16,1024]{1,0:T(8,128)S(1)}, bf16[4,128,256]{2,1,0:T(8,128)(2,1)S(1)}, f32[4,128,256]{2,1,0:T(8,128)S(1)}, bf16[80,1024]{1,0:T(8,128)(2,1)S(1)}) custom-call(s32[2]{0:T(128)S(1)} %pad_add_fusion.ids, s32[4]{0:T(128)S(1)} %bitcast.29, bf16[64,2176]{1,0:T(8,128)(2,1)S(1)} %shard_map.139.p0, ...), custom_call_target="tpu_custom_call" | custom-call | flops 300000000 | bytes 6291456 | tf_op jit(solution)/shard_map/pallas_call | solution.py:40
  33.0 1.6 %collective-permute-start.7 = (bf16[4,128,256]{2,1,0:T(8,128)(2,1)S(1)}, bf16[4,128,256]{2,1,0:T(8,128)(2,1)S(1)}, u32[]{:S(2)}, u32[]{:S(2)}) collective-permute-start(bf16[4,128,256]{2,1,0:T(8,128)(2,1)S(1)} %get-tuple-element.57), channel_id=1, source_target_pairs={{0,4},{4,0},{8,12},{12,8},{16,20},{20,16},{24,28},{28,24},{1,5},{5... | collective-permute-start | bytes 786440 | tf_op jit(solution)/shard_map/ppermute | solution.py:448
  34.6 4.2 %shard_map.141 = (bf16[2,80,2176]{2,1,0:T(8,128)(2,1)}, bf16[80,2176]{1,0:T(8,128)(2,1)}, bf16[80,2176]{1,0:T(8,128)(2,1)S(1)}, bf16[256,1024]{1,0:T(8,128)(2,1)S(1)}, bf16[64,256]{1,0:T(8,128)(2,1)S(1)}) custom-call(s32[2]{0:T(128)S(1)} %pad_add_fusion.ids, bf16[2048,1024]{1,0:T(8,128)(2,1)S(1)} %bitcast.18, bf16[3,1024,256]{2,1,0:T(8,128)(2,1)S(1)} %bitcast.21, ...), custom_call_target="tpu_custom_call" | custom-call | flops 1000000000 | bytes 8388608 | tf_op jit(solution)/shard_map/pallas_call | solution.py:40
  38.8 0.7 copy-done.4
  39.5 1.4 %shard_map.145 = bf16[8,272,256]{2,1,0:T(8,128)(2,1)} custom-call(bf16[256,1024]{1,0:T(8,128)(2,1)S(1)} %get-tuple-element.62.tbuf, bf16[256,256]{1,0:T(8,128)(2,1)S(1)} %get-tuple-element.63.qx, bf16[64,256]{1,0:T(8,128)(2,1)S(1)} %get-tuple-element.64.d_query, bf16[64,1024]{1,0:T(8,128)(2,1)S(1)} %get-tuple-element.41.cls, ...), custom_call_target="tpu_custom_call" | custom-call | flops 100000000 | bytes 3145728 | tf_op jit(solution)/shard_map/pallas_call | solution.py:40
  40.9 0.1 collective-permute-done.7.got
  41.1 5.6 %all-to-all-start = ((bf16[8,272,256]{2,1,0:T(8,128)(2,1)}), bf16[8,272,256]{2,1,0:T(8,128)(2,1)S(1)}, u32[]{:S(2)}, u32[]{:S(2)}) async-start(bf16[8,272,256]{2,1,0:T(8,128)(2,1)} %shard_map.145), calls=%async_computation | async-start | bytes 2228224 | tf_op jit(solution)/shard_map/all_to_all | solution.py:589
  46.7 0.9 %collective-permute-start.3 = (bf16[2,80,2176]{2,1,0:T(8,128)(2,1)}, bf16[2,80,2176]{2,1,0:T(8,128)(2,1)S(1)}, u32[]{:S(2)}, u32[]{:S(2)}) collective-permute-start(bf16[2,80,2176]{2,1,0:T(8,128)(2,1)} %get-tuple-element.52), channel_id=1, source_target_pairs={{0,2},{1,3},{2,0},{3,1},{4,6},{5,7},{6,4},{7,5},{8,10},{9,11},{10,... | collective-permute-start | bytes 2088968 | tf_op jit(solution)/shard_map/ppermute | solution.py:448
  47.6 2.0 %collective-permute-start.9 = (bf16[4,64,768]{2,1,0:T(8,128)(2,1)S(1)}, bf16[4,64,768]{2,1,0:T(8,128)(2,1)S(1)}, u32[]{:S(2)}, u32[]{:S(2)}) collective-permute-start(bf16[4,64,768]{2,1,0:T(8,128)(2,1)S(1)} %pad_maximum_fusion), channel_id=1, source_target_pairs={{0,4},{4,0},{8,12},{12,8},{16,20},{20,16},{24,28},{28,24},{1,5},{5... | collective-permute-start | bytes 1179656 | tf_op jit(solution)/shard_map/ppermute | solution.py:448
  49.7 1.5 %collective-permute-start.8 = (bf16[2,128,256]{2,1,0:T(8,128)(2,1)S(1)}, bf16[2,128,256]{2,1,0:T(8,128)(2,1)S(1)}, u32[]{:S(2)}, u32[]{:S(2)}) collective-permute-start(bf16[2,128,256]{2,1,0:T(8,128)(2,1)S(1)} %get-tuple-element.59), channel_id=1, source_target_pairs={{0,8},{4,12},{8,0},{12,4},{16,24},{20,28},{24,16},{28,20},{1,9},{5... | collective-permute-start | bytes 393224 | tf_op jit(solution)/shard_map/ppermute | solution.py:448
  51.1 15.6 %collective-permute-done.8.got = bf16[2,128,256]{2,1,0:T(8,128)(2,1)S(1)} collective-permute-done((bf16[2,128,256]{2,1,0:T(8,128)(2,1)S(1)}, bf16[2,128,256]{2,1,0:T(8,128)(2,1)S(1)}, u32[]{:S(2)}, u32[]{:S(2)}) %collective-permute-start.8) | collective-permute-done | bytes 131104 | tf_op jit(solution)/shard_map/ppermute | solution.py:448
  66.8 1.7 %collective-permute-done.9 = bf16[4,64,768]{2,1,0:T(8,128)(2,1)S(1)} collective-permute-done((bf16[4,64,768]{2,1,0:T(8,128)(2,1)S(1)}, bf16[4,64,768]{2,1,0:T(8,128)(2,1)S(1)}, u32[]{:S(2)}, u32[]{:S(2)}) %collective-permute-start.9) | collective-permute-done | bytes 393248 | tf_op jit(solution)/shard_map/ppermute | solution.py:448
  68.5 0.1 collective-permute-start.10
  68.6 0.1 slice_bitcast_fusion
  68.7 0.5 collective-permute-start.4
  69.2 3.0 %collective-permute-start.11 = (bf16[128,256]{1,0:T(8,128)(2,1)S(1)}, bf16[128,256]{1,0:T(8,128)(2,1)S(1)}, u32[]{:S(2)}, u32[]{:S(2)}) collective-permute-start(bf16[128,256]{1,0:T(8,128)(2,1)S(1)} %get-tuple-element.69), channel_id=1, source_target_pairs={{0,16},{4,20},{8,24},{12,28},{16,0},{20,4},{24,8},{28,12},{1,17},{... | collective-permute-start | bytes 196616 | tf_op jit(solution)/shard_map/ppermute | solution.py:448
  72.3 1.8 %shard_map.142 = bf16[16,32,1024]{2,1,0:T(8,128)(2,1)} custom-call(bf16[80,2176]{1,0:T(8,128)(2,1)S(1)} %copy-done.5, bf16[80,2176]{1,0:T(8,128)(2,1)S(1)} %collective-permute-done.2.p1, bf16[80,2176]{1,0:T(8,128)(2,1)S(1)} %get-tuple-element.74.p2, bf16[80,2176]{1,0:T(8,128)(2,1)S(1)} %collective-permute-done.4.p3, f32[16,1024]{1,0:T(8,128)S(1)} %get-tuple-element.53.own_resid), custom_call_target="tpu_custom_call" | custom-call | flops 300000000 | bytes 4194304 | tf_op jit(solution)/shard_map/pallas_call | solution.py:40
  74.1 3.0 %shard_map.146 = f32[8,32,1024]{2,1,0:T(8,128)} custom-call(s32[2]{0:T(128)S(1)} %pad_add_fusion.ids, bf16[8,64,768]{2,1,0:T(8,128)(2,1)S(1)} %constant_dynamic-update-slice_fusion.mine_all.gathered, bf16[8,64,768]{2,1,0:T(8,128)(2,1)S(1)} %collective-permute-done.10.other_all, bf16[8,272,256]{2,1,0:T(8,128)(2,1)S(1)} %all-to-all-done.spread, ...), custom_call_target="tpu_custom_call" | custom-call | flops 500000000 | bytes 4194304 | tf_op jit(solution)/shard_map/pallas_call | solution.py:40
  77.1 1.6 %shard_map.147 = (f32[3,128,256]{2,1,0:T(8,128)}, f32[256,128]{1,0:T(8,128)}, f32[2,128]{1,0:T(2,128)}) custom-call(s32[2]{0:T(128)S(1)} %pad_add_fusion.ids, bf16[8,64,768]{2,1,0:T(8,128)(2,1)S(1)} %constant_dynamic-update-slice_fusion.mine_all.gathered, bf16[8,272,256]{2,1,0:T(8,128)(2,1)S(1)} %all-to-all-done.spread, ...), custom_call_target="tpu_custom_call" | custom-call | flops 100000000 | bytes 1048576 | tf_op jit(solution)/shard_map/pallas_call | solution.py:40
  (36 shorter events, 0.2 us)
Async XLA Ops:
  0.6 0.7 copy-start.11
  1.3 15.0 %copy-start.2 = (bf16[8,256,1024]{2,1,0:T(8,128)(2,1)S(1)}, bf16[8,256,1024]{2,1,0:T(8,128)(2,1)}, u32[]{:S(2)}) copy-start(bf16[8,256,1024]{2,1,0:T(8,128)(2,1)} %table.1) | copy-start | bytes 12582916
  1.3 15.0 %copy-start.6 = (f32[1024]{0:T(1024)S(1)}, f32[1024]{0:T(1024)}, u32[]{:S(2)}) copy-start(f32[1024]{0:T(1024)} %param.13) | copy-start | bytes 12292
  1.3 15.0 %copy-start.7 = (f32[1024]{0:T(1024)S(1)}, f32[1024]{0:T(1024)}, u32[]{:S(2)}) copy-start(f32[1024]{0:T(1024)} %param.14) | copy-start | bytes 12292
  1.3 15.0 %copy-start.8 = (s32[1,4]{1,0:T(1,128)S(1)}, s32[1,4]{1,0:T(1,128)}, u32[]{:S(2)}) copy-start(s32[1,4]{1,0:T(1,128)} %param.19) | copy-start | bytes 52
  1.3 15.0 %copy-start.9 = (s32[64]{0:T(128)S(1)}, s32[64]{0:T(128)}, u32[]{:S(2)}) copy-start(s32[64]{0:T(128)} %param.17) | copy-start | bytes 772
  1.3 15.0 %copy-start.10 = (s32[64]{0:T(128)S(1)}, s32[64]{0:T(128)}, u32[]{:S(2)}) copy-start(s32[64]{0:T(128)} %param.18) | copy-start | bytes 772
  16.3 14.9 %copy-start.1 = (bf16[1024,3,256]{2,0,1:T(8,128)(2,1)S(1)}, bf16[1024,3,256]{2,0,1:T(8,128)(2,1)}, u32[]{:S(2)}) copy-start(bf16[1024,3,256]{2,0,1:T(8,128)(2,1)} %param.11) | copy-start | bytes 4718596
  19.8 11.5 %copy-start.3 = (bf16[256,1024]{1,0:T(8,128)(2,1)S(1)}, bf16[256,1024]{1,0:T(8,128)(2,1)}, u32[]{:S(2)}) copy-start(bf16[256,1024]{1,0:T(8,128)(2,1)} %wo_ref.1) | copy-start | bytes 1572868
  19.8 1.6 %collective-permute-start = (bf16[64,2176]{1,0:T(8,128)(2,1)S(1)}, bf16[64,2176]{1,0:T(8,128)(2,1)S(1)}, u32[]{:S(2)}, u32[]{:S(2)}) collective-permute-start(bf16[64,2176]{1,0:T(8,128)(2,1)S(1)} %get-tuple-element.43.p), channel_id=1, source_target_pairs={{0,1},{1,0},{2,3},{3,2},{4,5},{5,4},{6,7},{7,6},{8,9},{9,8},{10,11... | collective-permute-start | bytes 835592 | tf_op jit(solution)/shard_map/ppermute | solution.py:448
  21.3 13.3 %copy-start = (bf16[64,32,1024]{2,1,0:T(8,128)(2,1)S(1)}, bf16[64,32,1024]{2,1,0:T(8,128)(2,1)}, u32[]{:S(2)}) copy-start(bf16[64,32,1024]{2,1,0:T(8,128)(2,1)} %param.10) | copy-start | bytes 12582916
  21.5 9.7 %collective-permute-start.1 = (bf16[64,2176]{1,0:T(8,128)(2,1)S(1)}, bf16[64,2176]{1,0:T(8,128)(2,1)S(1)}, u32[]{:S(2)}, u32[]{:S(2)}) collective-permute-start(bf16[64,2176]{1,0:T(8,128)(2,1)S(1)} %shard_map.139.p0), channel_id=1, source_target_pairs={{0,2},{1,3},{2,0},{3,1},{4,6},{5,7},{6,4},{7,5},{8,10},{9,11},{10,... | collective-permute-start | bytes 835592 | tf_op jit(solution)/shard_map/ppermute | solution.py:448
  22.7 7.8 %collective-permute-start.5 = (bf16[64,768]{1,0:T(8,128)(2,1)S(1)}, bf16[64,768]{1,0:T(8,128)(2,1)S(1)}, u32[]{:S(2)}, u32[]{:S(2)}) collective-permute-start(bf16[64,768]{1,0:T(8,128)(2,1)S(1)} %get-tuple-element.55), channel_id=1, source_target_pairs={{0,16},{4,20},{8,24},{12,28},{16,0},{20,4},{24,8},{28,12},{1,17},{... | collective-permute-start | bytes 294920 | tf_op jit(solution)/shard_map/ppermute | solution.py:448
  30.5 10.4 %collective-permute-start.6 = (bf16[2,64,768]{2,1,0:T(8,128)(2,1)S(1)}, bf16[2,64,768]{2,1,0:T(8,128)(2,1)S(1)}, u32[]{:S(2)}, u32[]{:S(2)}) collective-permute-start(bf16[2,64,768]{2,1,0:T(8,128)(2,1)S(1)} %pad_maximum_fusion.1), channel_id=1, source_target_pairs={{0,8},{4,12},{8,0},{12,4},{16,24},{20,28},{24,16},{28,20},{1,9},{5... | collective-permute-start | bytes 589832 | tf_op jit(solution)/shard_map/ppermute | solution.py:448
  33.0 8.0 %collective-permute-start.7 = (bf16[4,128,256]{2,1,0:T(8,128)(2,1)S(1)}, bf16[4,128,256]{2,1,0:T(8,128)(2,1)S(1)}, u32[]{:S(2)}, u32[]{:S(2)}) collective-permute-start(bf16[4,128,256]{2,1,0:T(8,128)(2,1)S(1)} %get-tuple-element.57), channel_id=1, source_target_pairs={{0,4},{4,0},{8,12},{12,8},{16,20},{20,16},{24,28},{28,24},{1,5},{5... | collective-permute-start | bytes 786440 | tf_op jit(solution)/shard_map/ppermute | solution.py:448
  38.8 0.7 copy-start.4
  41.1 33.0 %all-to-all-start = ((bf16[8,272,256]{2,1,0:T(8,128)(2,1)}), bf16[8,272,256]{2,1,0:T(8,128)(2,1)S(1)}, u32[]{:S(2)}, u32[]{:S(2)}) async-start(bf16[8,272,256]{2,1,0:T(8,128)(2,1)} %shard_map.145), calls=%async_computation | async-start | bytes 2228224 | tf_op jit(solution)/shard_map/all_to_all | solution.py:589
  46.7 21.9 %collective-permute-start.3 = (bf16[2,80,2176]{2,1,0:T(8,128)(2,1)}, bf16[2,80,2176]{2,1,0:T(8,128)(2,1)S(1)}, u32[]{:S(2)}, u32[]{:S(2)}) collective-permute-start(bf16[2,80,2176]{2,1,0:T(8,128)(2,1)} %get-tuple-element.52), channel_id=1, source_target_pairs={{0,2},{1,3},{2,0},{3,1},{4,6},{5,7},{6,4},{7,5},{8,10},{9,11},{10,... | collective-permute-start | bytes 2088968 | tf_op jit(solution)/shard_map/ppermute | solution.py:448
  47.6 20.9 %collective-permute-start.9 = (bf16[4,64,768]{2,1,0:T(8,128)(2,1)S(1)}, bf16[4,64,768]{2,1,0:T(8,128)(2,1)S(1)}, u32[]{:S(2)}, u32[]{:S(2)}) collective-permute-start(bf16[4,64,768]{2,1,0:T(8,128)(2,1)S(1)} %pad_maximum_fusion), channel_id=1, source_target_pairs={{0,4},{4,0},{8,12},{12,8},{16,20},{20,16},{24,28},{28,24},{1,5},{5... | collective-permute-start | bytes 1179656 | tf_op jit(solution)/shard_map/ppermute | solution.py:448
  49.7 17.1 %collective-permute-start.8 = (bf16[2,128,256]{2,1,0:T(8,128)(2,1)S(1)}, bf16[2,128,256]{2,1,0:T(8,128)(2,1)S(1)}, u32[]{:S(2)}, u32[]{:S(2)}) collective-permute-start(bf16[2,128,256]{2,1,0:T(8,128)(2,1)S(1)} %get-tuple-element.59), channel_id=1, source_target_pairs={{0,8},{4,12},{8,0},{12,4},{16,24},{20,28},{24,16},{28,20},{1,9},{5... | collective-permute-start | bytes 393224 | tf_op jit(solution)/shard_map/ppermute | solution.py:448
  51.1 21.1 %collective-permute-start.2 = (bf16[80,2176]{1,0:T(8,128)(2,1)}, bf16[80,2176]{1,0:T(8,128)(2,1)S(1)}, u32[]{:S(2)}, u32[]{:S(2)}) collective-permute-start(bf16[80,2176]{1,0:T(8,128)(2,1)} %get-tuple-element.51), channel_id=1, source_target_pairs={{0,1},{1,0},{2,3},{3,2},{4,5},{5,4},{6,7},{7,6},{8,9},{9,8},{10,11... | collective-permute-start | bytes 1044488 | tf_op jit(solution)/shard_map/ppermute | solution.py:448
  66.8 5.5 %copy-start.5 = (bf16[80,2176]{1,0:T(8,128)(2,1)S(1)}, bf16[80,2176]{1,0:T(8,128)(2,1)}, u32[]{:S(2)}) copy-start(bf16[80,2176]{1,0:T(8,128)(2,1)} %copy-done.4) | copy-start | bytes 1044484
  68.5 5.6 %collective-permute-start.10 = (bf16[8,64,768]{2,1,0:T(8,128)(2,1)S(1)}, bf16[8,64,768]{2,1,0:T(8,128)(2,1)S(1)}, u32[]{:S(2)}, u32[]{:S(2)}) collective-permute-start(bf16[8,64,768]{2,1,0:T(8,128)(2,1)S(1)} %constant_dynamic-update-slice_fusion.mine_all.gathered), channel_id=1, source_target_pairs={{0,1},{1,0},{2,3},{3,2},{4,5},{5,4},{6,7},{7,6},{8,9},{9,8},{10,11... | collective-permute-start | bytes 2359304 | tf_op jit(solution)/shard_map/ppermute | solution.py:448
  68.7 3.6 %collective-permute-start.4 = (bf16[80,2176]{1,0:T(8,128)(2,1)S(1)}, bf16[80,2176]{1,0:T(8,128)(2,1)S(1)}, u32[]{:S(2)}, u32[]{:S(2)}) collective-permute-start(bf16[80,2176]{1,0:T(8,128)(2,1)S(1)} %get-tuple-element.73), channel_id=1, source_target_pairs={{0,1},{1,0},{2,3},{3,2},{4,5},{5,4},{6,7},{7,6},{8,9},{9,8},{10,11... | collective-permute-start | bytes 1044488 | tf_op jit(solution)/shard_map/ppermute | solution.py:448
  69.2 7.9 %collective-permute-start.11 = (bf16[128,256]{1,0:T(8,128)(2,1)S(1)}, bf16[128,256]{1,0:T(8,128)(2,1)S(1)}, u32[]{:S(2)}, u32[]{:S(2)}) collective-permute-start(bf16[128,256]{1,0:T(8,128)(2,1)S(1)} %get-tuple-element.69), channel_id=1, source_target_pairs={{0,16},{4,20},{8,24},{12,28},{16,0},{20,4},{24,8},{28,12},{1,17},{... | collective-permute-start | bytes 196616 | tf_op jit(solution)/shard_map/ppermute | solution.py:448

commit v5 on v4

--- a/solution.py
+++ b/solution.py
@@ -34,14 +34,14 @@
     return jax.ShapeDtypeStruct(shape, dtype)
 
 
-def call(body, outs, ins, scratch=(), flops=0, moved=0, limit=20, outside=0):
+def call(body, outs, ins, scratch=(), flops=0, moved=0, limit=20, outside=0, last=0):
     smem = sum(1 for x in ins if x.ndim == 1 and x.dtype == jnp.int32)
     inside = len(ins) - smem - outside
     return pl.pallas_call(
         body,
         out_shape=outs,
         in_specs=[SMEM] * smem + [VMEM] * inside + [HBM] * outside,
-        out_specs=[VMEM] * len(outs),
+        out_specs=[VMEM] * (len(outs) - last) + [HBM] * last,
         scratch_shapes=list(scratch),
         compiler_params=pltpu.CompilerParams(vmem_limit_bytes=limit * 2**20),
         cost_estimate=pl.CostEstimate(flops=flops, bytes_accessed=moved, transcendentals=0),
@@ -251,7 +251,7 @@
 
 def loss_body(
     ids, negs, p0, p1, normed_ref, rstd_ref, gain, w_ref, wo_ref, mix, gold_block, gold_row,
-    dv_out, own_resid, vsend, vkeep, wide, resid_buf, grad_buf,
+    dx_out, own_resid, vsend, vkeep, wide, resid_buf, grad_buf,
 ):
     count, width = normed_ref.shape
     heads = w_ref.shape[2] // HD
@@ -267,7 +267,7 @@
     half = d_resid.astype(BF)
     d_ctx = mm_nt(half, wo_ref[...]).astype(BF).astype(F32)
     dx = spread_heads(d_ctx, heads)
-    dv_out[...] = mm_nt(dx, w_ref[2]).astype(BF)
+    dx_out[...] = dx
     grad_buf[...] = mm_tn(mix[...], dx)
     store_parts(ids, grad_buf, vsend, vkeep)
     resid_buf[...] = d_resid
@@ -305,8 +305,9 @@
 
 
 def backward_body(
-    ids, hid, w_ref, probs_ref, dv, qk, folded, far, near, own, tbuf, d_query_out, buf, zbuf
+    ids, hid, w_ref, probs_ref, dx, qk, folded, far, near, tbuf, d_query_out, own_out, buf, zbuf, own, dv, sem
 ):
+    dv[...] = mm_nt(dx[...], w_ref[2]).astype(BF)
     tokens, width = hid.shape
     heads = w_ref.shape[2] // HD
     count = d_query_out.shape[0]
@@ -336,6 +337,10 @@
         out[0:share, 2 * width :] = buf[mine, :]
         out[share : share + few, 0:width] = zbuf[pl.ds(pl.multiple_of(peer * few, few), few), :]
         out[share : share + few, width:] = jnp.zeros((few, width + 128), BF)
+        if k == 0:
+            store = pltpu.make_async_copy(own, own_out, sem)
+            store.start()
+    store.wait()
 
 
 def spread_body(tbuf, qx, d_query, cls, wide, spread, grad_buf):
@@ -524,10 +529,10 @@
     )
     pay_pair = call(merge_body, [sds(pay.shape, BF)], [pay, ent(pay, 1)], moved=2**19)[0]
     pay_other = ent(pay_pair, 2)
-    dv, own_resid, vsend, vkeep, wide = call(
+    dx, own_resid, vsend, vkeep, wide = call(
         loss_body,
         [
-            sds((hrows, width), BF),
+            sds((hrows, cols), BF),
             sds((few, width), F32),
             sds((pairs, step, cols), BF),
             sds((pairs, step, cols), F32),
@@ -538,17 +543,24 @@
         flops=3 * 10**8,
         moved=6 * 2**20,
     )
-    far, near, own, mixed, d_query = call(
+    far, near, mixed, d_query, own = call(
         backward_body,
         [
             sds((2, share + few, 2 * width + 128), BF),
             sds((share + few, 2 * width + 128), BF),
-            sds((share + few, 2 * width + 128), BF),
             sds((hrows, width), BF),
             sds((count, cols), BF),
+            sds((share + few, 2 * width + 128), BF),
         ],
-        [ids, hid, w, probs, dv, qk, folded],
-        [pltpu.VMEM((hrows, 128), BF), pltpu.VMEM((count, width), BF)],
+        [ids, hid, w, probs, dx, qk, folded],
+        [
+            pltpu.VMEM((hrows, 128), BF),
+            pltpu.VMEM((count, width), BF),
+            pltpu.VMEM((share + few, 2 * width + 128), BF),
+            pltpu.VMEM((hrows, width), BF),
+            pltpu.SemaphoreType.DMA,
+        ],
+        last=1,
         flops=10**9,
         moved=8 * 2**20,
     )

time: 78.9 us -> 78.8 us (level)
  transfers between devices with their start and end apart: 13 -> 13, of which waited for: 5 -> 5; matrix products, arithmetic and copies ran while one was open for 0% -> 0% of each run, Pallas kernels for 15% -> 16%
where the time goes in v5:
time: 78.8 us; the launch traced here: 78.6 us
  waiting for transfers between devices  24.1 us (31%)
  Pallas kernels  24 us (30%)
  starting transfers between devices  20.1 us (26%)
  blocking collectives  8.65 us (11%)
  between operations  0.82 us (1%)
  local copies, waits for them, and re-layouts  0.8 us (1%)
    ppermute x12, waiting for transfers between devices, swap(): return lax.ppermute(x, axis, [(i, i ^ k) for i in range(size)])  24.1 us
    pallas_call x11, Pallas kernels, call(): pl.pallas_call(body, out_shape=outs, in_specs=[SMEM] * smem + [VMEM] * in...  24 us
    ppermute x12, starting transfers between devices, swap(): return lax.ppermute(x, axis, [(i, i ^ k) for i in range(size)])  14.5 us
    all_gather x1, blocking collectives, on_device(): attns = lax.all_gather(attn, 'ent')  8.65 us
    all_to_all x1, starting transfers between devices, on_device(): spread = lax.all_to_all(after(spread, v_sent, zs), 'ment', 0, 0)  5.6 us
  transfers between devices with their start and end apart: 13, of which 5 were waited for; matrix products, arithmetic and copies ran while one was open for 0% of the time, Pallas kernels for 16%

profile of v5, /device:TPU:0, one launch (start us, length us, event | category | flops | bytes accessed | tf_op | source)
XLA Modules:
  0.0 78.6 jit_solution(17044888656408385634)
XLA Ops:
  0.6 0.6 copy-done.11
  1.3 6.2 %shard_map.137 = (bf16[64,1024]{1,0:T(8,128)(2,1)S(1)}, bf16[64,1024]{1,0:T(8,128)(2,1)S(1)}, bf16[64,256]{1,0:T(8,128)(2,1)S(1)}, f32[256,256]{1,0:T(8,128)S(1)...) custom-call(s32[64]{0:T(128)S(1)} %copy-done.11, ...), custom_call_target="tpu_custom_call" | custom-call | flops 1000000000 | bytes 8388608 | tf_op jit(solution)/shard_map/pallas_call | solution.py:40
  7.5 8.6 %all-gather = bf16[256,1024]{1,0:T(8,128)(2,1)S(1)} all-gather(bf16[64,1024]{1,0:T(8,128)(2,1)S(1)} %get-tuple-element.40), channel_id=2, replica_groups=mesh['ment'=8,'ent'=4] {'ent'}, dimensions={0}, use_global_device_ids=true | all-gather | bytes 655360 | tf_op jit(solution)/shard_map/all_gather | solution.py:514
  16.2 0.1 pad_add_fusion.ids
  16.3 3.5 %shard_map.138 = (bf16[64,1024]{1,0:T(8,128)(2,1)}, f32[64,1024]{1,0:T(8,128)S(1)}, f32[64,128]{1,0:T(8,128)S(1)}, bf16[64,2176]{1,0:T(8,128)(2,1)S(1)}, bf16[64...) custom-call(s32[2]{0:T(128)S(1)} %pad_add_fusion.ids, s32[4]{0:T(128)S(1)} %bitcast.28, ...), custom_call_target="tpu_custom_call" | custom-call | flops 600000000 | bytes 6291456 | tf_op jit(solution)/shard_map/pallas_call | solution.py:40
  19.8 0.4 collective-permute-start
  20.1 1.2 %collective-permute-done.q = bf16[64,2176]{1,0:T(8,128)(2,1)S(1)} collective-permute-done((bf16[64,2176]{1,0:T(8,128)(2,1)S(1)}, bf16[64,2176]{1,0:T(8,128)(2,1)S(1)}, u32[]{:S(2)}, u32[]{:S(2)}) %collective-permute-start) | collective-permute-done | bytes 278560 | tf_op jit(solution)/shard_map/ppermute | solution.py:453
  21.3 0.2 shard_map.139.p0
  21.5 1.2 %collective-permute-start.1 = (bf16[64,2176]{1,0:T(8,128)(2,1)S(1)}, bf16[64,2176]{1,0:T(8,128)(2,1)S(1)}, u32[]{:S(2)}, u32[]{:S(2)}) collective-permute-start(bf16[64,2176]{1,0:T(8,128)(2,1)S(1)} %shard_map.139.p0), channel_id=1, source_target_pairs={{0,2},{1,3},{2,0},{3,1},{4,6},{5,7},{6,4},{7,5},{8,10},{9,11},{10,... | collective-permute-start | bytes 835592 | tf_op jit(solution)/shard_map/ppermute | solution.py:453
  22.7 2.6 %collective-permute-start.5 = (bf16[64,768]{1,0:T(8,128)(2,1)S(1)}, bf16[64,768]{1,0:T(8,128)(2,1)S(1)}, u32[]{:S(2)}, u32[]{:S(2)}) collective-permute-start(bf16[64,768]{1,0:T(8,128)(2,1)S(1)} %get-tuple-element.55), channel_id=1, source_target_pairs={{0,16},{4,20},{8,24},{12,28},{16,0},{20,4},{24,8},{28,12},{1,17},{... | collective-permute-start | bytes 294920 | tf_op jit(solution)/shard_map/ppermute | solution.py:453
  25.3 5.2 %collective-permute-done.5 = bf16[64,768]{1,0:T(8,128)(2,1)S(1)} collective-permute-done((bf16[64,768]{1,0:T(8,128)(2,1)S(1)}, bf16[64,768]{1,0:T(8,128)(2,1)S(1)}, u32[]{:S(2)}, u32[]{:S(2)}) %collective-permute-start.5) | collective-permute-done | bytes 98336 | tf_op jit(solution)/shard_map/ppermute | solution.py:453
  30.5 0.7 collective-permute-start.6
  31.2 1.7 %shard_map.140 = (bf16[256,256]{1,0:T(8,128)(2,1)S(1)}, f32[16,1024]{1,0:T(8,128)S(1)}, bf16[4,128,256]{2,1,0:T(8,128)(2,1)S(1)}, f32[4,128,256]{2,1,0:T(8,128)S(1)}, bf16[80,1024]{1,0:T(8,128)(2,1)S(1)}) custom-call(s32[2]{0:T(128)S(1)} %pad_add_fusion.ids, s32[4]{0:T(128)S(1)} %bitcast.29, bf16[64,2176]{1,0:T(8,128)(2,1)S(1)} %shard_map.139.p0, ...), custom_call_target="tpu_custom_call" | custom-call | flops 300000000 | bytes 6291456 | tf_op jit(solution)/shard_map/pallas_call | solution.py:40
  32.9 1.6 %collective-permute-start.7 = (bf16[4,128,256]{2,1,0:T(8,128)(2,1)S(1)}, bf16[4,128,256]{2,1,0:T(8,128)(2,1)S(1)}, u32[]{:S(2)}, u32[]{:S(2)}) collective-permute-start(bf16[4,128,256]{2,1,0:T(8,128)(2,1)S(1)} %get-tuple-element.57), channel_id=1, source_target_pairs={{0,4},{4,0},{8,12},{12,8},{16,20},{20,16},{24,28},{28,24},{1,5},{5... | collective-permute-start | bytes 786440 | tf_op jit(solution)/shard_map/ppermute | solution.py:453
  34.5 4.6 %shard_map.141 = (bf16[2,80,2176]{2,1,0:T(8,128)(2,1)}, bf16[80,2176]{1,0:T(8,128)(2,1)}, bf16[256,1024]{1,0:T(8,128)(2,1)S(1)}, bf16[64,256]{1,0:T(8,128)(2,1)S(1)}, bf16[80,2176]{1,0:T(8,128)(2,1)S(1)}) custom-call(s32[2]{0:T(128)S(1)} %pad_add_fusion.ids, bf16[2048,1024]{1,0:T(8,128)(2,1)S(1)} %bitcast.18, bf16[3,1024,256]{2,1,0:T(8,128)(2,1)S(1)} %bitcast.21, ...), custom_call_target="tpu_custom_call" | custom-call | flops 1000000000 | bytes 8388608 | tf_op jit(solution)/shard_map/pallas_call | solution.py:40
  39.1 0.0 copy-start.4
  39.1 1.4 %shard_map.145 = bf16[8,272,256]{2,1,0:T(8,128)(2,1)} custom-call(bf16[256,1024]{1,0:T(8,128)(2,1)S(1)} %get-tuple-element.62.tbuf, bf16[256,256]{1,0:T(8,128)(2,1)S(1)} %get-tuple-element.63.qx, bf16[64,256]{1,0:T(8,128)(2,1)S(1)} %get-tuple-element.64.d_query, bf16[64,1024]{1,0:T(8,128)(2,1)S(1)} %get-tuple-element.41.cls, ...), custom_call_target="tpu_custom_call" | custom-call | flops 100000000 | bytes 3145728 | tf_op jit(solution)/shard_map/pallas_call | solution.py:40
  40.5 0.5 collective-permute-done.7.got
  41.0 0.1 shard_map.143
  41.0 5.6 %all-to-all-start = ((bf16[8,272,256]{2,1,0:T(8,128)(2,1)}), bf16[8,272,256]{2,1,0:T(8,128)(2,1)S(1)}, u32[]{:S(2)}, u32[]{:S(2)}) async-start(bf16[8,272,256]{2,1,0:T(8,128)(2,1)} %shard_map.145), calls=%async_computation | async-start | bytes 2228224 | tf_op jit(solution)/shard_map/all_to_all | solution.py:601
  46.6 0.9 %collective-permute-start.3 = (bf16[2,80,2176]{2,1,0:T(8,128)(2,1)}, bf16[2,80,2176]{2,1,0:T(8,128)(2,1)S(1)}, u32[]{:S(2)}, u32[]{:S(2)}) collective-permute-start(bf16[2,80,2176]{2,1,0:T(8,128)(2,1)} %get-tuple-element.52), channel_id=1, source_target_pairs={{0,2},{1,3},{2,0},{3,1},{4,6},{5,7},{6,4},{7,5},{8,10},{9,11},{10,... | collective-permute-start | bytes 2088968 | tf_op jit(solution)/shard_map/ppermute | solution.py:453
  47.6 2.0 %collective-permute-start.9 = (bf16[4,64,768]{2,1,0:T(8,128)(2,1)S(1)}, bf16[4,64,768]{2,1,0:T(8,128)(2,1)S(1)}, u32[]{:S(2)}, u32[]{:S(2)}) collective-permute-start(bf16[4,64,768]{2,1,0:T(8,128)(2,1)S(1)} %pad_maximum_fusion), channel_id=1, source_target_pairs={{0,4},{4,0},{8,12},{12,8},{16,20},{20,16},{24,28},{28,24},{1,5},{5... | collective-permute-start | bytes 1179656 | tf_op jit(solution)/shard_map/ppermute | solution.py:453
  49.6 1.5 %collective-permute-start.8 = (bf16[2,128,256]{2,1,0:T(8,128)(2,1)S(1)}, bf16[2,128,256]{2,1,0:T(8,128)(2,1)S(1)}, u32[]{:S(2)}, u32[]{:S(2)}) collective-permute-start(bf16[2,128,256]{2,1,0:T(8,128)(2,1)S(1)} %get-tuple-element.59), channel_id=1, source_target_pairs={{0,8},{4,12},{8,0},{12,4},{16,24},{20,28},{24,16},{28,20},{1,9},{5... | collective-permute-start | bytes 393224 | tf_op jit(solution)/shard_map/ppermute | solution.py:453
  51.0 15.6 %collective-permute-done.8.got = bf16[2,128,256]{2,1,0:T(8,128)(2,1)S(1)} collective-permute-done((bf16[2,128,256]{2,1,0:T(8,128)(2,1)S(1)}, bf16[2,128,256]{2,1,0:T(8,128)(2,1)S(1)}, u32[]{:S(2)}, u32[]{:S(2)}) %collective-permute-start.8) | collective-permute-done | bytes 131104 | tf_op jit(solution)/shard_map/ppermute | solution.py:453
  66.7 1.7 %collective-permute-done.9 = bf16[4,64,768]{2,1,0:T(8,128)(2,1)S(1)} collective-permute-done((bf16[4,64,768]{2,1,0:T(8,128)(2,1)S(1)}, bf16[4,64,768]{2,1,0:T(8,128)(2,1)S(1)}, u32[]{:S(2)}, u32[]{:S(2)}) %collective-permute-start.9) | collective-permute-done | bytes 393248 | tf_op jit(solution)/shard_map/ppermute | solution.py:453
  68.4 0.1 collective-permute-start.10
  68.5 0.1 slice_bitcast_fusion
  68.6 0.5 collective-permute-start.4
  69.1 3.0 %collective-permute-start.11 = (bf16[128,256]{1,0:T(8,128)(2,1)S(1)}, bf16[128,256]{1,0:T(8,128)(2,1)S(1)}, u32[]{:S(2)}, u32[]{:S(2)}) collective-permute-start(bf16[128,256]{1,0:T(8,128)(2,1)S(1)} %get-tuple-element.69), channel_id=1, source_target_pairs={{0,16},{4,20},{8,24},{12,28},{16,0},{20,4},{24,8},{28,12},{1,17},{... | collective-permute-start | bytes 196616 | tf_op jit(solution)/shard_map/ppermute | solution.py:453
  72.2 1.8 %shard_map.142 = bf16[16,32,1024]{2,1,0:T(8,128)(2,1)} custom-call(bf16[80,2176]{1,0:T(8,128)(2,1)S(1)} %copy-done.5, bf16[80,2176]{1,0:T(8,128)(2,1)S(1)} %collective-permute-done.2.p1, bf16[80,2176]{1,0:T(8,128)(2,1)S(1)} %get-tuple-element.74.p2, bf16[80,2176]{1,0:T(8,128)(2,1)S(1)} %collective-permute-done.4.p3, f32[16,1024]{1,0:T(8,128)S(1)} %get-tuple-element.53.own_resid), custom_call_target="tpu_custom_call" | custom-call | flops 300000000 | bytes 4194304 | tf_op jit(solution)/shard_map/pallas_call | solution.py:40
  74.0 3.0 %shard_map.146 = f32[8,32,1024]{2,1,0:T(8,128)} custom-call(s32[2]{0:T(128)S(1)} %pad_add_fusion.ids, bf16[8,64,768]{2,1,0:T(8,128)(2,1)S(1)} %constant_dynamic-update-slice_fusion.mine_all.gathered, bf16[8,64,768]{2,1,0:T(8,128)(2,1)S(1)} %collective-permute-done.10.other_all, bf16[8,272,256]{2,1,0:T(8,128)(2,1)S(1)} %all-to-all-done.spread, ...), custom_call_target="tpu_custom_call" | custom-call | flops 500000000 | bytes 4194304 | tf_op jit(solution)/shard_map/pallas_call | solution.py:40
  77.0 1.6 %shard_map.147 = (f32[3,128,256]{2,1,0:T(8,128)}, f32[256,128]{1,0:T(8,128)}, f32[2,128]{1,0:T(2,128)}) custom-call(s32[2]{0:T(128)S(1)} %pad_add_fusion.ids, bf16[8,64,768]{2,1,0:T(8,128)(2,1)S(1)} %constant_dynamic-update-slice_fusion.mine_all.gathered, bf16[8,272,256]{2,1,0:T(8,128)(2,1)S(1)} %all-to-all-done.spread, ...), custom_call_target="tpu_custom_call" | custom-call | flops 100000000 | bytes 1048576 | tf_op jit(solution)/shard_map/pallas_call | solution.py:40
  (36 shorter events, 0.2 us)
Async XLA Ops:
  0.6 0.7 copy-start.11
  1.3 15.0 %copy-start.2 = (bf16[8,256,1024]{2,1,0:T(8,128)(2,1)S(1)}, bf16[8,256,1024]{2,1,0:T(8,128)(2,1)}, u32[]{:S(2)}) copy-start(bf16[8,256,1024]{2,1,0:T(8,128)(2,1)} %table.1) | copy-start | bytes 12582916
  1.3 15.0 %copy-start.6 = (f32[1024]{0:T(1024)S(1)}, f32[1024]{0:T(1024)}, u32[]{:S(2)}) copy-start(f32[1024]{0:T(1024)} %param.13) | copy-start | bytes 12292
  1.3 15.0 %copy-start.7 = (f32[1024]{0:T(1024)S(1)}, f32[1024]{0:T(1024)}, u32[]{:S(2)}) copy-start(f32[1024]{0:T(1024)} %param.14) | copy-start | bytes 12292
  1.3 15.0 %copy-start.8 = (s32[1,4]{1,0:T(1,128)S(1)}, s32[1,4]{1,0:T(1,128)}, u32[]{:S(2)}) copy-start(s32[1,4]{1,0:T(1,128)} %param.19) | copy-start | bytes 52
  1.3 15.0 %copy-start.9 = (s32[64]{0:T(128)S(1)}, s32[64]{0:T(128)}, u32[]{:S(2)}) copy-start(s32[64]{0:T(128)} %param.17) | copy-start | bytes 772
  1.3 15.0 %copy-start.10 = (s32[64]{0:T(128)S(1)}, s32[64]{0:T(128)}, u32[]{:S(2)}) copy-start(s32[64]{0:T(128)} %param.18) | copy-start | bytes 772
  16.3 14.9 %copy-start.1 = (bf16[1024,3,256]{2,0,1:T(8,128)(2,1)S(1)}, bf16[1024,3,256]{2,0,1:T(8,128)(2,1)}, u32[]{:S(2)}) copy-start(bf16[1024,3,256]{2,0,1:T(8,128)(2,1)} %param.11) | copy-start | bytes 4718596
  19.8 11.5 %copy-start.3 = (bf16[256,1024]{1,0:T(8,128)(2,1)S(1)}, bf16[256,1024]{1,0:T(8,128)(2,1)}, u32[]{:S(2)}) copy-start(bf16[256,1024]{1,0:T(8,128)(2,1)} %wo_ref.1) | copy-start | bytes 1572868
  19.8 1.6 %collective-permute-start = (bf16[64,2176]{1,0:T(8,128)(2,1)S(1)}, bf16[64,2176]{1,0:T(8,128)(2,1)S(1)}, u32[]{:S(2)}, u32[]{:S(2)}) collective-permute-start(bf16[64,2176]{1,0:T(8,128)(2,1)S(1)} %get-tuple-element.43.p), channel_id=1, source_target_pairs={{0,1},{1,0},{2,3},{3,2},{4,5},{5,4},{6,7},{7,6},{8,9},{9,8},{10,11... | collective-permute-start | bytes 835592 | tf_op jit(solution)/shard_map/ppermute | solution.py:453
  21.3 13.2 %copy-start = (bf16[64,32,1024]{2,1,0:T(8,128)(2,1)S(1)}, bf16[64,32,1024]{2,1,0:T(8,128)(2,1)}, u32[]{:S(2)}) copy-start(bf16[64,32,1024]{2,1,0:T(8,128)(2,1)} %param.10) | copy-start | bytes 12582916
  21.5 9.7 %collective-permute-start.1 = (bf16[64,2176]{1,0:T(8,128)(2,1)S(1)}, bf16[64,2176]{1,0:T(8,128)(2,1)S(1)}, u32[]{:S(2)}, u32[]{:S(2)}) collective-permute-start(bf16[64,2176]{1,0:T(8,128)(2,1)S(1)} %shard_map.139.p0), channel_id=1, source_target_pairs={{0,2},{1,3},{2,0},{3,1},{4,6},{5,7},{6,4},{7,5},{8,10},{9,11},{10,... | collective-permute-start | bytes 835592 | tf_op jit(solution)/shard_map/ppermute | solution.py:453
  22.7 7.8 %collective-permute-start.5 = (bf16[64,768]{1,0:T(8,128)(2,1)S(1)}, bf16[64,768]{1,0:T(8,128)(2,1)S(1)}, u32[]{:S(2)}, u32[]{:S(2)}) collective-permute-start(bf16[64,768]{1,0:T(8,128)(2,1)S(1)} %get-tuple-element.55), channel_id=1, source_target_pairs={{0,16},{4,20},{8,24},{12,28},{16,0},{20,4},{24,8},{28,12},{1,17},{... | collective-permute-start | bytes 294920 | tf_op jit(solution)/shard_map/ppermute | solution.py:453
  30.5 10.0 %collective-permute-start.6 = (bf16[2,64,768]{2,1,0:T(8,128)(2,1)S(1)}, bf16[2,64,768]{2,1,0:T(8,128)(2,1)S(1)}, u32[]{:S(2)}, u32[]{:S(2)}) collective-permute-start(bf16[2,64,768]{2,1,0:T(8,128)(2,1)S(1)} %pad_maximum_fusion.1), channel_id=1, source_target_pairs={{0,8},{4,12},{8,0},{12,4},{16,24},{20,28},{24,16},{28,20},{1,9},{5... | collective-permute-start | bytes 589832 | tf_op jit(solution)/shard_map/ppermute | solution.py:453
  32.9 8.0 %collective-permute-start.7 = (bf16[4,128,256]{2,1,0:T(8,128)(2,1)S(1)}, bf16[4,128,256]{2,1,0:T(8,128)(2,1)S(1)}, u32[]{:S(2)}, u32[]{:S(2)}) collective-permute-start(bf16[4,128,256]{2,1,0:T(8,128)(2,1)S(1)} %get-tuple-element.57), channel_id=1, source_target_pairs={{0,4},{4,0},{8,12},{12,8},{16,20},{20,16},{24,28},{28,24},{1,5},{5... | collective-permute-start | bytes 786440 | tf_op jit(solution)/shard_map/ppermute | solution.py:453
  39.1 1.9 %copy-start.4 = (bf16[80,2176]{1,0:T(8,128)(2,1)}, bf16[80,2176]{1,0:T(8,128)(2,1)S(1)}, u32[]{:S(2)}) copy-start(bf16[80,2176]{1,0:T(8,128)(2,1)S(1)} %get-tuple-element.50.p0) | copy-start | bytes 1044484
  41.0 33.0 %all-to-all-start = ((bf16[8,272,256]{2,1,0:T(8,128)(2,1)}), bf16[8,272,256]{2,1,0:T(8,128)(2,1)S(1)}, u32[]{:S(2)}, u32[]{:S(2)}) async-start(bf16[8,272,256]{2,1,0:T(8,128)(2,1)} %shard_map.145), calls=%async_computation | async-start | bytes 2228224 | tf_op jit(solution)/shard_map/all_to_all | solution.py:601
  46.6 21.9 %collective-permute-start.3 = (bf16[2,80,2176]{2,1,0:T(8,128)(2,1)}, bf16[2,80,2176]{2,1,0:T(8,128)(2,1)S(1)}, u32[]{:S(2)}, u32[]{:S(2)}) collective-permute-start(bf16[2,80,2176]{2,1,0:T(8,128)(2,1)} %get-tuple-element.52), channel_id=1, source_target_pairs={{0,2},{1,3},{2,0},{3,1},{4,6},{5,7},{6,4},{7,5},{8,10},{9,11},{10,... | collective-permute-start | bytes 2088968 | tf_op jit(solution)/shard_map/ppermute | solution.py:453
  47.6 20.9 %collective-permute-start.9 = (bf16[4,64,768]{2,1,0:T(8,128)(2,1)S(1)}, bf16[4,64,768]{2,1,0:T(8,128)(2,1)S(1)}, u32[]{:S(2)}, u32[]{:S(2)}) collective-permute-start(bf16[4,64,768]{2,1,0:T(8,128)(2,1)S(1)} %pad_maximum_fusion), channel_id=1, source_target_pairs={{0,4},{4,0},{8,12},{12,8},{16,20},{20,16},{24,28},{28,24},{1,5},{5... | collective-permute-start | bytes 1179656 | tf_op jit(solution)/shard_map/ppermute | solution.py:453
  49.6 17.1 %collective-permute-start.8 = (bf16[2,128,256]{2,1,0:T(8,128)(2,1)S(1)}, bf16[2,128,256]{2,1,0:T(8,128)(2,1)S(1)}, u32[]{:S(2)}, u32[]{:S(2)}) collective-permute-start(bf16[2,128,256]{2,1,0:T(8,128)(2,1)S(1)} %get-tuple-element.59), channel_id=1, source_target_pairs={{0,8},{4,12},{8,0},{12,4},{16,24},{20,28},{24,16},{28,20},{1,9},{5... | collective-permute-start | bytes 393224 | tf_op jit(solution)/shard_map/ppermute | solution.py:453
  51.0 21.1 %collective-permute-start.2 = (bf16[80,2176]{1,0:T(8,128)(2,1)}, bf16[80,2176]{1,0:T(8,128)(2,1)S(1)}, u32[]{:S(2)}, u32[]{:S(2)}) collective-permute-start(bf16[80,2176]{1,0:T(8,128)(2,1)} %get-tuple-element.51), channel_id=1, source_target_pairs={{0,1},{1,0},{2,3},{3,2},{4,5},{5,4},{6,7},{7,6},{8,9},{9,8},{10,11... | collective-permute-start | bytes 1044488 | tf_op jit(solution)/shard_map/ppermute | solution.py:453
  66.7 5.5 %copy-start.5 = (bf16[80,2176]{1,0:T(8,128)(2,1)S(1)}, bf16[80,2176]{1,0:T(8,128)(2,1)}, u32[]{:S(2)}) copy-start(bf16[80,2176]{1,0:T(8,128)(2,1)} %copy-done.4) | copy-start | bytes 1044484
  68.4 5.6 %collective-permute-start.10 = (bf16[8,64,768]{2,1,0:T(8,128)(2,1)S(1)}, bf16[8,64,768]{2,1,0:T(8,128)(2,1)S(1)}, u32[]{:S(2)}, u32[]{:S(2)}) collective-permute-start(bf16[8,64,768]{2,1,0:T(8,128)(2,1)S(1)} %constant_dynamic-update-slice_fusion.mine_all.gathered), channel_id=1, source_target_pairs={{0,1},{1,0},{2,3},{3,2},{4,5},{5,4},{6,7},{7,6},{8,9},{9,8},{10,11... | collective-permute-start | bytes 2359304 | tf_op jit(solution)/shard_map/ppermute | solution.py:453
  68.6 3.6 %collective-permute-start.4 = (bf16[80,2176]{1,0:T(8,128)(2,1)S(1)}, bf16[80,2176]{1,0:T(8,128)(2,1)S(1)}, u32[]{:S(2)}, u32[]{:S(2)}) collective-permute-start(bf16[80,2176]{1,0:T(8,128)(2,1)S(1)} %get-tuple-element.73), channel_id=1, source_target_pairs={{0,1},{1,0},{2,3},{3,2},{4,5},{5,4},{6,7},{7,6},{8,9},{9,8},{10,11... | collective-permute-start | bytes 1044488 | tf_op jit(solution)/shard_map/ppermute | solution.py:453
  69.1 7.9 %collective-permute-start.11 = (bf16[128,256]{1,0:T(8,128)(2,1)S(1)}, bf16[128,256]{1,0:T(8,128)(2,1)S(1)}, u32[]{:S(2)}, u32[]{:S(2)}) collective-permute-start(bf16[128,256]{1,0:T(8,128)(2,1)S(1)} %get-tuple-element.69), channel_id=1, source_target_pairs={{0,16},{4,20},{8,24},{12,28},{16,0},{20,4},{24,8},{28,12},{1,17},{... | collective-permute-start | bytes 196616 | tf_op jit(solution)/shard_map/ppermute | solution.py:453

commit v6 on v5

--- a/solution.py
+++ b/solution.py
@@ -35,7 +35,7 @@
 
 
 def call(body, outs, ins, scratch=(), flops=0, moved=0, limit=20, outside=0, last=0):
-    smem = sum(1 for x in ins if x.ndim == 1 and x.dtype == jnp.int32)
+    smem = sum(1 for x in ins[: len(ins) - outside] if x.ndim == 1 and x.dtype == jnp.int32)
     inside = len(ins) - smem - outside
     return pl.pallas_call(
         body,
@@ -67,8 +67,8 @@
 
 
 def forward_body(
-    key_len, hid_in, w_in, wo_in, attn, cls_out, ctx_out, probs_out, mix_out, qx_out, qk_out, fold_out,
-    hid, w_ref, wo_ref, sems,
+    hid_in, w_in, wo_in, key_in, attn, cls_out, ctx_out, probs_out, mix_out, qx_out, qk_out, fold_out,
+    hid, w_ref, wo_ref, key_len, sems,
 ):
     tokens, width = hid.shape
     cols = w_ref.shape[2]
@@ -87,6 +87,7 @@
     ]
     part += [pltpu.make_async_copy(w_in.at[k], w_ref.at[k], sems.at[groups + k]) for k in (1, 2)]
     part += [pltpu.make_async_copy(wo_in, wo_ref, sems.at[groups + 3])]
+    part += [pltpu.make_async_copy(key_in, key_len, sems.at[groups + 4])]
     for copy in part:
         copy.start()
     line = lax.broadcasted_iota(jnp.int32, (GROUP, width), 0)
@@ -107,6 +108,7 @@
     qx_out[...] = qx
     part[groups + 1].wait()
     qk_out[...] = mm_nt(qx, w_ref[1]).astype(BF)
+    part[groups + 4].wait()
     score = []
     live = []
     col = lax.broadcasted_iota(jnp.int32, (1, span), 1)
@@ -499,17 +501,18 @@
             sds((hrows, width), BF),
             sds((hrows, 128), BF),
         ],
-        [key_len, hid, w, w_out],
+        [hid, w, w_out, key_len],
         [
             pltpu.VMEM(hid.shape, BF),
             pltpu.VMEM(w.shape, BF),
             pltpu.VMEM(w_out.shape, BF),
-            pltpu.SemaphoreType.DMA((count // GROUP + 4,)),
+            pltpu.SMEM(key_len.shape, jnp.int32),
+            pltpu.SemaphoreType.DMA((count // GROUP + 5,)),
         ],
         flops=10**9,
         moved=8 * 2**20,
         limit=52,
-        outside=3,
+        outside=4,
     )
     attns = lax.all_gather(attn, "ent")
     embed, normed, rstd, pay, packed, table_rows = call(
@@ -596,8 +599,8 @@
         fold_z_body, [sds(tile, F32), sds(tile, BF)], [v_keep, ment(v_sent, 2)], moved=2**19
     )
     v_got = ment(v_send, 4)
-    gathered = jnp.concatenate([after(zs, v_keep), ment(zs, 1)], axis=0)
-    gathered_other = ent(gathered, 1)
+    gathered = jnp.concatenate([zs, ment(zs, 1)], axis=0)
+    gathered_other = ent(after(gathered, v_keep), 1)
     spread = lax.all_to_all(after(spread, v_sent, zs), "ment", 0, 0)
     grad_table = call(
         functools.partial(table_body, negs.shape[0]),

time: 78.8 us -> 78.7 us (level)
  no operation moved by 1% of the time
where the time goes in v6:
time: 78.7 us; the launch traced here: 78.5 us
  waiting for transfers between devices  24.2 us (31%)
  Pallas kernels  23.9 us (30%)
  starting transfers between devices  20 us (25%)
  blocking collectives  8.65 us (11%)
  between operations  0.82 us (1%)
    ppermute x12, waiting for transfers between devices, swap(): return lax.ppermute(x, axis, [(i, i ^ k) for i in range(size)])  24.2 us
    pallas_call x11, Pallas kernels, call(): pl.pallas_call(body, out_shape=outs, in_specs=[SMEM] * smem + [VMEM] * in...  23.9 us
    ppermute x12, starting transfers between devices, swap(): return lax.ppermute(x, axis, [(i, i ^ k) for i in range(size)])  14.4 us
    all_gather x1, blocking collectives, on_device(): attns = lax.all_gather(attn, 'ent')  8.65 us
    all_to_all x1, starting transfers between devices, on_device(): spread = lax.all_to_all(after(spread, v_sent, zs), 'ment', 0, 0)  5.6 us
  transfers between devices with their start and end apart: 13, of which 5 were waited for; matrix products, arithmetic and copies ran while one was open for 0% of the time, Pallas kernels for 16%

profile of v6, /device:TPU:0, one launch (start us, length us, event | category | flops | bytes accessed | tf_op | source)
XLA Modules:
  0.0 78.5 jit_solution(16030781826540988997)
XLA Ops:
  0.6 0.6 copy-done.11
  1.3 6.1 %shard_map.137 = (bf16[64,1024]{1,0:T(8,128)(2,1)S(1)}, bf16[64,1024]{1,0:T(8,128)(2,1)S(1)}, bf16[64,256]{1,0:T(8,128)(2,1)S(1)}, f32[256,256]{1,0:T(8,128)S(1)...) custom-call(bf16[2048,1024]{1,0:T(8,128)(2,1)} %bitcast.17, ...), custom_call_target="tpu_custom_call" | custom-call | flops 1000000000 | bytes 8388608 | tf_op jit(solution)/shard_map/pallas_call | solution.py:40
  7.4 8.6 %all-gather = bf16[256,1024]{1,0:T(8,128)(2,1)S(1)} all-gather(bf16[64,1024]{1,0:T(8,128)(2,1)S(1)} %get-tuple-element.40), channel_id=2, replica_groups=mesh['ment'=8,'ent'=4] {'ent'}, dimensions={0}, use_global_device_ids=true | all-gather | bytes 655360 | tf_op jit(solution)/shard_map/all_gather | solution.py:517
  16.1 0.1 pad_add_fusion.ids
  16.2 3.5 %shard_map.138 = (bf16[64,1024]{1,0:T(8,128)(2,1)}, f32[64,1024]{1,0:T(8,128)S(1)}, f32[64,128]{1,0:T(8,128)S(1)}, bf16[64,2176]{1,0:T(8,128)(2,1)S(1)}, bf16[64...) custom-call(s32[2]{0:T(128)S(1)} %pad_add_fusion.ids, s32[4]{0:T(128)S(1)} %bitcast.29, ...), custom_call_target="tpu_custom_call" | custom-call | flops 600000000 | bytes 6291456 | tf_op jit(solution)/shard_map/pallas_call | solution.py:40
  19.7 0.4 collective-permute-start
  20.0 1.2 %collective-permute-done.q = bf16[64,2176]{1,0:T(8,128)(2,1)S(1)} collective-permute-done((bf16[64,2176]{1,0:T(8,128)(2,1)S(1)}, bf16[64,2176]{1,0:T(8,128)(2,1)S(1)}, u32[]{:S(2)}, u32[]{:S(2)}) %collective-permute-start) | collective-permute-done | bytes 278560 | tf_op jit(solution)/shard_map/ppermute | solution.py:455
  21.2 0.2 shard_map.139.p0
  21.4 1.2 %collective-permute-start.1 = (bf16[64,2176]{1,0:T(8,128)(2,1)S(1)}, bf16[64,2176]{1,0:T(8,128)(2,1)S(1)}, u32[]{:S(2)}, u32[]{:S(2)}) collective-permute-start(bf16[64,2176]{1,0:T(8,128)(2,1)S(1)} %shard_map.139.p0), channel_id=1, source_target_pairs={{0,2},{1,3},{2,0},{3,1},{4,6},{5,7},{6,4},{7,5},{8,10},{9,11},{10,... | collective-permute-start | bytes 835592 | tf_op jit(solution)/shard_map/ppermute | solution.py:455
  22.6 2.6 %collective-permute-start.5 = (bf16[64,768]{1,0:T(8,128)(2,1)S(1)}, bf16[64,768]{1,0:T(8,128)(2,1)S(1)}, u32[]{:S(2)}, u32[]{:S(2)}) collective-permute-start(bf16[64,768]{1,0:T(8,128)(2,1)S(1)} %get-tuple-element.55), channel_id=1, source_target_pairs={{0,16},{4,20},{8,24},{12,28},{16,0},{20,4},{24,8},{28,12},{1,17},{... | collective-permute-start | bytes 294920 | tf_op jit(solution)/shard_map/ppermute | solution.py:455
  25.2 5.2 %collective-permute-done.5 = bf16[64,768]{1,0:T(8,128)(2,1)S(1)} collective-permute-done((bf16[64,768]{1,0:T(8,128)(2,1)S(1)}, bf16[64,768]{1,0:T(8,128)(2,1)S(1)}, u32[]{:S(2)}, u32[]{:S(2)}) %collective-permute-start.5) | collective-permute-done | bytes 98336 | tf_op jit(solution)/shard_map/ppermute | solution.py:455
  30.4 0.7 collective-permute-start.6
  31.1 1.7 %shard_map.140 = (bf16[256,256]{1,0:T(8,128)(2,1)S(1)}, f32[16,1024]{1,0:T(8,128)S(1)}, bf16[4,128,256]{2,1,0:T(8,128)(2,1)S(1)}, f32[4,128,256]{2,1,0:T(8,128)S(1)}, bf16[80,1024]{1,0:T(8,128)(2,1)S(1)}) custom-call(s32[2]{0:T(128)S(1)} %pad_add_fusion.ids, s32[4]{0:T(128)S(1)} %bitcast.30, bf16[64,2176]{1,0:T(8,128)(2,1)S(1)} %shard_map.139.p0, ...), custom_call_target="tpu_custom_call" | custom-call | flops 300000000 | bytes 6291456 | tf_op jit(solution)/shard_map/pallas_call | solution.py:40
  32.8 1.6 %collective-permute-start.8 = (bf16[4,128,256]{2,1,0:T(8,128)(2,1)S(1)}, bf16[4,128,256]{2,1,0:T(8,128)(2,1)S(1)}, u32[]{:S(2)}, u32[]{:S(2)}) collective-permute-start(bf16[4,128,256]{2,1,0:T(8,128)(2,1)S(1)} %get-tuple-element.61), channel_id=1, source_target_pairs={{0,4},{4,0},{8,12},{12,8},{16,20},{20,16},{24,28},{28,24},{1,5},{5... | collective-permute-start | bytes 786440 | tf_op jit(solution)/shard_map/ppermute | solution.py:455
  34.4 4.6 %shard_map.141 = (bf16[2,80,2176]{2,1,0:T(8,128)(2,1)}, bf16[80,2176]{1,0:T(8,128)(2,1)}, bf16[256,1024]{1,0:T(8,128)(2,1)S(1)}, bf16[64,256]{1,0:T(8,128)(2,1)S(1)}, bf16[80,2176]{1,0:T(8,128)(2,1)S(1)}) custom-call(s32[2]{0:T(128)S(1)} %pad_add_fusion.ids, bf16[2048,1024]{1,0:T(8,128)(2,1)S(1)} %bitcast.18, bf16[3,1024,256]{2,1,0:T(8,128)(2,1)S(1)} %bitcast.21, ...), custom_call_target="tpu_custom_call" | custom-call | flops 1000000000 | bytes 8388608 | tf_op jit(solution)/shard_map/pallas_call | solution.py:40
  39.0 1.4 %shard_map.143 = bf16[8,272,256]{2,1,0:T(8,128)(2,1)} custom-call(bf16[256,1024]{1,0:T(8,128)(2,1)S(1)} %get-tuple-element.56.tbuf, bf16[256,256]{1,0:T(8,128)(2,1)S(1)} %get-tuple-element.57.qx, bf16[64,256]{1,0:T(8,128)(2,1)S(1)} %get-tuple-element.58.d_query, bf16[64,1024]{1,0:T(8,128)(2,1)S(1)} %get-tuple-element.41.cls, ...), custom_call_target="tpu_custom_call" | custom-call | flops 100000000 | bytes 3145728 | tf_op jit(solution)/shard_map/pallas_call | solution.py:40
  40.4 0.4 collective-permute-done.8.got
  40.9 0.1 shard_map.144
  40.9 5.6 %all-to-all-start = ((bf16[8,272,256]{2,1,0:T(8,128)(2,1)}), bf16[8,272,256]{2,1,0:T(8,128)(2,1)S(1)}, u32[]{:S(2)}, u32[]{:S(2)}) async-start(bf16[8,272,256]{2,1,0:T(8,128)(2,1)} %shard_map.143), calls=%async_computation | async-start | bytes 2228224 | tf_op jit(solution)/shard_map/all_to_all | solution.py:604
  46.5 0.9 %collective-permute-start.3 = (bf16[2,80,2176]{2,1,0:T(8,128)(2,1)}, bf16[2,80,2176]{2,1,0:T(8,128)(2,1)S(1)}, u32[]{:S(2)}, u32[]{:S(2)}) collective-permute-start(bf16[2,80,2176]{2,1,0:T(8,128)(2,1)} %get-tuple-element.52), channel_id=1, source_target_pairs={{0,2},{1,3},{2,0},{3,1},{4,6},{5,7},{6,4},{7,5},{8,10},{9,11},{10,... | collective-permute-start | bytes 2088968 | tf_op jit(solution)/shard_map/ppermute | solution.py:455
  47.4 2.0 %collective-permute-start.7 = (bf16[4,64,768]{2,1,0:T(8,128)(2,1)S(1)}, bf16[4,64,768]{2,1,0:T(8,128)(2,1)S(1)}, u32[]{:S(2)}, u32[]{:S(2)}) collective-permute-start(bf16[4,64,768]{2,1,0:T(8,128)(2,1)S(1)} %pad_maximum_fusion.1), channel_id=1, source_target_pairs={{0,4},{4,0},{8,12},{12,8},{16,20},{20,16},{24,28},{28,24},{1,5},{5... | collective-permute-start | bytes 1179656 | tf_op jit(solution)/shard_map/ppermute | solution.py:455
  49.5 1.5 %collective-permute-start.9 = (bf16[2,128,256]{2,1,0:T(8,128)(2,1)S(1)}, bf16[2,128,256]{2,1,0:T(8,128)(2,1)S(1)}, u32[]{:S(2)}, u32[]{:S(2)}) collective-permute-start(bf16[2,128,256]{2,1,0:T(8,128)(2,1)S(1)} %get-tuple-element.62), channel_id=1, source_target_pairs={{0,8},{4,12},{8,0},{12,4},{16,24},{20,28},{24,16},{28,20},{1,9},{5... | collective-permute-start | bytes 393224 | tf_op jit(solution)/shard_map/ppermute | solution.py:455
  50.9 15.6 %collective-permute-done.9.got = bf16[2,128,256]{2,1,0:T(8,128)(2,1)S(1)} collective-permute-done((bf16[2,128,256]{2,1,0:T(8,128)(2,1)S(1)}, bf16[2,128,256]{2,1,0:T(8,128)(2,1)S(1)}, u32[]{:S(2)}, u32[]{:S(2)}) %collective-permute-start.9) | collective-permute-done | bytes 131104 | tf_op jit(solution)/shard_map/ppermute | solution.py:455
  66.6 1.7 %collective-permute-done.7 = bf16[4,64,768]{2,1,0:T(8,128)(2,1)S(1)} collective-permute-done((bf16[4,64,768]{2,1,0:T(8,128)(2,1)S(1)}, bf16[4,64,768]{2,1,0:T(8,128)(2,1)S(1)}, u32[]{:S(2)}, u32[]{:S(2)}) %collective-permute-start.7) | collective-permute-done | bytes 393248 | tf_op jit(solution)/shard_map/ppermute | solution.py:455
  68.3 0.1 pad_maximum_fusion.mine_all.gathered
  68.4 0.1 collective-permute-start.10
  68.5 0.1 slice_bitcast_fusion
  68.5 0.5 collective-permute-start.4
  69.1 3.0 %collective-permute-start.11 = (bf16[128,256]{1,0:T(8,128)(2,1)S(1)}, bf16[128,256]{1,0:T(8,128)(2,1)S(1)}, u32[]{:S(2)}, u32[]{:S(2)}) collective-permute-start(bf16[128,256]{1,0:T(8,128)(2,1)S(1)} %get-tuple-element.69), channel_id=1, source_target_pairs={{0,16},{4,20},{8,24},{12,28},{16,0},{20,4},{24,8},{28,12},{1,17},{... | collective-permute-start | bytes 196616 | tf_op jit(solution)/shard_map/ppermute | solution.py:455
  72.1 1.8 %shard_map.142 = bf16[16,32,1024]{2,1,0:T(8,128)(2,1)} custom-call(bf16[80,2176]{1,0:T(8,128)(2,1)S(1)} %copy-done.5, bf16[80,2176]{1,0:T(8,128)(2,1)S(1)} %collective-permute-done.2.p1, bf16[80,2176]{1,0:T(8,128)(2,1)S(1)} %get-tuple-element.74.p2, bf16[80,2176]{1,0:T(8,128)(2,1)S(1)} %collective-permute-done.4.p3, f32[16,1024]{1,0:T(8,128)S(1)} %get-tuple-element.53.own_resid), custom_call_target="tpu_custom_call" | custom-call | flops 300000000 | bytes 4194304 | tf_op jit(solution)/shard_map/pallas_call | solution.py:40
  73.9 3.0 %shard_map.146 = f32[8,32,1024]{2,1,0:T(8,128)} custom-call(s32[2]{0:T(128)S(1)} %pad_add_fusion.ids, bf16[8,64,768]{2,1,0:T(8,128)(2,1)S(1)} %pad_maximum_fusion.mine_all.gathered, bf16[8,64,768]{2,1,0:T(8,128)(2,1)S(1)} %collective-permute-done.10.other_all, bf16[8,272,256]{2,1,0:T(8,128)(2,1)S(1)} %all-to-all-done.spread, ...), custom_call_target="tpu_custom_call" | custom-call | flops 500000000 | bytes 4194304 | tf_op jit(solution)/shard_map/pallas_call | solution.py:40
  76.9 1.6 %shard_map.147 = (f32[3,128,256]{2,1,0:T(8,128)}, f32[256,128]{1,0:T(8,128)}, f32[2,128]{1,0:T(2,128)}) custom-call(s32[2]{0:T(128)S(1)} %pad_add_fusion.ids, bf16[8,64,768]{2,1,0:T(8,128)(2,1)S(1)} %pad_maximum_fusion.mine_all.gathered, bf16[8,272,256]{2,1,0:T(8,128)(2,1)S(1)} %all-to-all-done.spread, f32[128,256]{1,0:T(8,128)S(1)} %get-tuple-element.65.v0, ...), custom_call_target="tpu_custom_call" | custom-call | flops 100000000 | bytes 1048576 | tf_op jit(solution)/shard_map/pallas_call | solution.py:40
  (35 shorter events, 0.2 us)
Async XLA Ops:
  0.6 0.7 copy-start.11
  1.3 14.9 %copy-start.2 = (bf16[8,256,1024]{2,1,0:T(8,128)(2,1)S(1)}, bf16[8,256,1024]{2,1,0:T(8,128)(2,1)}, u32[]{:S(2)}) copy-start(bf16[8,256,1024]{2,1,0:T(8,128)(2,1)} %table.1) | copy-start | bytes 12582916
  1.3 14.9 %copy-start.6 = (f32[1024]{0:T(1024)S(1)}, f32[1024]{0:T(1024)}, u32[]{:S(2)}) copy-start(f32[1024]{0:T(1024)} %param.13) | copy-start | bytes 12292
  1.3 14.9 %copy-start.7 = (f32[1024]{0:T(1024)S(1)}, f32[1024]{0:T(1024)}, u32[]{:S(2)}) copy-start(f32[1024]{0:T(1024)} %param.14) | copy-start | bytes 12292
  1.3 14.9 %copy-start.8 = (s32[1,4]{1,0:T(1,128)S(1)}, s32[1,4]{1,0:T(1,128)}, u32[]{:S(2)}) copy-start(s32[1,4]{1,0:T(1,128)} %param.19) | copy-start | bytes 52
  1.3 14.9 %copy-start.9 = (s32[64]{0:T(128)S(1)}, s32[64]{0:T(128)}, u32[]{:S(2)}) copy-start(s32[64]{0:T(128)} %param.17) | copy-start | bytes 772
  1.3 14.9 %copy-start.10 = (s32[64]{0:T(128)S(1)}, s32[64]{0:T(128)}, u32[]{:S(2)}) copy-start(s32[64]{0:T(128)} %param.18) | copy-start | bytes 772
  16.2 14.9 %copy-start.1 = (bf16[1024,3,256]{2,0,1:T(8,128)(2,1)S(1)}, bf16[1024,3,256]{2,0,1:T(8,128)(2,1)}, u32[]{:S(2)}) copy-start(bf16[1024,3,256]{2,0,1:T(8,128)(2,1)} %param.11) | copy-start | bytes 4718596
  19.7 11.5 %copy-start.3 = (bf16[256,1024]{1,0:T(8,128)(2,1)S(1)}, bf16[256,1024]{1,0:T(8,128)(2,1)}, u32[]{:S(2)}) copy-start(bf16[256,1024]{1,0:T(8,128)(2,1)} %wo_ref.1) | copy-start | bytes 1572868
  19.7 1.6 %collective-permute-start = (bf16[64,2176]{1,0:T(8,128)(2,1)S(1)}, bf16[64,2176]{1,0:T(8,128)(2,1)S(1)}, u32[]{:S(2)}, u32[]{:S(2)}) collective-permute-start(bf16[64,2176]{1,0:T(8,128)(2,1)S(1)} %get-tuple-element.43.p), channel_id=1, source_target_pairs={{0,1},{1,0},{2,3},{3,2},{4,5},{5,4},{6,7},{7,6},{8,9},{9,8},{10,11... | collective-permute-start | bytes 835592 | tf_op jit(solution)/shard_map/ppermute | solution.py:455
  21.2 13.1 %copy-start = (bf16[64,32,1024]{2,1,0:T(8,128)(2,1)S(1)}, bf16[64,32,1024]{2,1,0:T(8,128)(2,1)}, u32[]{:S(2)}) copy-start(bf16[64,32,1024]{2,1,0:T(8,128)(2,1)} %param.10) | copy-start | bytes 12582916
  21.4 9.7 %collective-permute-start.1 = (bf16[64,2176]{1,0:T(8,128)(2,1)S(1)}, bf16[64,2176]{1,0:T(8,128)(2,1)S(1)}, u32[]{:S(2)}, u32[]{:S(2)}) collective-permute-start(bf16[64,2176]{1,0:T(8,128)(2,1)S(1)} %shard_map.139.p0), channel_id=1, source_target_pairs={{0,2},{1,3},{2,0},{3,1},{4,6},{5,7},{6,4},{7,5},{8,10},{9,11},{10,... | collective-permute-start | bytes 835592 | tf_op jit(solution)/shard_map/ppermute | solution.py:455
  22.6 7.8 %collective-permute-start.5 = (bf16[64,768]{1,0:T(8,128)(2,1)S(1)}, bf16[64,768]{1,0:T(8,128)(2,1)S(1)}, u32[]{:S(2)}, u32[]{:S(2)}) collective-permute-start(bf16[64,768]{1,0:T(8,128)(2,1)S(1)} %get-tuple-element.55), channel_id=1, source_target_pairs={{0,16},{4,20},{8,24},{12,28},{16,0},{20,4},{24,8},{28,12},{1,17},{... | collective-permute-start | bytes 294920 | tf_op jit(solution)/shard_map/ppermute | solution.py:455
  30.4 10.0 %collective-permute-start.6 = (bf16[2,64,768]{2,1,0:T(8,128)(2,1)S(1)}, bf16[2,64,768]{2,1,0:T(8,128)(2,1)S(1)}, u32[]{:S(2)}, u32[]{:S(2)}) collective-permute-start(bf16[2,64,768]{2,1,0:T(8,128)(2,1)S(1)} %pad_maximum_fusion.2), channel_id=1, source_target_pairs={{0,8},{4,12},{8,0},{12,4},{16,24},{20,28},{24,16},{28,20},{1,9},{5... | collective-permute-start | bytes 589832 | tf_op jit(solution)/shard_map/ppermute | solution.py:455
  32.8 8.0 %collective-permute-start.8 = (bf16[4,128,256]{2,1,0:T(8,128)(2,1)S(1)}, bf16[4,128,256]{2,1,0:T(8,128)(2,1)S(1)}, u32[]{:S(2)}, u32[]{:S(2)}) collective-permute-start(bf16[4,128,256]{2,1,0:T(8,128)(2,1)S(1)} %get-tuple-element.61), channel_id=1, source_target_pairs={{0,4},{4,0},{8,12},{12,8},{16,20},{20,16},{24,28},{28,24},{1,5},{5... | collective-permute-start | bytes 786440 | tf_op jit(solution)/shard_map/ppermute | solution.py:455
  39.0 1.9 %copy-start.4 = (bf16[80,2176]{1,0:T(8,128)(2,1)}, bf16[80,2176]{1,0:T(8,128)(2,1)S(1)}, u32[]{:S(2)}) copy-start(bf16[80,2176]{1,0:T(8,128)(2,1)S(1)} %get-tuple-element.50.p0) | copy-start | bytes 1044484
  40.9 33.0 %all-to-all-start = ((bf16[8,272,256]{2,1,0:T(8,128)(2,1)}), bf16[8,272,256]{2,1,0:T(8,128)(2,1)S(1)}, u32[]{:S(2)}, u32[]{:S(2)}) async-start(bf16[8,272,256]{2,1,0:T(8,128)(2,1)} %shard_map.143), calls=%async_computation | async-start | bytes 2228224 | tf_op jit(solution)/shard_map/all_to_all | solution.py:604
  46.5 21.9 %collective-permute-start.3 = (bf16[2,80,2176]{2,1,0:T(8,128)(2,1)}, bf16[2,80,2176]{2,1,0:T(8,128)(2,1)S(1)}, u32[]{:S(2)}, u32[]{:S(2)}) collective-permute-start(bf16[2,80,2176]{2,1,0:T(8,128)(2,1)} %get-tuple-element.52), channel_id=1, source_target_pairs={{0,2},{1,3},{2,0},{3,1},{4,6},{5,7},{6,4},{7,5},{8,10},{9,11},{10,... | collective-permute-start | bytes 2088968 | tf_op jit(solution)/shard_map/ppermute | solution.py:455
  47.4 20.9 %collective-permute-start.7 = (bf16[4,64,768]{2,1,0:T(8,128)(2,1)S(1)}, bf16[4,64,768]{2,1,0:T(8,128)(2,1)S(1)}, u32[]{:S(2)}, u32[]{:S(2)}) collective-permute-start(bf16[4,64,768]{2,1,0:T(8,128)(2,1)S(1)} %pad_maximum_fusion.1), channel_id=1, source_target_pairs={{0,4},{4,0},{8,12},{12,8},{16,20},{20,16},{24,28},{28,24},{1,5},{5... | collective-permute-start | bytes 1179656 | tf_op jit(solution)/shard_map/ppermute | solution.py:455
  49.5 17.1 %collective-permute-start.9 = (bf16[2,128,256]{2,1,0:T(8,128)(2,1)S(1)}, bf16[2,128,256]{2,1,0:T(8,128)(2,1)S(1)}, u32[]{:S(2)}, u32[]{:S(2)}) collective-permute-start(bf16[2,128,256]{2,1,0:T(8,128)(2,1)S(1)} %get-tuple-element.62), channel_id=1, source_target_pairs={{0,8},{4,12},{8,0},{12,4},{16,24},{20,28},{24,16},{28,20},{1,9},{5... | collective-permute-start | bytes 393224 | tf_op jit(solution)/shard_map/ppermute | solution.py:455
  50.9 21.2 %collective-permute-start.2 = (bf16[80,2176]{1,0:T(8,128)(2,1)}, bf16[80,2176]{1,0:T(8,128)(2,1)S(1)}, u32[]{:S(2)}, u32[]{:S(2)}) collective-permute-start(bf16[80,2176]{1,0:T(8,128)(2,1)} %get-tuple-element.51), channel_id=1, source_target_pairs={{0,1},{1,0},{2,3},{3,2},{4,5},{5,4},{6,7},{7,6},{8,9},{9,8},{10,11... | collective-permute-start | bytes 1044488 | tf_op jit(solution)/shard_map/ppermute | solution.py:455
  66.6 5.5 %copy-start.5 = (bf16[80,2176]{1,0:T(8,128)(2,1)S(1)}, bf16[80,2176]{1,0:T(8,128)(2,1)}, u32[]{:S(2)}) copy-start(bf16[80,2176]{1,0:T(8,128)(2,1)} %copy-done.4) | copy-start | bytes 1044484
  68.4 5.5 %collective-permute-start.10 = (bf16[8,64,768]{2,1,0:T(8,128)(2,1)S(1)}, bf16[8,64,768]{2,1,0:T(8,128)(2,1)S(1)}, u32[]{:S(2)}, u32[]{:S(2)}) collective-permute-start(bf16[8,64,768]{2,1,0:T(8,128)(2,1)S(1)} %pad_maximum_fusion.mine_all.gathered), channel_id=1, source_target_pairs={{0,1},{1,0},{2,3},{3,2},{4,5},{5,4},{6,7},{7,6},{8,9},{9,8},{10,11... | collective-permute-start | bytes 2359304 | tf_op jit(solution)/shard_map/ppermute | solution.py:455
  68.5 3.6 %collective-permute-start.4 = (bf16[80,2176]{1,0:T(8,128)(2,1)S(1)}, bf16[80,2176]{1,0:T(8,128)(2,1)S(1)}, u32[]{:S(2)}, u32[]{:S(2)}) collective-permute-start(bf16[80,2176]{1,0:T(8,128)(2,1)S(1)} %get-tuple-element.73), channel_id=1, source_target_pairs={{0,1},{1,0},{2,3},{3,2},{4,5},{5,4},{6,7},{7,6},{8,9},{9,8},{10,11... | collective-permute-start | bytes 1044488 | tf_op jit(solution)/shard_map/ppermute | solution.py:455
  69.1 7.8 %collective-permute-start.11 = (bf16[128,256]{1,0:T(8,128)(2,1)S(1)}, bf16[128,256]{1,0:T(8,128)(2,1)S(1)}, u32[]{:S(2)}, u32[]{:S(2)}) collective-permute-start(bf16[128,256]{1,0:T(8,128)(2,1)S(1)} %get-tuple-element.69), channel_id=1, source_target_pairs={{0,16},{4,20},{8,24},{12,28},{16,0},{20,4},{24,8},{28,12},{1,17},{... | collective-permute-start | bytes 196616 | tf_op jit(solution)/shard_map/ppermute | solution.py:455
